TPU v7x, 32 devices: a whole 2x2x4 slice. The times are simulated.
32 devices in a mesh: parts: 16 (over z, y, x), pair: 2 (over core).
Axes of the slice: x: 2, y: 2, z: 4, core: 2. Of those that a mesh axis runs over, the one named last changes fastest.
Arguments:
- pulse_rhs: float32 [32, 65536], P(None, ('parts', 'pair')), may hold values from -6 to 6
- blocks_fine: float32 [512, 4, 128, 128], P(('parts', 'pair'))
- columns_fine: int32 [512, 4], P(('parts', 'pair')), may hold values from 0 to 19, as said below
- aggregate_fine: int32 [65536], P(('parts', 'pair')), may hold values from 0 to 127
- blocks_mid: float32 [128, 4, 128, 128], P(('parts', 'pair'))
- columns_mid: int32 [128, 4], P(('parts', 'pair')), may hold values from 0 to 7, as said below
- aggregate_mid: int32 [16384], P(('parts', 'pair')), may hold values from 0 to 127
- blocks_low: float32 [64, 4, 128, 128], P(('parts', 'pair'))
- columns_low: int32 [64, 4], P(('parts', 'pair')), may hold values from 0 to 5, as said below
- aggregate_low: int32 [8192], P(('parts', 'pair')), may hold values from 0 to 63
- coarse_ops: float32 [32, 5, 128, 128], P(('parts', 'pair')), as said below
- coarse_maps: int32 [32, 4, 128], P(('parts', 'pair')), may hold values from 0 to 63, as said below
Outputs:
- solution: float32 [32, 65536], P(None, ('parts', 'pair'))
Inputs may be any that keep to these rules, and one draw needn't show every extreme that they name: `columns_fine`: row tile i of a device's tiles lists positions of its extended vector: entry 0 is i + 2, the others lie in i to i + 4; the first 2 row tiles reach the tiles before and the last 2 the tiles after. `columns_mid`: as for columns_fine, with 4 tiles a device. `columns_low`: as for columns_fine, with 2 tiles a device. `coarse_ops`: entry [d, j] is equal on all devices d with the same d divided by 2^(j+1), rounded down. `coarse_maps`: entry [d, j] is equal on all devices d with the same d divided by 2^(j+1), rounded down.
All inputs are finite; a program needn't handle non-finite values.
Results may differ from a plain program's by a relative error of at most 0.0003.
Values sent between devices are 32-bit elements; how exact they have to be, the bound alone decides.
No kernel may reach another device: no remote copies, remote signals or barrier semaphores. Data moves between devices by JAX's collectives and lax.ppermute only.
A program may use at most 128 MiB of HBM per device.

v0:
```python
import jax
import jax.numpy as jnp
from jax import lax
from jax.sharding import PartitionSpec as P

HALO = 2
SWEEPS = 3
COARSE_SWEEPS = 2
COARSEST_SWEEPS = 8


OMEGA = 0.7


def from_behind(value, axis, steps):
    count = lax.axis_size(axis)
    initial, last = (max(0, -steps), min(count, count - steps))
    return lax.ppermute(value, axis, [(source, source + steps) for source in range(initial, last)])


def tile_product(blocks, columns, extended):
    picked = extended[:, columns]
    return jnp.einsum("tkrc,btkc->btr", blocks, picked, precision=lax.Precision.HIGHEST)


def level_diagonal(blocks, columns):
    own_tile = jnp.arange(blocks.shape[0], dtype=jnp.int32) + HALO
    own_hits = (columns == own_tile[:, None]).astype(jnp.float32)
    return jnp.sum(jnp.diagonal(blocks, axis1=2, axis2=3) * own_hits[:, :, None], axis=1)


def with_rims(tile_rows):
    from_left = from_behind(tile_rows[:, -HALO:], ("parts", "pair"), 1)
    from_right = from_behind(tile_rows[:, :HALO], ("parts", "pair"), -1)
    return (from_left, from_right)


def level_apply(blocks, columns, tile_rows):
    from_left, from_right = with_rims(tile_rows)
    return tile_product(
        blocks, columns, jnp.concatenate([from_left, tile_rows, from_right], axis=1)
    )


def smooth_fine(blocks, columns, diagonal, source, iterate, sweeps):
    for sweep_index in range(sweeps):
        iterate = iterate + OMEGA * (source - level_apply(blocks, columns, iterate)) / diagonal
    return iterate


def coarse_apply(matrix, vector):
    return jnp.dot(vector, matrix.T, precision=lax.Precision.HIGHEST)


def smooth_coarse(matrix, diagonal, source, iterate, sweeps):
    for sweep_index in range(sweeps):
        iterate = iterate + OMEGA * (source - coarse_apply(matrix, iterate)) / diagonal
    return iterate


def coarse_chain(own_piece, coarse_ops, coarse_maps):
    position = lax.axis_index(("parts", "pair"))
    depths = lax.axis_size(("parts", "pair")).bit_length() - 1
    half_width = own_piece.shape[1]
    stored = []
    for section_index in range(depths):
        upper_bit = position // 2**section_index % 2
        partner = from_behind(own_piece, ("parts", "pair"), -(2**section_index))
        merged = jnp.concatenate([own_piece, partner], axis=1)
        matrix = coarse_ops[0, section_index]
        diagonal = jnp.diagonal(matrix)
        sweeps = COARSEST_SWEEPS if section_index == depths - 1 else COARSE_SWEEPS
        iterate = smooth_coarse(matrix, diagonal, merged, OMEGA * merged / diagonal, sweeps - 1)
        selector = None
        if section_index < depths - 1:
            residual = merged - coarse_apply(matrix, iterate)
            selector = (
                coarse_maps[0, section_index][:, None]
                == jnp.arange(half_width, dtype=jnp.int32)[None, :]
            ).astype(jnp.float32)
            own_piece = jnp.dot(residual, selector, precision=lax.Precision.HIGHEST)
        stored.append((merged, iterate, matrix, diagonal, selector, upper_bit))
    halves = None
    for section_index in reversed(range(depths)):
        merged, iterate, matrix, diagonal, selector, upper_bit = stored[section_index]
        if section_index < depths - 1:
            iterate = iterate + jnp.dot(halves, selector.T, precision=lax.Precision.HIGHEST)
            iterate = smooth_coarse(matrix, diagonal, merged, iterate, COARSE_SWEEPS)
        returned = from_behind(iterate[:, half_width:], ("parts", "pair"), 2**section_index)
        halves = jnp.where(upper_bit == 0, iterate[:, :half_width], returned)
    return halves


def fine_cycle(levels, level_index, source, coarse_ops, coarse_maps):
    blocks, columns, aggregate = levels[level_index]
    tile_count = blocks.shape[0]
    width = blocks.shape[-1]
    panels = source.shape[0]
    diagonal = level_diagonal(blocks, columns)
    iterate = smooth_fine(blocks, columns, diagonal, source, OMEGA * source / diagonal, SWEEPS - 1)
    residual = source - level_apply(blocks, columns, iterate)
    if level_index < 2:
        coarse_count = levels[level_index + 1][0].shape[0]
        factor = tile_count // coarse_count
        selector = (
            aggregate.reshape(coarse_count, factor * width)[:, :, None]
            == jnp.arange(width, dtype=jnp.int32)[None, None, :]
        ).astype(jnp.float32)
        coarse_source = jnp.einsum(
            "bcf,cfa->bca",
            residual.reshape(panels, coarse_count, factor * width),
            selector,
            precision=lax.Precision.HIGHEST,
        )
        correction = fine_cycle(levels, level_index + 1, coarse_source, coarse_ops, coarse_maps)
        lifted = jnp.einsum(
            "cfa,bca->bcf", selector, correction, precision=lax.Precision.HIGHEST
        ).reshape(source.shape)
    else:
        half_width = width // 2
        selector = (aggregate[:, None] == jnp.arange(half_width, dtype=jnp.int32)[None, :]).astype(
            jnp.float32
        )
        own_piece = jnp.dot(residual.reshape(panels, -1), selector, precision=lax.Precision.HIGHEST)
        halves = coarse_chain(own_piece, coarse_ops, coarse_maps)
        lifted = jnp.dot(halves, selector.T, precision=lax.Precision.HIGHEST).reshape(source.shape)
    iterate = iterate + lifted
    return smooth_fine(blocks, columns, diagonal, source, iterate, SWEEPS)


def on_device(
    pulse_rhs,
    blocks_fine,
    columns_fine,
    aggregate_fine,
    blocks_mid,
    columns_mid,
    aggregate_mid,
    blocks_low,
    columns_low,
    aggregate_low,
    coarse_ops,
    coarse_maps,
):
    levels = (
        (blocks_fine, columns_fine, aggregate_fine),
        (blocks_mid, columns_mid, aggregate_mid),
        (blocks_low, columns_low, aggregate_low),
    )
    width = blocks_fine.shape[-1]
    source = pulse_rhs.reshape(pulse_rhs.shape[0], blocks_fine.shape[0], width)
    result = fine_cycle(levels, 0, source, coarse_ops, coarse_maps)
    return result.reshape(pulse_rhs.shape)


def solution(mesh):
    in_specs = (
        P(None, ("parts", "pair")),
        P(("parts", "pair"), None, None, None),
        P(("parts", "pair"), None),
        P(("parts", "pair")),
        P(("parts", "pair"), None, None, None),
        P(("parts", "pair"), None),
        P(("parts", "pair")),
        P(("parts", "pair"), None, None, None),
        P(("parts", "pair"), None),
        P(("parts", "pair")),
        P(("parts", "pair"), None, None, None),
        P(("parts", "pair"), None, None),
    )
    out_specs = P(None, ("parts", "pair"))
    return jax.shard_map(
        on_device, mesh=mesh, in_specs=in_specs, out_specs=out_specs, check_vma=False
    )
```

profile of v0, /device:TPU:7, one launch (start us, length us, event | category | flops | bytes accessed | tf_op | source)
XLA Modules:
  0.0 342.1 jit_solution(4481717170619555059)
XLA Ops:
  0.0 18.4 %copy.38 = f32[16,4,128,128]{0,1,3,2:T(4,128)} copy(f32[16,4,128,128]{3,2,1,0:T(8,128)} %param.13) | data formatting | bytes 8388608 | tf_op args[1]
  23.3 4.8 %collective-permute-start = (f32[32,2,128]{2,0,1:T(8,128)S(1)}, f32[32,2,128]{2,0,1:T(8,128)S(1)}, u32[]{:S(2)}, u32[]{:S(2)}) collective-permute-start(f32[32,2,128]{2,0,1:T(8,128)S(1)} %get-tuple-element.20), channel_id=1, source_target_pairs={{0,1},{1,2},{2,3},{3,4},{4,5},{5,6},{6,7},{7,8},{8,9},{9,10},{10,1... | collective-permute-start | bytes 98312 | tf_op jit(solution)/shard_map/ppermute | solution.py:18
  29.7 5.9 %fusion.3 = f32[32,16,128]{2,0,1:T(8,128)S(1)} fusion(f32[32,16,4,128]{3,0,2,1:T(8,128)S(1)} %bitcast.433, f32[16,4,128,128]{3,2,1,0:T(8,128)} %param.13, f32[16,128]{1,0:T(8,128)S(1)} %copy.39, f32[32,2048]{1,0:T(8,128)S(1)} %copy-done), kind=kOutput, calls=%fused_computation.35 | convolution fusion | flops 403046400 | bytes 5775360 | tf_op jit(solution)/shard_map/tkrc,btkc->btr/dot_general | solution.py:23
  37.6 6.0 %collective-permute-start.2 = (f32[32,2,128]{2,0,1:T(8,128)S(1)}, f32[32,2,128]{2,0,1:T(8,128)S(1)}, u32[]{:S(2)}, u32[]{:S(2)}) collective-permute-start(f32[32,2,128]{2,0,1:T(8,128)S(1)} %get-tuple-element.18), channel_id=1, source_target_pairs={{0,1},{1,2},{2,3},{3,4},{4,5},{5,6},{6,7},{7,8},{8,9},{9,10},{10,1... | collective-permute-start | bytes 98312 | tf_op jit(solution)/shard_map/ppermute | solution.py:18
  43.7 16.8 %copy.46 = f32[4,4,128,128]{1,0,3,2:T(4,128)} copy(f32[4,4,128,128]{3,2,1,0:T(8,128)S(1)} %copy-done.1) | data formatting | bytes 2097152 | tf_op args[4]
  63.7 6.0 %fusion.7 = f32[32,16,128]{2,0,1:T(8,128)S(1)} fusion(f32[32,16,128]{2,0,1:T(8,128)S(1)} %fusion.3, f32[32,16,4,128]{3,0,2,1:T(8,128)S(1)} %bitcast.430, f32[16,4,128,128]{3,2,1,0:T(8,128)} %param.13, f32[16,128]{1,0:T(8,128)S(1)} %copy.39, f32[32,2048]{1,0:T(8,128)S(1)} %copy-done), kind=kOutput, calls=%fused_computation.39 | convolution fusion | flops 402915328 | bytes 6037504 | tf_op jit(solution)/shard_map/tkrc,btkc->btr/dot_general | solution.py:23
  71.6 5.4 %collective-permute-start.4 = (f32[32,2,128]{2,0,1:T(8,128)S(1)}, f32[32,2,128]{2,0,1:T(8,128)S(1)}, u32[]{:S(2)}, u32[]{:S(2)}) collective-permute-start(f32[32,2,128]{2,0,1:T(8,128)S(1)} %get-tuple-element.16), channel_id=1, source_target_pairs={{0,1},{1,2},{2,3},{3,4},{4,5},{5,6},{6,7},{7,8},{8,9},{9,10},{10,1... | collective-permute-start | bytes 98312 | tf_op jit(solution)/shard_map/ppermute | solution.py:18
  78.8 5.9 %fusion.8 = f32[32,16,128]{2,0,1:T(8,128)S(1)} fusion(f32[32,16,4,128]{3,0,2,1:T(8,128)S(1)} %bitcast.434, f32[16,4,128,128]{3,2,1,0:T(8,128)} %param.13, f32[32,2048]{1,0:T(8,128)S(1)} %copy-done), kind=kOutput, calls=%fused_computation.40 | convolution fusion | flops 402718720 | bytes 5767168 | tf_op jit(solution)/shard_map/tkrc,btkc->btr/dot_general | solution.py:23
  87.8 6.0 %collective-permute-start.6 = (f32[32,2,128]{2,0,1:T(8,128)S(1)}, f32[32,2,128]{2,0,1:T(8,128)S(1)}, u32[]{:S(2)}, u32[]{:S(2)}) collective-permute-start(f32[32,2,128]{2,0,1:T(8,128)S(1)} %get-tuple-element.32), channel_id=1, source_target_pairs={{0,1},{1,2},{2,3},{3,4},{4,5},{5,6},{6,7},{7,8},{8,9},{9,10},{10,1... | collective-permute-start | bytes 98312 | tf_op jit(solution)/shard_map/ppermute | solution.py:18
  98.5 6.0 %collective-permute-start.8 = (f32[32,2,128]{2,0,1:T(8,128)S(1)}, f32[32,2,128]{2,0,1:T(8,128)S(1)}, u32[]{:S(2)}, u32[]{:S(2)}) collective-permute-start(f32[32,2,128]{2,0,1:T(8,128)S(1)} %get-tuple-element.30), channel_id=1, source_target_pairs={{0,1},{1,2},{2,3},{3,4},{4,5},{5,6},{6,7},{7,8},{8,9},{9,10},{10,1... | collective-permute-start | bytes 98312 | tf_op jit(solution)/shard_map/ppermute | solution.py:18
  104.5 11.4 %copy.50 = f32[2,4,128,128]{1,0,3,2:T(2,128)} copy(f32[2,4,128,128]{3,2,1,0:T(8,128)S(1)} %copy-done.2) | data formatting | bytes 1048576 | tf_op args[7]
  115.9 6.7 %gather_fusion.8 = f32[128,2,4]{2,1,0:T(2,128)S(1)} fusion(f32[2,4,128,128]{1,0,3,2:T(2,128)} %copy.50, s32[128]{0:T(128)S(1)} %or_bitcast_fusion), kind=kCustom, calls=%fused_computation.8 | custom fusion | bytes 9216 | tf_op jit(solution)/shard_map/jit(diagonal)/gather | solution.py:29
  126.4 5.6 %collective-permute-start.10 = (f32[32,2,128]{2,0,1:T(8,128)S(1)}, f32[32,2,128]{2,0,1:T(8,128)S(1)}, u32[]{:S(2)}, u32[]{:S(2)}) collective-permute-start(f32[32,2,128]{2,0,1:T(8,128)S(1)} %get-tuple-element.28), channel_id=1, source_target_pairs={{0,1},{1,2},{2,3},{3,4},{4,5},{5,6},{6,7},{7,8},{8,9},{9,10},{10,1... | collective-permute-start | bytes 98312 | tf_op jit(solution)/shard_map/ppermute | solution.py:18
  136.9 6.0 %collective-permute-start.12 = (f32[32,2,128]{2,0,1:T(8,128)S(1)}, f32[32,2,128]{2,0,1:T(8,128)S(1)}, u32[]{:S(2)}, u32[]{:S(2)}) collective-permute-start(f32[32,2,128]{2,0,1:T(8,128)S(1)} %get-tuple-element.40), channel_id=1, source_target_pairs={{0,1},{1,2},{2,3},{3,4},{4,5},{5,6},{6,7},{7,8},{8,9},{9,10},{10,1... | collective-permute-start | bytes 98312 | tf_op jit(solution)/shard_map/ppermute | solution.py:18
  147.1 6.0 %collective-permute-start.14 = (f32[32,2,128]{2,0,1:T(8,128)S(1)}, f32[32,2,128]{2,0,1:T(8,128)S(1)}, u32[]{:S(2)}, u32[]{:S(2)}) collective-permute-start(f32[32,2,128]{2,0,1:T(8,128)S(1)} %fusion.64), channel_id=1, source_target_pairs={{0,1},{1,2},{2,3},{3,4},{4,5},{5,6},{6,7},{7,8},{8,9},{9,10},{10,1... | collective-permute-start | bytes 98312 | tf_op jit(solution)/shard_map/ppermute | solution.py:18
  157.2 6.0 %collective-permute-start.16 = (f32[32,2,128]{2,0,1:T(8,128)S(1)}, f32[32,2,128]{2,0,1:T(8,128)S(1)}, u32[]{:S(2)}, u32[]{:S(2)}) collective-permute-start(f32[32,2,128]{2,0,1:T(8,128)S(1)} %fusion.60), channel_id=1, source_target_pairs={{0,1},{1,2},{2,3},{3,4},{4,5},{5,6},{6,7},{7,8},{8,9},{9,10},{10,1... | collective-permute-start | bytes 98312 | tf_op jit(solution)/shard_map/ppermute | solution.py:18
  168.9 4.2 %collective-permute-done.18 = f32[32,64]{1,0:T(8,128)S(1)} collective-permute-done((f32[32,64]{1,0:T(8,128)S(1)}, f32[32,64]{1,0:T(8,128)S(1)}, u32[]{:S(2)}, u32[]{:S(2)}) %collective-permute-start.18) | collective-permute-done | bytes 8224 | tf_op jit(solution)/shard_map/ppermute | solution.py:18
  177.0 3.1 collective-permute-done.19
  203.1 3.2 collective-permute-start.24
  218.5 10.6 %collective-permute-start.27 = (f32[32,64]{1,0:T(8,128)S(1)}, f32[32,64]{1,0:T(8,128)S(1)}, u32[]{:S(2)}, u32[]{:S(2)}) collective-permute-start(f32[32,64]{1,0:T(8,128)S(1)} %slice.245), channel_id=1, source_target_pairs={{0,1},{1,2},{2,3},{3,4},{4,5},{5,6},{6,7},{7,8},{8,9},{9,10},{10,1... | collective-permute-start | bytes 24584 | tf_op jit(solution)/shard_map/ppermute | solution.py:18
  232.2 6.0 %collective-permute-start.28 = (f32[32,2,128]{2,0,1:T(8,128)S(1)}, f32[32,2,128]{2,0,1:T(8,128)S(1)}, u32[]{:S(2)}, u32[]{:S(2)}) collective-permute-start(f32[32,2,128]{2,0,1:T(8,128)S(1)} %bitcast_add_fusion), channel_id=1, source_target_pairs={{0,1},{1,2},{2,3},{3,4},{4,5},{5,6},{6,7},{7,8},{8,9},{9,10},{10,1... | collective-permute-start | bytes 98312 | tf_op jit(solution)/shard_map/ppermute | solution.py:18
  242.3 6.0 %collective-permute-start.30 = (f32[32,2,128]{2,0,1:T(8,128)S(1)}, f32[32,2,128]{2,0,1:T(8,128)S(1)}, u32[]{:S(2)}, u32[]{:S(2)}) collective-permute-start(f32[32,2,128]{2,0,1:T(8,128)S(1)} %fusion.54), channel_id=1, source_target_pairs={{0,1},{1,2},{2,3},{3,4},{4,5},{5,6},{6,7},{7,8},{8,9},{9,10},{10,1... | collective-permute-start | bytes 98312 | tf_op jit(solution)/shard_map/ppermute | solution.py:18
  252.4 6.0 %collective-permute-start.32 = (f32[32,2,128]{2,0,1:T(8,128)S(1)}, f32[32,2,128]{2,0,1:T(8,128)S(1)}, u32[]{:S(2)}, u32[]{:S(2)}) collective-permute-start(f32[32,2,128]{2,0,1:T(8,128)S(1)} %fusion.50), channel_id=1, source_target_pairs={{0,1},{1,2},{2,3},{3,4},{4,5},{5,6},{6,7},{7,8},{8,9},{9,10},{10,1... | collective-permute-start | bytes 98312 | tf_op jit(solution)/shard_map/ppermute | solution.py:18
  263.1 6.0 %collective-permute-start.34 = (f32[32,2,128]{2,0,1:T(8,128)S(1)}, f32[32,2,128]{2,0,1:T(8,128)S(1)}, u32[]{:S(2)}, u32[]{:S(2)}) collective-permute-start(f32[32,2,128]{2,0,1:T(8,128)S(1)} %get-tuple-element.26), channel_id=1, source_target_pairs={{0,1},{1,2},{2,3},{3,4},{4,5},{5,6},{6,7},{7,8},{8,9},{9,10},{10,1... | collective-permute-start | bytes 98312 | tf_op jit(solution)/shard_map/ppermute | solution.py:18
  273.8 6.2 %collective-permute-start.36 = (f32[32,2,128]{2,0,1:T(8,128)S(1)}, f32[32,2,128]{2,0,1:T(8,128)S(1)}, u32[]{:S(2)}, u32[]{:S(2)}) collective-permute-start(f32[32,2,128]{2,0,1:T(8,128)S(1)} %get-tuple-element.24), channel_id=1, source_target_pairs={{0,1},{1,2},{2,3},{3,4},{4,5},{5,6},{6,7},{7,8},{8,9},{9,10},{10,1... | collective-permute-start | bytes 98312 | tf_op jit(solution)/shard_map/ppermute | solution.py:18
  284.5 6.0 %collective-permute-start.38 = (f32[32,2,128]{2,0,1:T(8,128)S(1)}, f32[32,2,128]{2,0,1:T(8,128)S(1)}, u32[]{:S(2)}, u32[]{:S(2)}) collective-permute-start(f32[32,2,128]{2,0,1:T(8,128)S(1)} %get-tuple-element.22), channel_id=1, source_target_pairs={{0,1},{1,2},{2,3},{3,4},{4,5},{5,6},{6,7},{7,8},{8,9},{9,10},{10,1... | collective-permute-start | bytes 98312 | tf_op jit(solution)/shard_map/ppermute | solution.py:18
  296.7 6.0 %collective-permute-start.40 = (f32[32,2,128]{2,0,1:T(8,128)S(1)}, f32[32,2,128]{2,0,1:T(8,128)S(1)}, u32[]{:S(2)}, u32[]{:S(2)}) collective-permute-start(f32[32,2,128]{2,0,1:T(8,128)S(1)} %get-tuple-element.14), channel_id=1, source_target_pairs={{0,1},{1,2},{2,3},{3,4},{4,5},{5,6},{6,7},{7,8},{8,9},{9,10},{10,1... | collective-permute-start | bytes 98312 | tf_op jit(solution)/shard_map/ppermute | solution.py:18
  304.4 5.9 %fusion.12 = f32[32,16,128]{2,0,1:T(8,128)S(1)} fusion(f32[32,16,128]{2,0,1:T(8,128)S(1)} %copy_add_fusion, f32[32,16,4,128]{3,0,2,1:T(8,128)S(1)} %bitcast.431, f32[16,4,128,128]{3,2,1,0:T(8,128)} %param.13, f32[16,128]{1,0:T(8,128)S(1)} %copy.39, f32[32,2048]{1,0:T(8,128)S(1)} %copy-done), kind=kOutput, calls=%fused_computation.44 | convolution fusion | flops 402915328 | bytes 6037504 | tf_op jit(solution)/shard_map/tkrc,btkc->btr/dot_general | solution.py:23
  312.2 6.0 %collective-permute-start.42 = (f32[32,2,128]{2,0,1:T(8,128)S(1)}, f32[32,2,128]{2,0,1:T(8,128)S(1)}, u32[]{:S(2)}, u32[]{:S(2)}) collective-permute-start(f32[32,2,128]{2,0,1:T(8,128)S(1)} %get-tuple-element.12), channel_id=1, source_target_pairs={{0,1},{1,2},{2,3},{3,4},{4,5},{5,6},{6,7},{7,8},{8,9},{9,10},{10,1... | collective-permute-start | bytes 98312 | tf_op jit(solution)/shard_map/ppermute | solution.py:18
  319.9 5.9 %fusion.16 = f32[32,16,128]{2,0,1:T(8,128)S(1)} fusion(f32[32,16,128]{2,0,1:T(8,128)S(1)} %fusion.12, f32[32,16,4,128]{3,0,2,1:T(8,128)S(1)} %bitcast.432, f32[16,4,128,128]{3,2,1,0:T(8,128)} %param.13, f32[16,128]{1,0:T(8,128)S(1)} %copy.39, f32[32,2048]{1,0:T(8,128)S(1)} %copy-done), kind=kOutput, calls=%fused_computation.48 | convolution fusion | flops 402915328 | bytes 6037504 | tf_op jit(solution)/shard_map/tkrc,btkc->btr/dot_general | solution.py:23
  327.8 6.0 %collective-permute-start.44 = (f32[32,2,128]{2,0,1:T(8,128)S(1)}, f32[32,2,128]{2,0,1:T(8,128)S(1)}, u32[]{:S(2)}, u32[]{:S(2)}) collective-permute-start(f32[32,2,128]{2,0,1:T(8,128)S(1)} %get-tuple-element.10), channel_id=1, source_target_pairs={{0,1},{1,2},{2,3},{3,4},{4,5},{5,6},{6,7},{7,8},{8,9},{9,10},{10,1... | collective-permute-start | bytes 98312 | tf_op jit(solution)/shard_map/ppermute | solution.py:18
  335.5 5.9 %fusion.21 = f32[16,4,8,128]{3,2,1,0:T(8,128)S(1)} fusion(f32[32,16,128]{2,0,1:T(8,128)S(1)} %fusion.16, f32[32,16,4,128]{3,0,2,1:T(8,128)S(1)} %bitcast.429, f32[16,4,128,128]{3,2,1,0:T(8,128)} %param.13, f32[16,128]{1,0:T(8,128)S(1)} %copy.39, f32[32,2048]{1,0:T(8,128)S(1)} %copy-done), kind=kOutput, calls=%fused_computation.54 | convolution fusion | flops 402915328 | bytes 6037504 | tf_op jit(solution)/shard_map/tkrc,btkc->btr/dot_general | solution.py:23
  (248 shorter events, 124.1 us)
Async XLA Ops:
  20.7 7.7 %collective-permute-start.1 = (f32[32,2,128]{2,0,1:T(8,128)S(1)}, f32[32,2,128]{2,0,1:T(8,128)S(1)}, u32[]{:S(2)}, u32[]{:S(2)}) collective-permute-start(f32[32,2,128]{2,0,1:T(8,128)S(1)} %get-tuple-element.21), channel_id=1, source_target_pairs={{1,0},{2,1},{3,2},{4,3},{5,4},{6,5},{7,6},{8,7},{9,8},{10,9},{11,1... | collective-permute-start | bytes 98312 | tf_op jit(solution)/shard_map/ppermute | solution.py:18
  35.7 27.4 %collective-permute-start.3 = (f32[32,2,128]{2,0,1:T(8,128)S(1)}, f32[32,2,128]{2,0,1:T(8,128)S(1)}, u32[]{:S(2)}, u32[]{:S(2)}) collective-permute-start(f32[32,2,128]{2,0,1:T(8,128)S(1)} %get-tuple-element.19), channel_id=1, source_target_pairs={{1,0},{2,1},{3,2},{4,3},{5,4},{6,5},{7,6},{8,7},{9,8},{10,9},{11,1... | collective-permute-start | bytes 98312 | tf_op jit(solution)/shard_map/ppermute | solution.py:18
  37.6 25.4 %collective-permute-start.2 = (f32[32,2,128]{2,0,1:T(8,128)S(1)}, f32[32,2,128]{2,0,1:T(8,128)S(1)}, u32[]{:S(2)}, u32[]{:S(2)}) collective-permute-start(f32[32,2,128]{2,0,1:T(8,128)S(1)} %get-tuple-element.18), channel_id=1, source_target_pairs={{0,1},{1,2},{2,3},{3,4},{4,5},{5,6},{6,7},{7,8},{8,9},{9,10},{10,1... | collective-permute-start | bytes 98312 | tf_op jit(solution)/shard_map/ppermute | solution.py:18
  69.7 7.8 %collective-permute-start.5 = (f32[32,2,128]{2,0,1:T(8,128)S(1)}, f32[32,2,128]{2,0,1:T(8,128)S(1)}, u32[]{:S(2)}, u32[]{:S(2)}) collective-permute-start(f32[32,2,128]{2,0,1:T(8,128)S(1)} %get-tuple-element.17), channel_id=1, source_target_pairs={{1,0},{2,1},{3,2},{4,3},{5,4},{6,5},{7,6},{8,7},{9,8},{10,9},{11,1... | collective-permute-start | bytes 98312 | tf_op jit(solution)/shard_map/ppermute | solution.py:18
  85.8 8.0 %collective-permute-start.7 = (f32[32,2,128]{2,0,1:T(8,128)S(1)}, f32[32,2,128]{2,0,1:T(8,128)S(1)}, u32[]{:S(2)}, u32[]{:S(2)}) collective-permute-start(f32[32,2,128]{2,0,1:T(8,128)S(1)} %get-tuple-element.33), channel_id=1, source_target_pairs={{1,0},{2,1},{3,2},{4,3},{5,4},{6,5},{7,6},{8,7},{9,8},{10,9},{11,1... | collective-permute-start | bytes 98312 | tf_op jit(solution)/shard_map/ppermute | solution.py:18
  87.8 7.0 %collective-permute-start.6 = (f32[32,2,128]{2,0,1:T(8,128)S(1)}, f32[32,2,128]{2,0,1:T(8,128)S(1)}, u32[]{:S(2)}, u32[]{:S(2)}) collective-permute-start(f32[32,2,128]{2,0,1:T(8,128)S(1)} %get-tuple-element.32), channel_id=1, source_target_pairs={{0,1},{1,2},{2,3},{3,4},{4,5},{5,6},{6,7},{7,8},{8,9},{9,10},{10,1... | collective-permute-start | bytes 98312 | tf_op jit(solution)/shard_map/ppermute | solution.py:18
  96.5 26.2 %collective-permute-start.9 = (f32[32,2,128]{2,0,1:T(8,128)S(1)}, f32[32,2,128]{2,0,1:T(8,128)S(1)}, u32[]{:S(2)}, u32[]{:S(2)}) collective-permute-start(f32[32,2,128]{2,0,1:T(8,128)S(1)} %get-tuple-element.31), channel_id=1, source_target_pairs={{1,0},{2,1},{3,2},{4,3},{5,4},{6,5},{7,6},{8,7},{9,8},{10,9},{11,1... | collective-permute-start | bytes 98312 | tf_op jit(solution)/shard_map/ppermute | solution.py:18
  98.5 24.2 %collective-permute-start.8 = (f32[32,2,128]{2,0,1:T(8,128)S(1)}, f32[32,2,128]{2,0,1:T(8,128)S(1)}, u32[]{:S(2)}, u32[]{:S(2)}) collective-permute-start(f32[32,2,128]{2,0,1:T(8,128)S(1)} %get-tuple-element.30), channel_id=1, source_target_pairs={{0,1},{1,2},{2,3},{3,4},{4,5},{5,6},{6,7},{7,8},{8,9},{9,10},{10,1... | collective-permute-start | bytes 98312 | tf_op jit(solution)/shard_map/ppermute | solution.py:18
  124.5 7.9 %collective-permute-start.11 = (f32[32,2,128]{2,0,1:T(8,128)S(1)}, f32[32,2,128]{2,0,1:T(8,128)S(1)}, u32[]{:S(2)}, u32[]{:S(2)}) collective-permute-start(f32[32,2,128]{2,0,1:T(8,128)S(1)} %get-tuple-element.29), channel_id=1, source_target_pairs={{1,0},{2,1},{3,2},{4,3},{5,4},{6,5},{7,6},{8,7},{9,8},{10,9},{11,1... | collective-permute-start | bytes 98312 | tf_op jit(solution)/shard_map/ppermute | solution.py:18
  135.0 8.0 %collective-permute-start.13 = (f32[32,2,128]{2,0,1:T(8,128)S(1)}, f32[32,2,128]{2,0,1:T(8,128)S(1)}, u32[]{:S(2)}, u32[]{:S(2)}) collective-permute-start(f32[32,2,128]{2,0,1:T(8,128)S(1)} %get-tuple-element.40), channel_id=1, source_target_pairs={{1,0},{2,1},{3,2},{4,3},{5,4},{6,5},{7,6},{8,7},{9,8},{10,9},{11,1... | collective-permute-start | bytes 98312 | tf_op jit(solution)/shard_map/ppermute | solution.py:18
  145.1 8.0 %collective-permute-start.15 = (f32[32,2,128]{2,0,1:T(8,128)S(1)}, f32[32,2,128]{2,0,1:T(8,128)S(1)}, u32[]{:S(2)}, u32[]{:S(2)}) collective-permute-start(f32[32,2,128]{2,0,1:T(8,128)S(1)} %fusion.64), channel_id=1, source_target_pairs={{1,0},{2,1},{3,2},{4,3},{5,4},{6,5},{7,6},{8,7},{9,8},{10,9},{11,1... | collective-permute-start | bytes 98312 | tf_op jit(solution)/shard_map/ppermute | solution.py:18
  147.1 7.0 %collective-permute-start.14 = (f32[32,2,128]{2,0,1:T(8,128)S(1)}, f32[32,2,128]{2,0,1:T(8,128)S(1)}, u32[]{:S(2)}, u32[]{:S(2)}) collective-permute-start(f32[32,2,128]{2,0,1:T(8,128)S(1)} %fusion.64), channel_id=1, source_target_pairs={{0,1},{1,2},{2,3},{3,4},{4,5},{5,6},{6,7},{7,8},{8,9},{9,10},{10,1... | collective-permute-start | bytes 98312 | tf_op jit(solution)/shard_map/ppermute | solution.py:18
  155.3 8.0 %collective-permute-start.17 = (f32[32,2,128]{2,0,1:T(8,128)S(1)}, f32[32,2,128]{2,0,1:T(8,128)S(1)}, u32[]{:S(2)}, u32[]{:S(2)}) collective-permute-start(f32[32,2,128]{2,0,1:T(8,128)S(1)} %fusion.60), channel_id=1, source_target_pairs={{1,0},{2,1},{3,2},{4,3},{5,4},{6,5},{7,6},{8,7},{9,8},{10,9},{11,1... | collective-permute-start | bytes 98312 | tf_op jit(solution)/shard_map/ppermute | solution.py:18
  157.2 7.0 %collective-permute-start.16 = (f32[32,2,128]{2,0,1:T(8,128)S(1)}, f32[32,2,128]{2,0,1:T(8,128)S(1)}, u32[]{:S(2)}, u32[]{:S(2)}) collective-permute-start(f32[32,2,128]{2,0,1:T(8,128)S(1)} %fusion.60), channel_id=1, source_target_pairs={{0,1},{1,2},{2,3},{3,4},{4,5},{5,6},{6,7},{7,8},{8,9},{9,10},{10,1... | collective-permute-start | bytes 98312 | tf_op jit(solution)/shard_map/ppermute | solution.py:18
  165.6 7.4 %collective-permute-start.18 = (f32[32,64]{1,0:T(8,128)S(1)}, f32[32,64]{1,0:T(8,128)S(1)}, u32[]{:S(2)}, u32[]{:S(2)}) collective-permute-start(f32[32,64]{1,0:T(8,128)S(1)} %fusion.126), channel_id=1, source_target_pairs={{1,0},{2,1},{3,2},{4,3},{5,4},{6,5},{7,6},{8,7},{9,8},{10,9},{11,1... | collective-permute-start | bytes 24584 | tf_op jit(solution)/shard_map/ppermute | solution.py:18
  218.5 11.4 %collective-permute-start.27 = (f32[32,64]{1,0:T(8,128)S(1)}, f32[32,64]{1,0:T(8,128)S(1)}, u32[]{:S(2)}, u32[]{:S(2)}) collective-permute-start(f32[32,64]{1,0:T(8,128)S(1)} %slice.245), channel_id=1, source_target_pairs={{0,1},{1,2},{2,3},{3,4},{4,5},{5,6},{6,7},{7,8},{8,9},{9,10},{10,1... | collective-permute-start | bytes 24584 | tf_op jit(solution)/shard_map/ppermute | solution.py:18
  230.2 7.9 %collective-permute-start.29 = (f32[32,2,128]{2,0,1:T(8,128)S(1)}, f32[32,2,128]{2,0,1:T(8,128)S(1)}, u32[]{:S(2)}, u32[]{:S(2)}) collective-permute-start(f32[32,2,128]{2,0,1:T(8,128)S(1)} %bitcast_add_fusion), channel_id=1, source_target_pairs={{1,0},{2,1},{3,2},{4,3},{5,4},{6,5},{7,6},{8,7},{9,8},{10,9},{11,1... | collective-permute-start | bytes 98312 | tf_op jit(solution)/shard_map/ppermute | solution.py:18
  240.4 8.0 %collective-permute-start.31 = (f32[32,2,128]{2,0,1:T(8,128)S(1)}, f32[32,2,128]{2,0,1:T(8,128)S(1)}, u32[]{:S(2)}, u32[]{:S(2)}) collective-permute-start(f32[32,2,128]{2,0,1:T(8,128)S(1)} %fusion.54), channel_id=1, source_target_pairs={{1,0},{2,1},{3,2},{4,3},{5,4},{6,5},{7,6},{8,7},{9,8},{10,9},{11,1... | collective-permute-start | bytes 98312 | tf_op jit(solution)/shard_map/ppermute | solution.py:18
  242.3 7.0 %collective-permute-start.30 = (f32[32,2,128]{2,0,1:T(8,128)S(1)}, f32[32,2,128]{2,0,1:T(8,128)S(1)}, u32[]{:S(2)}, u32[]{:S(2)}) collective-permute-start(f32[32,2,128]{2,0,1:T(8,128)S(1)} %fusion.54), channel_id=1, source_target_pairs={{0,1},{1,2},{2,3},{3,4},{4,5},{5,6},{6,7},{7,8},{8,9},{9,10},{10,1... | collective-permute-start | bytes 98312 | tf_op jit(solution)/shard_map/ppermute | solution.py:18
  250.5 8.0 %collective-permute-start.33 = (f32[32,2,128]{2,0,1:T(8,128)S(1)}, f32[32,2,128]{2,0,1:T(8,128)S(1)}, u32[]{:S(2)}, u32[]{:S(2)}) collective-permute-start(f32[32,2,128]{2,0,1:T(8,128)S(1)} %fusion.50), channel_id=1, source_target_pairs={{1,0},{2,1},{3,2},{4,3},{5,4},{6,5},{7,6},{8,7},{9,8},{10,9},{11,1... | collective-permute-start | bytes 98312 | tf_op jit(solution)/shard_map/ppermute | solution.py:18
  252.4 7.0 %collective-permute-start.32 = (f32[32,2,128]{2,0,1:T(8,128)S(1)}, f32[32,2,128]{2,0,1:T(8,128)S(1)}, u32[]{:S(2)}, u32[]{:S(2)}) collective-permute-start(f32[32,2,128]{2,0,1:T(8,128)S(1)} %fusion.50), channel_id=1, source_target_pairs={{0,1},{1,2},{2,3},{3,4},{4,5},{5,6},{6,7},{7,8},{8,9},{9,10},{10,1... | collective-permute-start | bytes 98312 | tf_op jit(solution)/shard_map/ppermute | solution.py:18
  261.2 8.0 %collective-permute-start.35 = (f32[32,2,128]{2,0,1:T(8,128)S(1)}, f32[32,2,128]{2,0,1:T(8,128)S(1)}, u32[]{:S(2)}, u32[]{:S(2)}) collective-permute-start(f32[32,2,128]{2,0,1:T(8,128)S(1)} %get-tuple-element.27), channel_id=1, source_target_pairs={{1,0},{2,1},{3,2},{4,3},{5,4},{6,5},{7,6},{8,7},{9,8},{10,9},{11,1... | collective-permute-start | bytes 98312 | tf_op jit(solution)/shard_map/ppermute | solution.py:18
  263.1 7.0 %collective-permute-start.34 = (f32[32,2,128]{2,0,1:T(8,128)S(1)}, f32[32,2,128]{2,0,1:T(8,128)S(1)}, u32[]{:S(2)}, u32[]{:S(2)}) collective-permute-start(f32[32,2,128]{2,0,1:T(8,128)S(1)} %get-tuple-element.26), channel_id=1, source_target_pairs={{0,1},{1,2},{2,3},{3,4},{4,5},{5,6},{6,7},{7,8},{8,9},{9,10},{10,1... | collective-permute-start | bytes 98312 | tf_op jit(solution)/shard_map/ppermute | solution.py:18
  271.9 8.2 %collective-permute-start.37 = (f32[32,2,128]{2,0,1:T(8,128)S(1)}, f32[32,2,128]{2,0,1:T(8,128)S(1)}, u32[]{:S(2)}, u32[]{:S(2)}) collective-permute-start(f32[32,2,128]{2,0,1:T(8,128)S(1)} %get-tuple-element.25), channel_id=1, source_target_pairs={{1,0},{2,1},{3,2},{4,3},{5,4},{6,5},{7,6},{8,7},{9,8},{10,9},{11,1... | collective-permute-start | bytes 98312 | tf_op jit(solution)/shard_map/ppermute | solution.py:18
  273.8 7.0 %collective-permute-start.36 = (f32[32,2,128]{2,0,1:T(8,128)S(1)}, f32[32,2,128]{2,0,1:T(8,128)S(1)}, u32[]{:S(2)}, u32[]{:S(2)}) collective-permute-start(f32[32,2,128]{2,0,1:T(8,128)S(1)} %get-tuple-element.24), channel_id=1, source_target_pairs={{0,1},{1,2},{2,3},{3,4},{4,5},{5,6},{6,7},{7,8},{8,9},{9,10},{10,1... | collective-permute-start | bytes 98312 | tf_op jit(solution)/shard_map/ppermute | solution.py:18
  282.6 8.0 %collective-permute-start.39 = (f32[32,2,128]{2,0,1:T(8,128)S(1)}, f32[32,2,128]{2,0,1:T(8,128)S(1)}, u32[]{:S(2)}, u32[]{:S(2)}) collective-permute-start(f32[32,2,128]{2,0,1:T(8,128)S(1)} %get-tuple-element.23), channel_id=1, source_target_pairs={{1,0},{2,1},{3,2},{4,3},{5,4},{6,5},{7,6},{8,7},{9,8},{10,9},{11,1... | collective-permute-start | bytes 98312 | tf_op jit(solution)/shard_map/ppermute | solution.py:18
  284.5 7.0 %collective-permute-start.38 = (f32[32,2,128]{2,0,1:T(8,128)S(1)}, f32[32,2,128]{2,0,1:T(8,128)S(1)}, u32[]{:S(2)}, u32[]{:S(2)}) collective-permute-start(f32[32,2,128]{2,0,1:T(8,128)S(1)} %get-tuple-element.22), channel_id=1, source_target_pairs={{0,1},{1,2},{2,3},{3,4},{4,5},{5,6},{6,7},{7,8},{8,9},{9,10},{10,1... | collective-permute-start | bytes 98312 | tf_op jit(solution)/shard_map/ppermute | solution.py:18
  294.7 8.0 %collective-permute-start.41 = (f32[32,2,128]{2,0,1:T(8,128)S(1)}, f32[32,2,128]{2,0,1:T(8,128)S(1)}, u32[]{:S(2)}, u32[]{:S(2)}) collective-permute-start(f32[32,2,128]{2,0,1:T(8,128)S(1)} %get-tuple-element.15), channel_id=1, source_target_pairs={{1,0},{2,1},{3,2},{4,3},{5,4},{6,5},{7,6},{8,7},{9,8},{10,9},{11,1... | collective-permute-start | bytes 98312 | tf_op jit(solution)/shard_map/ppermute | solution.py:18
  296.7 7.0 %collective-permute-start.40 = (f32[32,2,128]{2,0,1:T(8,128)S(1)}, f32[32,2,128]{2,0,1:T(8,128)S(1)}, u32[]{:S(2)}, u32[]{:S(2)}) collective-permute-start(f32[32,2,128]{2,0,1:T(8,128)S(1)} %get-tuple-element.14), channel_id=1, source_target_pairs={{0,1},{1,2},{2,3},{3,4},{4,5},{5,6},{6,7},{7,8},{8,9},{9,10},{10,1... | collective-permute-start | bytes 98312 | tf_op jit(solution)/shard_map/ppermute | solution.py:18
  310.3 8.0 %collective-permute-start.43 = (f32[32,2,128]{2,0,1:T(8,128)S(1)}, f32[32,2,128]{2,0,1:T(8,128)S(1)}, u32[]{:S(2)}, u32[]{:S(2)}) collective-permute-start(f32[32,2,128]{2,0,1:T(8,128)S(1)} %get-tuple-element.13), channel_id=1, source_target_pairs={{1,0},{2,1},{3,2},{4,3},{5,4},{6,5},{7,6},{8,7},{9,8},{10,9},{11,1... | collective-permute-start | bytes 98312 | tf_op jit(solution)/shard_map/ppermute | solution.py:18
  312.2 7.0 %collective-permute-start.42 = (f32[32,2,128]{2,0,1:T(8,128)S(1)}, f32[32,2,128]{2,0,1:T(8,128)S(1)}, u32[]{:S(2)}, u32[]{:S(2)}) collective-permute-start(f32[32,2,128]{2,0,1:T(8,128)S(1)} %get-tuple-element.12), channel_id=1, source_target_pairs={{0,1},{1,2},{2,3},{3,4},{4,5},{5,6},{6,7},{7,8},{8,9},{9,10},{10,1... | collective-permute-start | bytes 98312 | tf_op jit(solution)/shard_map/ppermute | solution.py:18
  325.8 8.0 %collective-permute-start.45 = (f32[32,2,128]{2,0,1:T(8,128)S(1)}, f32[32,2,128]{2,0,1:T(8,128)S(1)}, u32[]{:S(2)}, u32[]{:S(2)}) collective-permute-start(f32[32,2,128]{2,0,1:T(8,128)S(1)} %get-tuple-element.11), channel_id=1, source_target_pairs={{1,0},{2,1},{3,2},{4,3},{5,4},{6,5},{7,6},{8,7},{9,8},{10,9},{11,1... | collective-permute-start | bytes 98312 | tf_op jit(solution)/shard_map/ppermute | solution.py:18
  (26 other events, 391.9 us)
where the time goes:
time: 347 us; the launch traced here: 342 us
  starting transfers between devices  171 us (49%)
  local copies, waits for them, and re-layouts  77 us (22%)
  matrix products  55.9 us (16%)
  waiting for transfers between devices  35 us (10%)
    ppermute x46, starting transfers between devices, from_behind(): lax.ppermute(value, axis, [(source, source + steps) for source in range(i...  171 us
    unnamed x27, local copies, waits for them, and re-layouts  46.6 us
    dot_general x18, matrix products, tile_product(): jnp.einsum('tkrc,btkc->btr', blocks, picked, precision=lax.Precision.HIGH...  45.9 us
    ppermute x46, waiting for transfers between devices, from_behind(): lax.ppermute(value, axis, [(source, source + steps) for source in range(i...  35 us
    gather x3, local copies, waits for them, and re-layouts, level_diagonal(): jnp.diagonal(blocks, axis1=2, axis2=3) * own_hits[:, :, None]  11.2 us
    gather x18, local copies, waits for them, and re-layouts, tile_product(): picked = extended[:, columns]  10.5 us
  transfers between devices with their start and end apart: 46, of which 26 were waited for; matrix products, arithmetic and copies ran while one was open for 13% of the time, Pallas kernels for 0%

commit v1 on v0

v1 whole, which is shorter than its diff:
```python
import functools

import jax
import jax.numpy as jnp
from jax import lax
from jax.experimental import pallas as pl
from jax.experimental.pallas import tpu as pltpu
from jax.sharding import PartitionSpec as P

HALO = 2
COARSE_SWEEPS = 2
COARSEST_SWEEPS = 8
OMEGA = 0.7
AXES = ("parts", "pair")
NT = (((1,), (1,)), ((), ()))
NN = (((1,), (0,)), ((), ()))
F32 = jnp.float32
BF16 = jnp.bfloat16


def split(value):
    high = value.astype(BF16)
    return high, (value - high.astype(F32)).astype(BF16)


def stack(value):
    return jnp.concatenate(split(value), axis=0)


def fold_rows(value):
    half = value.shape[0] // 2
    return value[:half] + value[half:]


def product(stacked, weights, dims, width):
    full = lax.dot_general(stacked, weights, dims, preferred_element_type=F32)
    rows = full.shape[0] // 2
    return full[:rows, :width] + (full[:rows, width:] + full[rows:, :width])


def picked_sum(stacked, one_hot, dims):
    return fold_rows(lax.dot_general(stacked, one_hot, dims, preferred_element_type=F32))


def position():
    return lax.axis_index("parts") * lax.axis_size("pair") + lax.axis_index("pair")


def diagonal_row(block):
    size = block.shape[-1]
    rows = lax.broadcasted_iota(jnp.int32, (size, size), 0)
    lanes = lax.broadcasted_iota(jnp.int32, (size, size), 1)
    return jnp.sum(jnp.where(rows == lanes, block, 0.0), axis=0, keepdims=True)


def tile_diagonal(columns, blocks, tile):
    total = None
    for link in range(blocks.shape[1]):
        own = (columns[tile, link] == tile + HALO).astype(F32)
        term = diagonal_row(blocks[tile, link]) * own
        total = term if total is None else total + term
    return total


def get_tile(ref, tile, panels, width):
    if ref.shape[0] == panels:
        return ref[:, tile * width:(tile + 1) * width]
    return ref[pl.ds(tile * panels, panels)]


def put_tile(ref, tile, value, panels, width):
    if ref.shape[0] == panels and ref.shape[1] != width:
        ref[:, tile * width:(tile + 1) * width] = value
    else:
        ref[pl.ds(tile * panels, panels)] = value


def fill_extended(extended, vector, pair_halo, chip_halo, count, panels):
    core = lax.axis_index("pair")
    for tile in range(count):
        extended[tile + HALO] = stack(vector[pl.ds(tile * panels, panels)])
    for tile in range(HALO):
        rows = pl.ds(tile * panels, panels)
        extended[core * (count + HALO) + tile] = stack(chip_halo[rows])
        extended[(1 - core) * (count + HALO) + tile] = stack(pair_halo[rows])


def tile_apply(columns, blocks, extended, tile):
    links, width = blocks.shape[1], blocks.shape[-1]
    left = jnp.concatenate([extended[columns[tile, k]] for k in range(links)], axis=1)
    parts = [split(blocks[tile, k]) for k in range(links)]
    weights = jnp.concatenate(
        [jnp.concatenate([p[0] for p in parts], axis=1), jnp.concatenate([p[1] for p in parts], axis=1)], axis=0
    )
    return product(left, weights, NT, width)


def put_edges(vector, count, panels, pair_edge, chip_edge):
    core = lax.axis_index("pair")
    last = (count - HALO) * panels
    size = HALO * panels
    pair_edge[...] = vector[pl.ds(pl.multiple_of((1 - core) * last, panels), size)]
    chip_edge[...] = vector[pl.ds(pl.multiple_of(core * last, panels), size)]


def first_kernel(columns, source, blocks, diagonal, vector, pair_edge, chip_edge):
    panels = source.shape[0]
    count, width = blocks.shape[0], blocks.shape[-1]
    for tile in range(count):
        row = tile_diagonal(columns, blocks, tile)
        diagonal[pl.ds(tile, 1)] = row
        vector[pl.ds(tile * panels, panels)] = OMEGA * get_tile(source, tile, panels, width) / row
    put_edges(vector, count, panels, pair_edge, chip_edge)


def sweep_kernel(panels, edges, columns, vector, pair_halo, chip_halo, source, diagonal, blocks, result, *rest):
    extended = rest[-1]
    count, width = blocks.shape[0], blocks.shape[-1]
    fill_extended(extended, vector, pair_halo, chip_halo, count, panels)
    for tile in range(count):
        product_tile = tile_apply(columns, blocks, extended, tile)
        old = vector[pl.ds(tile * panels, panels)]
        new = old + OMEGA * (get_tile(source, tile, panels, width) - product_tile) / diagonal[pl.ds(tile, 1)]
        put_tile(result, tile, new, panels, width)
    if edges:
        put_edges(result, count, panels, rest[0], rest[1])


def residual_kernel(
    panels, columns, vector, pair_halo, chip_halo, source, blocks, aggregate, next_columns, next_blocks,
    next_source, next_diagonal, next_vector, pair_edge, chip_edge, extended,
):
    count, width = blocks.shape[0], blocks.shape[-1]
    next_count = next_blocks.shape[0]
    factor = count // next_count
    fill_extended(extended, vector, pair_halo, chip_halo, count, panels)
    for group in range(next_count):
        pieces = []
        for tile in range(group * factor, (group + 1) * factor):
            rest = get_tile(source, tile, panels, width) - tile_apply(columns, blocks, extended, tile)
            pieces.append(stack(rest))
        one_hot = one_hot_rows(aggregate[:, group * factor * width:(group + 1) * factor * width], width)
        gathered = picked_sum(jnp.concatenate(pieces, axis=1), one_hot, NT)
        row = tile_diagonal(next_columns, next_blocks, group)
        rows = pl.ds(group * panels, panels)
        next_source[rows] = gathered
        next_diagonal[pl.ds(group, 1)] = row
        next_vector[rows] = OMEGA * gathered / row
    put_edges(next_vector, next_count, panels, pair_edge, chip_edge)


def one_hot_rows(indices, width):
    rows = lax.broadcasted_iota(jnp.int32, (width, indices.shape[1]), 0)
    return (rows == indices).astype(F32).astype(BF16)


def one_hot_twice(indices, width):
    rows = lax.broadcasted_iota(jnp.int32, (width, indices.shape[1]), 0)
    half = width // 2
    return (jnp.where(rows < half, rows, rows - half) == indices).astype(F32).astype(BF16)


def prolong_kernel(
    panels, columns, vector, pair_halo, chip_halo, source, diagonal, blocks, aggregate, upper,
    next_vector, pair_edge, chip_edge, extended,
):
    count, width = blocks.shape[0], blocks.shape[-1]
    upper_count = upper.shape[0] // panels
    factor = upper_count // count
    fill_extended(extended, vector, pair_halo, chip_halo, count, panels)
    for tile in range(count):
        product_tile = tile_apply(columns, blocks, extended, tile)
        old = vector[pl.ds(tile * panels, panels)]
        new = old + OMEGA * (get_tile(source, tile, panels, width) - product_tile) / diagonal[pl.ds(tile, 1)]
        one_hot = one_hot_rows(aggregate[:, tile * factor * width:(tile + 1) * factor * width], width)
        lifted = picked_sum(stack(new), one_hot, NN)
        for k in range(factor):
            rows = pl.ds((tile * factor + k) * panels, panels)
            next_vector[rows] = upper[rows] + lifted[:, k * width:(k + 1) * width]
    put_edges(next_vector, upper_count, panels, pair_edge, chip_edge)


def chain_weights(operators, depths):
    weights, diagonals = [], []
    for level in range(depths):
        matrix = operators[0, level]
        weights.append(jnp.concatenate(split(matrix), axis=0))
        diagonals.append(diagonal_row(matrix))
    return weights, diagonals


def coarse_apply(weights, value):
    return product(stack(value), weights, NT, value.shape[1])


def coarse_sweeps(weights, diagonal, source, value, sweeps):
    for _ in range(sweeps):
        value = value + OMEGA * (source - coarse_apply(weights, value)) / diagonal
    return value


def lane_half(rows, width):
    return (lax.broadcasted_iota(jnp.int32, (rows, width), 1) >= width // 2).astype(jnp.int32)


def maps_kernel(operators, maps, result):
    depths, width = operators.shape[1], operators.shape[-1]
    half = width // 2
    here = position()
    weights, diagonals = chain_weights(operators, depths - 1)
    lanes = lax.broadcasted_iota(jnp.int32, (half, width), 1)
    rows = lax.broadcasted_iota(jnp.int32, (half, width), 0)
    piece = (jnp.where(lanes < half, lanes, lanes - half) == rows).astype(F32)
    halves = lane_half(half, width)
    for level in range(depths):
        high, low = split(piece)
        result[:, 2 * level * width:(2 * level + 1) * width] = high
        result[:, (2 * level + 1) * width:(2 * level + 2) * width] = low
        if level < depths - 1:
            bit = (here >> level) & 1
            merged = jnp.where(halves == bit, piece, 0.0)
            value = coarse_sweeps(
                weights[level], diagonals[level], merged, OMEGA * merged / diagonals[level], COARSE_SWEEPS - 1
            )
            rest = merged - coarse_apply(weights[level], value)
            piece = picked_sum(stack(rest), one_hot_twice(maps[0, pl.ds(level, 1)], width), NT)


def lowest_kernel(
    panels, columns, vector, pair_halo, chip_halo, source, blocks, aggregate, images,
    own_piece, outgoing, extended,
):
    count, width = blocks.shape[0], blocks.shape[-1]
    half = width // 2
    here = position()
    fill_extended(extended, vector, pair_halo, chip_halo, count, panels)
    pieces = []
    for tile in range(count):
        rest = get_tile(source, tile, panels, width) - tile_apply(columns, blocks, extended, tile)
        pieces.append(stack(rest))
    one_hot = one_hot_twice(aggregate[...], width)
    gathered = picked_sum(jnp.concatenate(pieces, axis=1), one_hot, NT)
    own_piece[...] = gathered
    shares = lax.dot_general(stack(gathered)[:, :half], images[...], NN, preferred_element_type=F32)
    depths = images.shape[1] // (2 * width)
    top = lax.broadcasted_iota(jnp.int32, (panels // 2, width), 1) < half
    for level in range(depths):
        low = shares[:, 2 * level * width:(2 * level + 2) * width]
        share = low[:panels, :width] + (low[:panels, width:] + low[panels:, :width])
        packed = jnp.where(top, share[:panels // 2], share[panels // 2:])
        start = ((here >> level) ^ 1) << level
        if level == 0:
            outgoing[pl.ds(here, 1)] = packed[None]
        outgoing[pl.ds(start, 2**level)] = jnp.broadcast_to(packed[None], (2**level,) + packed.shape)


def chain_kernel(panels, own_piece, incoming, operators, maps, aggregate, upper, result):
    depths, width = operators.shape[1], operators.shape[-1]
    half = width // 2
    here = position()
    weights, diagonals = chain_weights(operators, depths)
    halves = lane_half(panels, width)
    top = lax.broadcasted_iota(jnp.int32, (panels // 2, width), 1) < half
    piece = own_piece[...]
    stored = []
    for level in range(depths):
        bit = (here >> level) & 1
        start = ((here >> level) ^ 1) << level
        packed = jnp.sum(incoming[pl.ds(start, 2**level)], axis=0)
        swapped = jnp.concatenate([packed[:, half:], packed[:, :half]], axis=1)
        other = jnp.concatenate([jnp.where(top, packed, swapped), jnp.where(top, swapped, packed)], axis=0)
        merged = jnp.where(halves == bit, piece, other)
        sweeps = COARSEST_SWEEPS if level == depths - 1 else COARSE_SWEEPS
        value = coarse_sweeps(weights[level], diagonals[level], merged, OMEGA * merged / diagonals[level], sweeps - 1)
        stored.append((merged, value))
        if level < depths - 1:
            rest = merged - coarse_apply(weights[level], value)
            piece = picked_sum(stack(rest), one_hot_twice(maps[0, pl.ds(level, 1)], width), NT)
    for level in reversed(range(depths)):
        merged, below = stored[level]
        if level < depths - 1:
            bit = (here >> (level + 1)) & 1
            one_hot = one_hot_rows(maps[0, pl.ds(level, 1)] + bit * half, width)
            value = below + picked_sum(stack(value), one_hot, NN)
            value = coarse_sweeps(weights[level], diagonals[level], merged, value, COARSE_SWEEPS)
    one_hot = one_hot_rows(aggregate[...] + (here & 1) * half, width)
    lifted = picked_sum(stack(value), one_hot, NN)
    for tile in range(aggregate.shape[1] // width):
        rows = pl.ds(tile * panels, panels)
        result[rows] = upper[rows] + lifted[:, tile * width:(tile + 1) * width]


def call(kernel, shapes, operands, scalars=(), scratch=(), name=None):
    vmem = pl.BlockSpec(memory_space=pltpu.VMEM)
    smem = pl.BlockSpec(memory_space=pltpu.SMEM)
    specs = [smem if k in scalars else vmem for k in range(len(operands))]
    outs = pl.pallas_call(
        kernel,
        out_shape=[jax.ShapeDtypeStruct(s, t) for s, t in shapes],
        in_specs=specs,
        out_specs=[vmem] * len(shapes),
        scratch_shapes=list(scratch),
        compiler_params=pltpu.CompilerParams(vmem_limit_bytes=32 * 2**20),
        name=name,
    )(*operands)
    return outs


def swaps(pairs):
    return [p for a, b in pairs for p in ((a, b), (b, a))]


def exchange(pair_edge, chip_edge):
    count = lax.axis_size(AXES)
    inner = swaps([(2 * k, 2 * k + 1) for k in range(count // 2)])
    outer = swaps([(2 * k + 1, 2 * k + 2) for k in range(count // 2 - 1)])
    return lax.ppermute(pair_edge, AXES, inner), lax.ppermute(chip_edge, AXES, outer)


def on_device(
    pulse_rhs, blocks_fine, columns_fine, aggregate_fine, blocks_mid, columns_mid, aggregate_mid,
    blocks_low, columns_low, aggregate_low, coarse_ops, coarse_maps,
):
    panels, width = pulse_rhs.shape[0], blocks_fine.shape[-1]
    devices = lax.axis_size(AXES)
    blocks = (blocks_fine, blocks_mid, blocks_low)
    columns = (columns_fine, columns_mid, columns_low)
    aggregates = tuple(a.reshape(1, -1) for a in (aggregate_fine, aggregate_mid, aggregate_low))
    counts = tuple(b.shape[0] for b in blocks)
    depths = coarse_ops.shape[1]

    def vec(level):
        return ((counts[level] * panels, width), F32)

    def diag(level):
        return ((counts[level], width), F32)

    edge = ((HALO * panels, width), F32)

    def ext(level):
        return [pltpu.VMEM((counts[level] + 2 * HALO, 2 * panels, width), BF16)]

    def sweep(level, vector, halos, last=False):
        shapes = [(pulse_rhs.shape, F32)] if last else [vec(level), edge, edge]
        outs = call(
            functools.partial(sweep_kernel, panels, not last),
            shapes,
            (columns[level], vector, *halos, sources[level], diagonals[level], blocks[level]),
            scalars=(0,), scratch=ext(level), name=f"sweep{level}",
        )
        return outs[0] if last else (outs[0], exchange(outs[1], outs[2]))

    images = call(maps_kernel, [((width // 2, 2 * depths * width), BF16)], (coarse_ops, coarse_maps), name="maps")[0]
    sources, diagonals, kept = [pulse_rhs], [], []
    diagonal, vector, pair_edge, chip_edge = call(
        first_kernel, [diag(0), vec(0), edge, edge], (columns[0], pulse_rhs, blocks[0]), scalars=(0,), name="first"
    )
    diagonals.append(diagonal)
    halos = exchange(pair_edge, chip_edge)
    for level in range(3):
        vector, halos = sweep(level, vector, halos)
        vector, halos = sweep(level, vector, halos)
        kept.append(vector)
        if level < 2:
            source, diagonal, vector, pair_edge, chip_edge = call(
                functools.partial(residual_kernel, panels),
                [vec(level + 1), diag(level + 1), vec(level + 1), edge, edge],
                (columns[level], vector, *halos, sources[level], blocks[level], aggregates[level],
                 columns[level + 1], blocks[level + 1]),
                scalars=(0, 7), scratch=ext(level), name=f"residual{level}",
            )
            sources.append(source)
            diagonals.append(diagonal)
            halos = exchange(pair_edge, chip_edge)
    own_piece, outgoing = call(
        functools.partial(lowest_kernel, panels),
        [((panels, width), F32), ((devices, panels // 2, width), F32)],
        (columns[2], vector, *halos, sources[2], blocks[2], aggregates[2], images),
        scalars=(0,), scratch=ext(2), name="lowest",
    )
    incoming = lax.all_to_all(outgoing, AXES, 0, 0)
    vector = call(
        functools.partial(chain_kernel, panels), [vec(2)],
        (own_piece, incoming, coarse_ops, coarse_maps, aggregates[2], kept[2]), name="chain",
    )[0]
    halos = exchange(vector, vector)
    for level in (2, 1, 0):
        vector, halos = sweep(level, vector, halos)
        vector, halos = sweep(level, vector, halos)
        if level == 0:
            return sweep(0, vector, halos, last=True)
        vector, pair_edge, chip_edge = call(
            functools.partial(prolong_kernel, panels), [vec(level - 1), edge, edge],
            (columns[level], vector, *halos, sources[level], diagonals[level], blocks[level],
             aggregates[level - 1], kept[level - 1]),
            scalars=(0,), scratch=ext(level), name=f"prolong{level}",
        )
        halos = exchange(pair_edge, chip_edge)


def solution(mesh):
    split_first = P(AXES)
    rhs = P(None, AXES)
    return jax.shard_map(
        on_device, mesh=mesh, in_specs=(rhs,) + (split_first,) * 11, out_specs=rhs, check_vma=False
    )
```

time: 347 us -> 180 us (0.52)
  starting transfers between devices: 171 us -> 70.1 us
  local copies, waits for them, and re-layouts: 77 us -> 3.96 us
  matrix products: 55.9 us -> 0 us
  Pallas kernels: 0 us -> 33.7 us
  waiting for transfers between devices: 35 us -> 56.8 us
  blocking collectives: 0 us -> 13.3 us
    ppermute x46 -> x36, starting transfers between devices: 171 us -> 70.1 us  [the longest x18 68.2 us: exchange(): lax.ppermute(chip_edge, AXES, outer)]
    dot_general x55 -> x0, matrix products: 55.9 us -> none  [the longest x18 45.9 us: tile_product(): jnp.einsum('tkrc,btkc->btr', blocks, picked, precision=lax.Precision.HIGH...]
    unnamed x27, local copies, waits for them, and re-layouts: 46.6 us -> 3.96 us
    pallas_call x0 -> x21, Pallas kernels: none -> 33.7 us  [call(): pl.pallas_call(kernel, out_shape=[jax.ShapeDtypeStruct(s, t) for s, t in...]
    gather x26 -> x0, local copies, waits for them, and re-layouts: 27.9 us -> none  [the longest x3 11.2 us: level_diagonal(): jnp.diagonal(blocks, axis1=2, axis2=3) * own_hits[:, :, None]]
    ppermute x46 -> x36, waiting for transfers between devices: 35 us -> 56.8 us  [the longest x18 56.8 us: exchange(): lax.ppermute(chip_edge, AXES, outer)]
    all_to_all x0 -> x1, blocking collectives: none -> 13.3 us  [on_device(): incoming = lax.all_to_all(outgoing, AXES, 0, 0)]
  transfers between devices with their start and end apart: 46 -> 36, of which waited for: 26 -> 18; matrix products, arithmetic and copies ran while one was open for 13% -> 0% of each run, Pallas kernels for 0% -> 1%
where the time goes in v1:
time: 180 us; the launch traced here: 178 us
  starting transfers between devices  70.1 us (39%)
  waiting for transfers between devices  56.8 us (32%)
  Pallas kernels  33.7 us (19%)
  blocking collectives  13.3 us (7%)
  local copies, waits for them, and re-layouts  3.96 us (2%)
    ppermute x18, starting transfers between devices, exchange(): lax.ppermute(chip_edge, AXES, outer)  68.2 us
    ppermute x18, waiting for transfers between devices, exchange(): lax.ppermute(chip_edge, AXES, outer)  56.8 us
    pallas_call x21, Pallas kernels, call(): pl.pallas_call(kernel, out_shape=[jax.ShapeDtypeStruct(s, t) for s, t in...  33.7 us
    all_to_all x1, blocking collectives, on_device(): incoming = lax.all_to_all(outgoing, AXES, 0, 0)  13.3 us
    unnamed x27, local copies, waits for them, and re-layouts  3.96 us
  transfers between devices with their start and end apart: 36, of which 18 were waited for; matrix products, arithmetic and copies ran while one was open for 0% of the time, Pallas kernels for 1%

profile of v1, /device:TPU:7, one launch (start us, length us, event | category | flops | bytes accessed | tf_op | source)
XLA Modules:
  0.0 178.5 jit_solution(11432285202550310710)
XLA Ops:
  5.7 3.0 %collective-permute-start.1 = (f32[64,128]{1,0:T(8,128)S(1)}, f32[64,128]{1,0:T(8,128)S(1)}, u32[]{:S(2)}, u32[]{:S(2)}) collective-permute-start(f32[64,128]{1,0:T(8,128)S(1)} %get-tuple-element.65), channel_id=1, source_target_pairs={{1,2},{2,1},{3,4},{4,3},{5,6},{6,5},{7,8},{8,7},{9,10},{10,9},{11,... | collective-permute-start | bytes 98312 | tf_op jit(solution)/shard_map/ppermute | solution.py:317
  8.7 4.0 %collective-permute-done.1.chip_halo = f32[64,128]{1,0:T(8,128)S(1)} collective-permute-done((f32[64,128]{1,0:T(8,128)S(1)}, f32[64,128]{1,0:T(8,128)S(1)}, u32[]{:S(2)}, u32[]{:S(2)}) %collective-permute-start.1) | collective-permute-done | bytes 32800 | tf_op jit(solution)/shard_map/ppermute | solution.py:317
  14.9 3.1 %collective-permute-start.3 = (f32[64,128]{1,0:T(8,128)S(1)}, f32[64,128]{1,0:T(8,128)S(1)}, u32[]{:S(2)}, u32[]{:S(2)}) collective-permute-start(f32[64,128]{1,0:T(8,128)S(1)} %get-tuple-element.69), channel_id=1, source_target_pairs={{1,2},{2,1},{3,4},{4,3},{5,6},{6,5},{7,8},{8,7},{9,10},{10,9},{11,... | collective-permute-start | bytes 98312 | tf_op jit(solution)/shard_map/ppermute | solution.py:317
  18.1 3.9 %collective-permute-done.3.chip_halo = f32[64,128]{1,0:T(8,128)S(1)} collective-permute-done((f32[64,128]{1,0:T(8,128)S(1)}, f32[64,128]{1,0:T(8,128)S(1)}, u32[]{:S(2)}, u32[]{:S(2)}) %collective-permute-start.3) | collective-permute-done | bytes 32800 | tf_op jit(solution)/shard_map/ppermute | solution.py:317
  24.2 3.3 %collective-permute-start.5 = (f32[64,128]{1,0:T(8,128)S(1)}, f32[64,128]{1,0:T(8,128)S(1)}, u32[]{:S(2)}, u32[]{:S(2)}) collective-permute-start(f32[64,128]{1,0:T(8,128)S(1)} %get-tuple-element.72), channel_id=1, source_target_pairs={{1,2},{2,1},{3,4},{4,3},{5,6},{6,5},{7,8},{8,7},{9,10},{10,9},{11,... | collective-permute-start | bytes 98312 | tf_op jit(solution)/shard_map/ppermute | solution.py:317
  27.4 3.9 %collective-permute-done.5.chip_halo = f32[64,128]{1,0:T(8,128)S(1)} collective-permute-done((f32[64,128]{1,0:T(8,128)S(1)}, f32[64,128]{1,0:T(8,128)S(1)}, u32[]{:S(2)}, u32[]{:S(2)}) %collective-permute-start.5) | collective-permute-done | bytes 32800 | tf_op jit(solution)/shard_map/ppermute | solution.py:317
  34.1 3.3 %collective-permute-start.7 = (f32[64,128]{1,0:T(8,128)S(1)}, f32[64,128]{1,0:T(8,128)S(1)}, u32[]{:S(2)}, u32[]{:S(2)}) collective-permute-start(f32[64,128]{1,0:T(8,128)S(1)} %get-tuple-element.75), channel_id=1, source_target_pairs={{1,2},{2,1},{3,4},{4,3},{5,6},{6,5},{7,8},{8,7},{9,10},{10,9},{11,... | collective-permute-start | bytes 98312 | tf_op jit(solution)/shard_map/ppermute | solution.py:317
  37.4 3.9 %collective-permute-done.7.chip_halo = f32[64,128]{1,0:T(8,128)S(1)} collective-permute-done((f32[64,128]{1,0:T(8,128)S(1)}, f32[64,128]{1,0:T(8,128)S(1)}, u32[]{:S(2)}, u32[]{:S(2)}) %collective-permute-start.7) | collective-permute-done | bytes 32800 | tf_op jit(solution)/shard_map/ppermute | solution.py:317
  42.4 3.1 %collective-permute-start.9 = (f32[64,128]{1,0:T(8,128)S(1)}, f32[64,128]{1,0:T(8,128)S(1)}, u32[]{:S(2)}, u32[]{:S(2)}) collective-permute-start(f32[64,128]{1,0:T(8,128)S(1)} %get-tuple-element.80), channel_id=1, source_target_pairs={{1,2},{2,1},{3,4},{4,3},{5,6},{6,5},{7,8},{8,7},{9,10},{10,9},{11,... | collective-permute-start | bytes 98312 | tf_op jit(solution)/shard_map/ppermute | solution.py:317
  45.5 3.9 %collective-permute-done.9.chip_halo = f32[64,128]{1,0:T(8,128)S(1)} collective-permute-done((f32[64,128]{1,0:T(8,128)S(1)}, f32[64,128]{1,0:T(8,128)S(1)}, u32[]{:S(2)}, u32[]{:S(2)}) %collective-permute-start.9) | collective-permute-done | bytes 32800 | tf_op jit(solution)/shard_map/ppermute | solution.py:317
  50.5 3.1 %collective-permute-start.11 = (f32[64,128]{1,0:T(8,128)S(1)}, f32[64,128]{1,0:T(8,128)S(1)}, u32[]{:S(2)}, u32[]{:S(2)}) collective-permute-start(f32[64,128]{1,0:T(8,128)S(1)} %get-tuple-element.83), channel_id=1, source_target_pairs={{1,2},{2,1},{3,4},{4,3},{5,6},{6,5},{7,8},{8,7},{9,10},{10,9},{11,... | collective-permute-start | bytes 98312 | tf_op jit(solution)/shard_map/ppermute | solution.py:317
  53.6 3.9 %collective-permute-done.11.chip_halo = f32[64,128]{1,0:T(8,128)S(1)} collective-permute-done((f32[64,128]{1,0:T(8,128)S(1)}, f32[64,128]{1,0:T(8,128)S(1)}, u32[]{:S(2)}, u32[]{:S(2)}) %collective-permute-start.11) | collective-permute-done | bytes 32800 | tf_op jit(solution)/shard_map/ppermute | solution.py:317
  58.9 3.1 %collective-permute-start.13 = (f32[64,128]{1,0:T(8,128)S(1)}, f32[64,128]{1,0:T(8,128)S(1)}, u32[]{:S(2)}, u32[]{:S(2)}) collective-permute-start(f32[64,128]{1,0:T(8,128)S(1)} %get-tuple-element.86), channel_id=1, source_target_pairs={{1,2},{2,1},{3,4},{4,3},{5,6},{6,5},{7,8},{8,7},{9,10},{10,9},{11,... | collective-permute-start | bytes 98312 | tf_op jit(solution)/shard_map/ppermute | solution.py:317
  62.0 3.9 %collective-permute-done.13.chip_halo = f32[64,128]{1,0:T(8,128)S(1)} collective-permute-done((f32[64,128]{1,0:T(8,128)S(1)}, f32[64,128]{1,0:T(8,128)S(1)}, u32[]{:S(2)}, u32[]{:S(2)}) %collective-permute-start.13) | collective-permute-done | bytes 32800 | tf_op jit(solution)/shard_map/ppermute | solution.py:317
  66.8 3.1 %collective-permute-start.15 = (f32[64,128]{1,0:T(8,128)S(1)}, f32[64,128]{1,0:T(8,128)S(1)}, u32[]{:S(2)}, u32[]{:S(2)}) collective-permute-start(f32[64,128]{1,0:T(8,128)S(1)} %get-tuple-element.91), channel_id=1, source_target_pairs={{1,2},{2,1},{3,4},{4,3},{5,6},{6,5},{7,8},{8,7},{9,10},{10,9},{11,... | collective-permute-start | bytes 98312 | tf_op jit(solution)/shard_map/ppermute | solution.py:317
  70.0 3.9 %collective-permute-done.15.chip_halo = f32[64,128]{1,0:T(8,128)S(1)} collective-permute-done((f32[64,128]{1,0:T(8,128)S(1)}, f32[64,128]{1,0:T(8,128)S(1)}, u32[]{:S(2)}, u32[]{:S(2)}) %collective-permute-start.15) | collective-permute-done | bytes 32800 | tf_op jit(solution)/shard_map/ppermute | solution.py:317
  74.8 3.4 %collective-permute-start.17 = (f32[64,128]{1,0:T(8,128)S(1)}, f32[64,128]{1,0:T(8,128)S(1)}, u32[]{:S(2)}, u32[]{:S(2)}) collective-permute-start(f32[64,128]{1,0:T(8,128)S(1)} %get-tuple-element.94), channel_id=1, source_target_pairs={{1,2},{2,1},{3,4},{4,3},{5,6},{6,5},{7,8},{8,7},{9,10},{10,9},{11,... | collective-permute-start | bytes 98312 | tf_op jit(solution)/shard_map/ppermute | solution.py:317
  83.3 13.3 %all_to_all.5.incoming = f32[32,16,128]{2,1,0:T(8,128)S(1)} all-to-all(f32[32,16,128]{2,1,0:T(8,128)S(1)} %get-tuple-element.96), channel_id=1, replica_groups=mesh['parts'=16,'pair'=2] {'parts','pair'}, dimensions={0} | all-to-all | bytes 524288 | tf_op jit(solution)/shard_map/all_to_all | solution.py:381
  96.6 4.2 %chain.1.vector = f32[64,128]{1,0:T(8,128)S(1)} custom-call(f32[32,128]{1,0:T(8,128)S(1)} %get-tuple-element.95.own_piece, f32[32,16,128]{2,1,0:T(8,128)S(1)} %all_to_all.5.incoming, f32[1,5,128,128]{3,2,1,0:T(8,128)S(1)} %copy-done.6, s32[1,4,128]{2,1,0:T(4,128)S(1)} %copy-done.10, s32[1,256]{1,0:T(1,128)S(1)} %bitcast.8, ...), custom_call_target="tpu_custom_call" | custom-call | tf_op jit(solution)/shard_map/chain/pallas_call | solution.py:297
  100.8 4.4 %collective-permute-start.19 = (f32[64,128]{1,0:T(8,128)S(1)}, f32[64,128]{1,0:T(8,128)S(1)}, u32[]{:S(2)}, u32[]{:S(2)}) collective-permute-start(f32[64,128]{1,0:T(8,128)S(1)} %chain.1.vector), channel_id=1, source_target_pairs={{1,2},{2,1},{3,4},{4,3},{5,6},{6,5},{7,8},{8,7},{9,10},{10,9},{11,... | collective-permute-start | bytes 98312 | tf_op jit(solution)/shard_map/ppermute | solution.py:317
  108.8 4.4 %collective-permute-start.21 = (f32[64,128]{1,0:T(8,128)S(1)}, f32[64,128]{1,0:T(8,128)S(1)}, u32[]{:S(2)}, u32[]{:S(2)}) collective-permute-start(f32[64,128]{1,0:T(8,128)S(1)} %get-tuple-element.99), channel_id=1, source_target_pairs={{1,2},{2,1},{3,4},{4,3},{5,6},{6,5},{7,8},{8,7},{9,10},{10,9},{11,... | collective-permute-start | bytes 98312 | tf_op jit(solution)/shard_map/ppermute | solution.py:317
  113.2 2.6 %collective-permute-done.21.chip_halo = f32[64,128]{1,0:T(8,128)S(1)} collective-permute-done((f32[64,128]{1,0:T(8,128)S(1)}, f32[64,128]{1,0:T(8,128)S(1)}, u32[]{:S(2)}, u32[]{:S(2)}) %collective-permute-start.21) | collective-permute-done | bytes 32800 | tf_op jit(solution)/shard_map/ppermute | solution.py:317
  116.7 4.4 %collective-permute-start.23 = (f32[64,128]{1,0:T(8,128)S(1)}, f32[64,128]{1,0:T(8,128)S(1)}, u32[]{:S(2)}, u32[]{:S(2)}) collective-permute-start(f32[64,128]{1,0:T(8,128)S(1)} %get-tuple-element.102), channel_id=1, source_target_pairs={{1,2},{2,1},{3,4},{4,3},{5,6},{6,5},{7,8},{8,7},{9,10},{10,9},{11,... | collective-permute-start | bytes 98312 | tf_op jit(solution)/shard_map/ppermute | solution.py:317
  125.1 4.4 %collective-permute-start.25 = (f32[64,128]{1,0:T(8,128)S(1)}, f32[64,128]{1,0:T(8,128)S(1)}, u32[]{:S(2)}, u32[]{:S(2)}) collective-permute-start(f32[64,128]{1,0:T(8,128)S(1)} %get-tuple-element.105), channel_id=1, source_target_pairs={{1,2},{2,1},{3,4},{4,3},{5,6},{6,5},{7,8},{8,7},{9,10},{10,9},{11,... | collective-permute-start | bytes 98312 | tf_op jit(solution)/shard_map/ppermute | solution.py:317
  133.2 4.4 %collective-permute-start.27 = (f32[64,128]{1,0:T(8,128)S(1)}, f32[64,128]{1,0:T(8,128)S(1)}, u32[]{:S(2)}, u32[]{:S(2)}) collective-permute-start(f32[64,128]{1,0:T(8,128)S(1)} %get-tuple-element.108), channel_id=1, source_target_pairs={{1,2},{2,1},{3,4},{4,3},{5,6},{6,5},{7,8},{8,7},{9,10},{10,9},{11,... | collective-permute-start | bytes 98312 | tf_op jit(solution)/shard_map/ppermute | solution.py:317
  141.3 4.4 %collective-permute-start.29 = (f32[64,128]{1,0:T(8,128)S(1)}, f32[64,128]{1,0:T(8,128)S(1)}, u32[]{:S(2)}, u32[]{:S(2)}) collective-permute-start(f32[64,128]{1,0:T(8,128)S(1)} %get-tuple-element.111), channel_id=1, source_target_pairs={{1,2},{2,1},{3,4},{4,3},{5,6},{6,5},{7,8},{8,7},{9,10},{10,9},{11,... | collective-permute-start | bytes 98312 | tf_op jit(solution)/shard_map/ppermute | solution.py:317
  150.3 4.6 %collective-permute-start.31 = (f32[64,128]{1,0:T(8,128)S(1)}, f32[64,128]{1,0:T(8,128)S(1)}, u32[]{:S(2)}, u32[]{:S(2)}) collective-permute-start(f32[64,128]{1,0:T(8,128)S(1)} %get-tuple-element.114), channel_id=1, source_target_pairs={{1,2},{2,1},{3,4},{4,3},{5,6},{6,5},{7,8},{8,7},{9,10},{10,9},{11,... | collective-permute-start | bytes 98312 | tf_op jit(solution)/shard_map/ppermute | solution.py:317
  159.5 4.4 %collective-permute-start.33 = (f32[64,128]{1,0:T(8,128)S(1)}, f32[64,128]{1,0:T(8,128)S(1)}, u32[]{:S(2)}, u32[]{:S(2)}) collective-permute-start(f32[64,128]{1,0:T(8,128)S(1)} %get-tuple-element.117), channel_id=1, source_target_pairs={{1,2},{2,1},{3,4},{4,3},{5,6},{6,5},{7,8},{8,7},{9,10},{10,9},{11,... | collective-permute-start | bytes 98312 | tf_op jit(solution)/shard_map/ppermute | solution.py:317
  163.9 2.6 %collective-permute-done.33.chip_halo = f32[64,128]{1,0:T(8,128)S(1)} collective-permute-done((f32[64,128]{1,0:T(8,128)S(1)}, f32[64,128]{1,0:T(8,128)S(1)}, u32[]{:S(2)}, u32[]{:S(2)}) %collective-permute-start.33) | collective-permute-done | bytes 32800 | tf_op jit(solution)/shard_map/ppermute | solution.py:317
  168.7 4.4 %collective-permute-start.35 = (f32[64,128]{1,0:T(8,128)S(1)}, f32[64,128]{1,0:T(8,128)S(1)}, u32[]{:S(2)}, u32[]{:S(2)}) collective-permute-start(f32[64,128]{1,0:T(8,128)S(1)} %get-tuple-element.120), channel_id=1, source_target_pairs={{1,2},{2,1},{3,4},{4,3},{5,6},{6,5},{7,8},{8,7},{9,10},{10,9},{11,... | collective-permute-start | bytes 98312 | tf_op jit(solution)/shard_map/ppermute | solution.py:317
  173.1 2.6 %collective-permute-done.35.chip_halo = f32[64,128]{1,0:T(8,128)S(1)} collective-permute-done((f32[64,128]{1,0:T(8,128)S(1)}, f32[64,128]{1,0:T(8,128)S(1)}, u32[]{:S(2)}, u32[]{:S(2)}) %collective-permute-start.35) | collective-permute-done | bytes 32800 | tf_op jit(solution)/shard_map/ppermute | solution.py:317
  175.7 2.8 %sweep0.9 = f32[32,2048]{1,0:T(8,128)} custom-call(s32[16,4]{1,0:T(8,128)S(1)} %copy.19.columns, f32[512,128]{1,0:T(8,128)S(1)} %get-tuple-element.118.vector, f32[64,128]{1,0:T(8,128)S(1)} %collective-permute-done.34.pair_halo, f32[64,128]{1,0:T(8,128)S(1)} %collective-permute-done.35.chip_halo, f32[32,2048]{1,0:T(8,128)S(1)} %copy-done.5, ...), custom_call_target="tpu_custom_call" | custom-call | tf_op jit(solution)/shard_map/sweep0/pallas_call | solution.py:297
  (89 shorter events, 50.3 us)
Async XLA Ops:
  4.9 3.8 %collective-permute-start = (f32[64,128]{1,0:T(8,128)S(1)}, f32[64,128]{1,0:T(8,128)S(1)}, u32[]{:S(2)}, u32[]{:S(2)}) collective-permute-start(f32[64,128]{1,0:T(8,128)S(1)} %get-tuple-element.64), channel_id=1, source_target_pairs={{0,1},{1,0},{2,3},{3,2},{4,5},{5,4},{6,7},{7,6},{8,9},{9,8},{10,11... | collective-permute-start | bytes 98312 | tf_op jit(solution)/shard_map/ppermute | solution.py:317
  5.7 7.0 %collective-permute-start.1 = (f32[64,128]{1,0:T(8,128)S(1)}, f32[64,128]{1,0:T(8,128)S(1)}, u32[]{:S(2)}, u32[]{:S(2)}) collective-permute-start(f32[64,128]{1,0:T(8,128)S(1)} %get-tuple-element.65), channel_id=1, source_target_pairs={{1,2},{2,1},{3,4},{4,3},{5,6},{6,5},{7,8},{8,7},{9,10},{10,9},{11,... | collective-permute-start | bytes 98312 | tf_op jit(solution)/shard_map/ppermute | solution.py:317
  14.8 3.2 %collective-permute-start.2 = (f32[64,128]{1,0:T(8,128)S(1)}, f32[64,128]{1,0:T(8,128)S(1)}, u32[]{:S(2)}, u32[]{:S(2)}) collective-permute-start(f32[64,128]{1,0:T(8,128)S(1)} %get-tuple-element.68), channel_id=1, source_target_pairs={{0,1},{1,0},{2,3},{3,2},{4,5},{5,4},{6,7},{7,6},{8,9},{9,8},{10,11... | collective-permute-start | bytes 98312 | tf_op jit(solution)/shard_map/ppermute | solution.py:317
  14.9 7.0 %collective-permute-start.3 = (f32[64,128]{1,0:T(8,128)S(1)}, f32[64,128]{1,0:T(8,128)S(1)}, u32[]{:S(2)}, u32[]{:S(2)}) collective-permute-start(f32[64,128]{1,0:T(8,128)S(1)} %get-tuple-element.69), channel_id=1, source_target_pairs={{1,2},{2,1},{3,4},{4,3},{5,6},{6,5},{7,8},{8,7},{9,10},{10,9},{11,... | collective-permute-start | bytes 98312 | tf_op jit(solution)/shard_map/ppermute | solution.py:317
  24.1 3.4 %collective-permute-start.4 = (f32[64,128]{1,0:T(8,128)S(1)}, f32[64,128]{1,0:T(8,128)S(1)}, u32[]{:S(2)}, u32[]{:S(2)}) collective-permute-start(f32[64,128]{1,0:T(8,128)S(1)} %get-tuple-element.71), channel_id=1, source_target_pairs={{0,1},{1,0},{2,3},{3,2},{4,5},{5,4},{6,7},{7,6},{8,9},{9,8},{10,11... | collective-permute-start | bytes 98312 | tf_op jit(solution)/shard_map/ppermute | solution.py:317
  24.2 7.2 %collective-permute-start.5 = (f32[64,128]{1,0:T(8,128)S(1)}, f32[64,128]{1,0:T(8,128)S(1)}, u32[]{:S(2)}, u32[]{:S(2)}) collective-permute-start(f32[64,128]{1,0:T(8,128)S(1)} %get-tuple-element.72), channel_id=1, source_target_pairs={{1,2},{2,1},{3,4},{4,3},{5,6},{6,5},{7,8},{8,7},{9,10},{10,9},{11,... | collective-permute-start | bytes 98312 | tf_op jit(solution)/shard_map/ppermute | solution.py:317
  34.0 3.4 %collective-permute-start.6 = (f32[64,128]{1,0:T(8,128)S(1)}, f32[64,128]{1,0:T(8,128)S(1)}, u32[]{:S(2)}, u32[]{:S(2)}) collective-permute-start(f32[64,128]{1,0:T(8,128)S(1)} %get-tuple-element.74), channel_id=1, source_target_pairs={{0,1},{1,0},{2,3},{3,2},{4,5},{5,4},{6,7},{7,6},{8,9},{9,8},{10,11... | collective-permute-start | bytes 98312 | tf_op jit(solution)/shard_map/ppermute | solution.py:317
  34.1 7.2 %collective-permute-start.7 = (f32[64,128]{1,0:T(8,128)S(1)}, f32[64,128]{1,0:T(8,128)S(1)}, u32[]{:S(2)}, u32[]{:S(2)}) collective-permute-start(f32[64,128]{1,0:T(8,128)S(1)} %get-tuple-element.75), channel_id=1, source_target_pairs={{1,2},{2,1},{3,4},{4,3},{5,6},{6,5},{7,8},{8,7},{9,10},{10,9},{11,... | collective-permute-start | bytes 98312 | tf_op jit(solution)/shard_map/ppermute | solution.py:317
  42.4 7.0 %collective-permute-start.9 = (f32[64,128]{1,0:T(8,128)S(1)}, f32[64,128]{1,0:T(8,128)S(1)}, u32[]{:S(2)}, u32[]{:S(2)}) collective-permute-start(f32[64,128]{1,0:T(8,128)S(1)} %get-tuple-element.80), channel_id=1, source_target_pairs={{1,2},{2,1},{3,4},{4,3},{5,6},{6,5},{7,8},{8,7},{9,10},{10,9},{11,... | collective-permute-start | bytes 98312 | tf_op jit(solution)/shard_map/ppermute | solution.py:317
  50.5 7.0 %collective-permute-start.11 = (f32[64,128]{1,0:T(8,128)S(1)}, f32[64,128]{1,0:T(8,128)S(1)}, u32[]{:S(2)}, u32[]{:S(2)}) collective-permute-start(f32[64,128]{1,0:T(8,128)S(1)} %get-tuple-element.83), channel_id=1, source_target_pairs={{1,2},{2,1},{3,4},{4,3},{5,6},{6,5},{7,8},{8,7},{9,10},{10,9},{11,... | collective-permute-start | bytes 98312 | tf_op jit(solution)/shard_map/ppermute | solution.py:317
  58.9 7.0 %collective-permute-start.13 = (f32[64,128]{1,0:T(8,128)S(1)}, f32[64,128]{1,0:T(8,128)S(1)}, u32[]{:S(2)}, u32[]{:S(2)}) collective-permute-start(f32[64,128]{1,0:T(8,128)S(1)} %get-tuple-element.86), channel_id=1, source_target_pairs={{1,2},{2,1},{3,4},{4,3},{5,6},{6,5},{7,8},{8,7},{9,10},{10,9},{11,... | collective-permute-start | bytes 98312 | tf_op jit(solution)/shard_map/ppermute | solution.py:317
  66.7 3.2 %collective-permute-start.14 = (f32[64,128]{1,0:T(8,128)S(1)}, f32[64,128]{1,0:T(8,128)S(1)}, u32[]{:S(2)}, u32[]{:S(2)}) collective-permute-start(f32[64,128]{1,0:T(8,128)S(1)} %get-tuple-element.90), channel_id=1, source_target_pairs={{0,1},{1,0},{2,3},{3,2},{4,5},{5,4},{6,7},{7,6},{8,9},{9,8},{10,11... | collective-permute-start | bytes 98312 | tf_op jit(solution)/shard_map/ppermute | solution.py:317
  66.8 7.0 %collective-permute-start.15 = (f32[64,128]{1,0:T(8,128)S(1)}, f32[64,128]{1,0:T(8,128)S(1)}, u32[]{:S(2)}, u32[]{:S(2)}) collective-permute-start(f32[64,128]{1,0:T(8,128)S(1)} %get-tuple-element.91), channel_id=1, source_target_pairs={{1,2},{2,1},{3,4},{4,3},{5,6},{6,5},{7,8},{8,7},{9,10},{10,9},{11,... | collective-permute-start | bytes 98312 | tf_op jit(solution)/shard_map/ppermute | solution.py:317
  74.7 5.2 %collective-permute-start.16 = (f32[64,128]{1,0:T(8,128)S(1)}, f32[64,128]{1,0:T(8,128)S(1)}, u32[]{:S(2)}, u32[]{:S(2)}) collective-permute-start(f32[64,128]{1,0:T(8,128)S(1)} %get-tuple-element.93), channel_id=1, source_target_pairs={{0,1},{1,0},{2,3},{3,2},{4,5},{5,4},{6,7},{7,6},{8,9},{9,8},{10,11... | collective-permute-start | bytes 98312 | tf_op jit(solution)/shard_map/ppermute | solution.py:317
  74.8 7.3 %collective-permute-start.17 = (f32[64,128]{1,0:T(8,128)S(1)}, f32[64,128]{1,0:T(8,128)S(1)}, u32[]{:S(2)}, u32[]{:S(2)}) collective-permute-start(f32[64,128]{1,0:T(8,128)S(1)} %get-tuple-element.94), channel_id=1, source_target_pairs={{1,2},{2,1},{3,4},{4,3},{5,6},{6,5},{7,8},{8,7},{9,10},{10,9},{11,... | collective-permute-start | bytes 98312 | tf_op jit(solution)/shard_map/ppermute | solution.py:317
  100.8 7.0 %collective-permute-start.19 = (f32[64,128]{1,0:T(8,128)S(1)}, f32[64,128]{1,0:T(8,128)S(1)}, u32[]{:S(2)}, u32[]{:S(2)}) collective-permute-start(f32[64,128]{1,0:T(8,128)S(1)} %chain.1.vector), channel_id=1, source_target_pairs={{1,2},{2,1},{3,4},{4,3},{5,6},{6,5},{7,8},{8,7},{9,10},{10,9},{11,... | collective-permute-start | bytes 98312 | tf_op jit(solution)/shard_map/ppermute | solution.py:317
  108.7 4.5 %collective-permute-start.20 = (f32[64,128]{1,0:T(8,128)S(1)}, f32[64,128]{1,0:T(8,128)S(1)}, u32[]{:S(2)}, u32[]{:S(2)}) collective-permute-start(f32[64,128]{1,0:T(8,128)S(1)} %get-tuple-element.98), channel_id=1, source_target_pairs={{0,1},{1,0},{2,3},{3,2},{4,5},{5,4},{6,7},{7,6},{8,9},{9,8},{10,11... | collective-permute-start | bytes 98312 | tf_op jit(solution)/shard_map/ppermute | solution.py:317
  108.8 7.0 %collective-permute-start.21 = (f32[64,128]{1,0:T(8,128)S(1)}, f32[64,128]{1,0:T(8,128)S(1)}, u32[]{:S(2)}, u32[]{:S(2)}) collective-permute-start(f32[64,128]{1,0:T(8,128)S(1)} %get-tuple-element.99), channel_id=1, source_target_pairs={{1,2},{2,1},{3,4},{4,3},{5,6},{6,5},{7,8},{8,7},{9,10},{10,9},{11,... | collective-permute-start | bytes 98312 | tf_op jit(solution)/shard_map/ppermute | solution.py:317
  116.7 4.5 %collective-permute-start.22 = (f32[64,128]{1,0:T(8,128)S(1)}, f32[64,128]{1,0:T(8,128)S(1)}, u32[]{:S(2)}, u32[]{:S(2)}) collective-permute-start(f32[64,128]{1,0:T(8,128)S(1)} %get-tuple-element.101), channel_id=1, source_target_pairs={{0,1},{1,0},{2,3},{3,2},{4,5},{5,4},{6,7},{7,6},{8,9},{9,8},{10,11... | collective-permute-start | bytes 98312 | tf_op jit(solution)/shard_map/ppermute | solution.py:317
  116.7 7.0 %collective-permute-start.23 = (f32[64,128]{1,0:T(8,128)S(1)}, f32[64,128]{1,0:T(8,128)S(1)}, u32[]{:S(2)}, u32[]{:S(2)}) collective-permute-start(f32[64,128]{1,0:T(8,128)S(1)} %get-tuple-element.102), channel_id=1, source_target_pairs={{1,2},{2,1},{3,4},{4,3},{5,6},{6,5},{7,8},{8,7},{9,10},{10,9},{11,... | collective-permute-start | bytes 98312 | tf_op jit(solution)/shard_map/ppermute | solution.py:317
  125.0 4.5 %collective-permute-start.24 = (f32[64,128]{1,0:T(8,128)S(1)}, f32[64,128]{1,0:T(8,128)S(1)}, u32[]{:S(2)}, u32[]{:S(2)}) collective-permute-start(f32[64,128]{1,0:T(8,128)S(1)} %get-tuple-element.104), channel_id=1, source_target_pairs={{0,1},{1,0},{2,3},{3,2},{4,5},{5,4},{6,7},{7,6},{8,9},{9,8},{10,11... | collective-permute-start | bytes 98312 | tf_op jit(solution)/shard_map/ppermute | solution.py:317
  125.1 7.0 %collective-permute-start.25 = (f32[64,128]{1,0:T(8,128)S(1)}, f32[64,128]{1,0:T(8,128)S(1)}, u32[]{:S(2)}, u32[]{:S(2)}) collective-permute-start(f32[64,128]{1,0:T(8,128)S(1)} %get-tuple-element.105), channel_id=1, source_target_pairs={{1,2},{2,1},{3,4},{4,3},{5,6},{6,5},{7,8},{8,7},{9,10},{10,9},{11,... | collective-permute-start | bytes 98312 | tf_op jit(solution)/shard_map/ppermute | solution.py:317
  133.1 4.5 %collective-permute-start.26 = (f32[64,128]{1,0:T(8,128)S(1)}, f32[64,128]{1,0:T(8,128)S(1)}, u32[]{:S(2)}, u32[]{:S(2)}) collective-permute-start(f32[64,128]{1,0:T(8,128)S(1)} %get-tuple-element.107), channel_id=1, source_target_pairs={{0,1},{1,0},{2,3},{3,2},{4,5},{5,4},{6,7},{7,6},{8,9},{9,8},{10,11... | collective-permute-start | bytes 98312 | tf_op jit(solution)/shard_map/ppermute | solution.py:317
  133.2 7.0 %collective-permute-start.27 = (f32[64,128]{1,0:T(8,128)S(1)}, f32[64,128]{1,0:T(8,128)S(1)}, u32[]{:S(2)}, u32[]{:S(2)}) collective-permute-start(f32[64,128]{1,0:T(8,128)S(1)} %get-tuple-element.108), channel_id=1, source_target_pairs={{1,2},{2,1},{3,4},{4,3},{5,6},{6,5},{7,8},{8,7},{9,10},{10,9},{11,... | collective-permute-start | bytes 98312 | tf_op jit(solution)/shard_map/ppermute | solution.py:317
  141.3 4.5 %collective-permute-start.28 = (f32[64,128]{1,0:T(8,128)S(1)}, f32[64,128]{1,0:T(8,128)S(1)}, u32[]{:S(2)}, u32[]{:S(2)}) collective-permute-start(f32[64,128]{1,0:T(8,128)S(1)} %get-tuple-element.110), channel_id=1, source_target_pairs={{0,1},{1,0},{2,3},{3,2},{4,5},{5,4},{6,7},{7,6},{8,9},{9,8},{10,11... | collective-permute-start | bytes 98312 | tf_op jit(solution)/shard_map/ppermute | solution.py:317
  141.3 7.0 %collective-permute-start.29 = (f32[64,128]{1,0:T(8,128)S(1)}, f32[64,128]{1,0:T(8,128)S(1)}, u32[]{:S(2)}, u32[]{:S(2)}) collective-permute-start(f32[64,128]{1,0:T(8,128)S(1)} %get-tuple-element.111), channel_id=1, source_target_pairs={{1,2},{2,1},{3,4},{4,3},{5,6},{6,5},{7,8},{8,7},{9,10},{10,9},{11,... | collective-permute-start | bytes 98312 | tf_op jit(solution)/shard_map/ppermute | solution.py:317
  150.2 4.6 %collective-permute-start.30 = (f32[64,128]{1,0:T(8,128)S(1)}, f32[64,128]{1,0:T(8,128)S(1)}, u32[]{:S(2)}, u32[]{:S(2)}) collective-permute-start(f32[64,128]{1,0:T(8,128)S(1)} %get-tuple-element.113), channel_id=1, source_target_pairs={{0,1},{1,0},{2,3},{3,2},{4,5},{5,4},{6,7},{7,6},{8,9},{9,8},{10,11... | collective-permute-start | bytes 98312 | tf_op jit(solution)/shard_map/ppermute | solution.py:317
  150.3 7.0 %collective-permute-start.31 = (f32[64,128]{1,0:T(8,128)S(1)}, f32[64,128]{1,0:T(8,128)S(1)}, u32[]{:S(2)}, u32[]{:S(2)}) collective-permute-start(f32[64,128]{1,0:T(8,128)S(1)} %get-tuple-element.114), channel_id=1, source_target_pairs={{1,2},{2,1},{3,4},{4,3},{5,6},{6,5},{7,8},{8,7},{9,10},{10,9},{11,... | collective-permute-start | bytes 98312 | tf_op jit(solution)/shard_map/ppermute | solution.py:317
  159.4 4.5 %collective-permute-start.32 = (f32[64,128]{1,0:T(8,128)S(1)}, f32[64,128]{1,0:T(8,128)S(1)}, u32[]{:S(2)}, u32[]{:S(2)}) collective-permute-start(f32[64,128]{1,0:T(8,128)S(1)} %get-tuple-element.116), channel_id=1, source_target_pairs={{0,1},{1,0},{2,3},{3,2},{4,5},{5,4},{6,7},{7,6},{8,9},{9,8},{10,11... | collective-permute-start | bytes 98312 | tf_op jit(solution)/shard_map/ppermute | solution.py:317
  159.5 7.0 %collective-permute-start.33 = (f32[64,128]{1,0:T(8,128)S(1)}, f32[64,128]{1,0:T(8,128)S(1)}, u32[]{:S(2)}, u32[]{:S(2)}) collective-permute-start(f32[64,128]{1,0:T(8,128)S(1)} %get-tuple-element.117), channel_id=1, source_target_pairs={{1,2},{2,1},{3,4},{4,3},{5,6},{6,5},{7,8},{8,7},{9,10},{10,9},{11,... | collective-permute-start | bytes 98312 | tf_op jit(solution)/shard_map/ppermute | solution.py:317
  168.6 4.5 %collective-permute-start.34 = (f32[64,128]{1,0:T(8,128)S(1)}, f32[64,128]{1,0:T(8,128)S(1)}, u32[]{:S(2)}, u32[]{:S(2)}) collective-permute-start(f32[64,128]{1,0:T(8,128)S(1)} %get-tuple-element.119), channel_id=1, source_target_pairs={{0,1},{1,0},{2,3},{3,2},{4,5},{5,4},{6,7},{7,6},{8,9},{9,8},{10,11... | collective-permute-start | bytes 98312 | tf_op jit(solution)/shard_map/ppermute | solution.py:317
  168.7 7.0 %collective-permute-start.35 = (f32[64,128]{1,0:T(8,128)S(1)}, f32[64,128]{1,0:T(8,128)S(1)}, u32[]{:S(2)}, u32[]{:S(2)}) collective-permute-start(f32[64,128]{1,0:T(8,128)S(1)} %get-tuple-element.120), channel_id=1, source_target_pairs={{1,2},{2,1},{3,4},{4,3},{5,6},{6,5},{7,8},{8,7},{9,10},{10,9},{11,... | collective-permute-start | bytes 98312 | tf_op jit(solution)/shard_map/ppermute | solution.py:317
  (17 other events, 473.5 us)

commit v2 on v1

--- a/solution.py
+++ b/solution.py
@@ -8,6 +8,7 @@
 from jax.sharding import PartitionSpec as P
 
 HALO = 2
+VMEM_BYTES = 24 * 2**20
 COARSE_SWEEPS = 2
 COARSEST_SWEEPS = 8
 OMEGA = 0.7
@@ -53,10 +54,16 @@
     return jnp.sum(jnp.where(rows == lanes, block, 0.0), axis=0, keepdims=True)
 
 
+def column(columns, blocks, tile, link):
+    if columns.shape == blocks.shape[:2]:
+        return columns[tile, link]
+    return columns[link, tile]
+
+
 def tile_diagonal(columns, blocks, tile):
     total = None
     for link in range(blocks.shape[1]):
-        own = (columns[tile, link] == tile + HALO).astype(F32)
+        own = (column(columns, blocks, tile, link) == tile + HALO).astype(F32)
         term = diagonal_row(blocks[tile, link]) * own
         total = term if total is None else total + term
     return total
@@ -85,32 +92,68 @@
         extended[(1 - core) * (count + HALO) + tile] = stack(pair_halo[rows])
 
 
-def tile_apply(columns, blocks, extended, tile):
-    links, width = blocks.shape[1], blocks.shape[-1]
-    left = jnp.concatenate([extended[columns[tile, k]] for k in range(links)], axis=1)
-    parts = [split(blocks[tile, k]) for k in range(links)]
-    weights = jnp.concatenate(
+def weights_of(blocks, tile):
+    parts = [split(blocks[tile, k]) for k in range(blocks.shape[1])]
+    return jnp.concatenate(
         [jnp.concatenate([p[0] for p in parts], axis=1), jnp.concatenate([p[1] for p in parts], axis=1)], axis=0
     )
-    return product(left, weights, NT, width)
+
+
+def tile_apply(columns, blocks, extended, tile, shift=0):
+    picked = [extended[column(columns, blocks, tile, k) + shift] for k in range(blocks.shape[1])]
+    return product(jnp.concatenate(picked, axis=1), weights_of(blocks, tile), NT, blocks.shape[-1])
 
 
 def put_edges(vector, count, panels, pair_edge, chip_edge):
     core = lax.axis_index("pair")
     last = (count - HALO) * panels
     size = HALO * panels
-    pair_edge[...] = vector[pl.ds(pl.multiple_of((1 - core) * last, panels), size)]
-    chip_edge[...] = vector[pl.ds(pl.multiple_of(core * last, panels), size)]
-
-
-def first_kernel(columns, source, blocks, diagonal, vector, pair_edge, chip_edge):
+    pair_edge[pl.ds(0, size)] = vector[pl.ds(pl.multiple_of((1 - core) * last, panels), size)]
+    chip_edge[pl.ds(0, size)] = vector[pl.ds(pl.multiple_of(core * last, panels), size)]
+
+
+def put_wide_edges(vector, count, panels, wide, pair_edge, chip_edge):
+    core = lax.axis_index("pair")
+    reach = wide - HALO
+    for edge, turn in ((pair_edge, 1 - core), (chip_edge, core)):
+        near = pl.multiple_of(turn * (count - reach) * panels, panels)
+        far = pl.multiple_of(jnp.where(turn == 1, count - wide, reach) * panels, panels)
+        edge[pl.ds(0, reach * panels)] = vector[pl.ds(near, reach * panels)]
+        edge[pl.ds(reach * panels, HALO * panels)] = vector[pl.ds(far, HALO * panels)]
+
+
+def integer_row(values, width):
+    lanes = lax.broadcasted_iota(jnp.int32, (8, width), 1)
+    row = jnp.zeros((8, width), F32)
+    for k, value in enumerate(values):
+        row = jnp.where(lanes == k, value.astype(F32), row)
+    return row
+
+
+def columns_row(columns, blocks, first, tiles, width):
+    links = blocks.shape[1]
+    return integer_row([column(columns, blocks, first + t, k) for t in range(tiles) for k in range(links)], width)
+
+
+def first_kernel(reach, columns, source, blocks, diagonal, vector, pair_edge, chip_edge):
     panels = source.shape[0]
     count, width = blocks.shape[0], blocks.shape[-1]
+    core = lax.axis_index("pair")
+    start = HALO * panels
+    for edge, turn in ((pair_edge, 1 - core), (chip_edge, core)):
+        edge[pl.ds(start, 8)] = columns_row(columns, blocks, turn * (count - reach), reach, width)
+        for tile in range(reach):
+            ahead, behind = get_tile(source, tile, panels, width), get_tile(source, count - reach + tile, panels, width)
+            edge[pl.ds(start + 8 + tile * panels, panels)] = jnp.where(turn == 1, behind, ahead)
     for tile in range(count):
         row = tile_diagonal(columns, blocks, tile)
         diagonal[pl.ds(tile, 1)] = row
         vector[pl.ds(tile * panels, panels)] = OMEGA * get_tile(source, tile, panels, width) / row
     put_edges(vector, count, panels, pair_edge, chip_edge)
+
+
+def copy_kernel(*_):
+    pass
 
 
 def sweep_kernel(panels, edges, columns, vector, pair_halo, chip_halo, source, diagonal, blocks, result, *rest):
@@ -126,27 +169,45 @@
         put_edges(result, count, panels, rest[0], rest[1])
 
 
-def residual_kernel(
-    panels, columns, vector, pair_halo, chip_halo, source, blocks, aggregate, next_columns, next_blocks,
-    next_source, next_diagonal, next_vector, pair_edge, chip_edge, extended,
-):
-    count, width = blocks.shape[0], blocks.shape[-1]
-    next_count = next_blocks.shape[0]
-    factor = count // next_count
-    fill_extended(extended, vector, pair_halo, chip_halo, count, panels)
+def restrict(pieces, aggregate, next_columns, next_blocks, panels, next_source, next_diagonal, next_vector):
+    width, next_count = next_blocks.shape[-1], next_blocks.shape[0]
+    factor = len(pieces) // next_count
     for group in range(next_count):
-        pieces = []
-        for tile in range(group * factor, (group + 1) * factor):
-            rest = get_tile(source, tile, panels, width) - tile_apply(columns, blocks, extended, tile)
-            pieces.append(stack(rest))
         one_hot = one_hot_rows(aggregate[:, group * factor * width:(group + 1) * factor * width], width)
-        gathered = picked_sum(jnp.concatenate(pieces, axis=1), one_hot, NT)
+        stacked = jnp.concatenate([stack(p) for p in pieces[group * factor:(group + 1) * factor]], axis=1)
+        gathered = picked_sum(stacked, one_hot, NT)
         row = tile_diagonal(next_columns, next_blocks, group)
         rows = pl.ds(group * panels, panels)
         next_source[rows] = gathered
         next_diagonal[pl.ds(group, 1)] = row
         next_vector[rows] = OMEGA * gathered / row
-    put_edges(next_vector, next_count, panels, pair_edge, chip_edge)
+
+
+def residual_kernel(
+    panels, columns, vector, pair_halo, chip_halo, source, blocks, aggregate, next_columns, next_blocks,
+    next_source, next_diagonal, next_vector, packed, extended,
+):
+    count, width = blocks.shape[0], blocks.shape[-1]
+    fill_extended(extended, vector, pair_halo, chip_halo, count, panels)
+    pieces = [
+        get_tile(source, tile, panels, width) - tile_apply(columns, blocks, extended, tile) for tile in range(count)
+    ]
+    restrict(pieces, aggregate, next_columns, next_blocks, panels, next_source, next_diagonal, next_vector)
+    put_packed(packed, next_vector, panels, next_source, next_columns, next_blocks)
+
+
+def put_packed(packed, vector, panels, source=None, columns=None, blocks=None):
+    size, width = vector.shape
+    packed[pl.ds(0, size)] = vector[...]
+    at = size
+    if source is not None:
+        packed[pl.ds(at, size)] = source[...]
+        packed[pl.ds(at + size, 8)] = columns_row(columns, blocks, 0, blocks.shape[0], width)
+        at += size + 8
+    if packed.shape[0] > at:
+        edge = HALO * panels
+        first = pl.multiple_of((1 - lax.axis_index("pair")) * (size - edge), panels)
+        packed[pl.ds(at, edge)] = vector[pl.ds(first, edge)]
 
 
 def one_hot_rows(indices, width):
@@ -160,24 +221,27 @@
     return (jnp.where(rows < half, rows, rows - half) == indices).astype(F32).astype(BF16)
 
 
+def prolong(tile, value, aggregate, upper, panels, width, own_tiles, result):
+    factor = upper.shape[0] // panels // own_tiles
+    one_hot = one_hot_rows(aggregate[:, tile * factor * width:(tile + 1) * factor * width], width)
+    lifted = picked_sum(stack(value), one_hot, NN)
+    for k in range(factor):
+        rows = pl.ds((tile * factor + k) * panels, panels)
+        result[rows] = upper[rows] + lifted[:, k * width:(k + 1) * width]
+
+
 def prolong_kernel(
     panels, columns, vector, pair_halo, chip_halo, source, diagonal, blocks, aggregate, upper,
-    next_vector, pair_edge, chip_edge, extended,
+    next_vector, packed, extended,
 ):
     count, width = blocks.shape[0], blocks.shape[-1]
-    upper_count = upper.shape[0] // panels
-    factor = upper_count // count
     fill_extended(extended, vector, pair_halo, chip_halo, count, panels)
     for tile in range(count):
         product_tile = tile_apply(columns, blocks, extended, tile)
         old = vector[pl.ds(tile * panels, panels)]
         new = old + OMEGA * (get_tile(source, tile, panels, width) - product_tile) / diagonal[pl.ds(tile, 1)]
-        one_hot = one_hot_rows(aggregate[:, tile * factor * width:(tile + 1) * factor * width], width)
-        lifted = picked_sum(stack(new), one_hot, NN)
-        for k in range(factor):
-            rows = pl.ds((tile * factor + k) * panels, panels)
-            next_vector[rows] = upper[rows] + lifted[:, k * width:(k + 1) * width]
-    put_edges(next_vector, upper_count, panels, pair_edge, chip_edge)
+        prolong(tile, new, aggregate, upper, panels, width, count, next_vector)
+    put_packed(packed, next_vector, panels)
 
 
 def chain_weights(operators, depths):
@@ -226,18 +290,10 @@
             piece = picked_sum(stack(rest), one_hot_twice(maps[0, pl.ds(level, 1)], width), NT)
 
 
-def lowest_kernel(
-    panels, columns, vector, pair_halo, chip_halo, source, blocks, aggregate, images,
-    own_piece, outgoing, extended,
-):
-    count, width = blocks.shape[0], blocks.shape[-1]
+def send_shares(pieces, aggregate, images, panels, own_piece, outgoing):
+    width = own_piece.shape[1]
     half = width // 2
     here = position()
-    fill_extended(extended, vector, pair_halo, chip_halo, count, panels)
-    pieces = []
-    for tile in range(count):
-        rest = get_tile(source, tile, panels, width) - tile_apply(columns, blocks, extended, tile)
-        pieces.append(stack(rest))
     one_hot = one_hot_twice(aggregate[...], width)
     gathered = picked_sum(jnp.concatenate(pieces, axis=1), one_hot, NT)
     own_piece[...] = gathered
@@ -252,6 +308,19 @@
         if level == 0:
             outgoing[pl.ds(here, 1)] = packed[None]
         outgoing[pl.ds(start, 2**level)] = jnp.broadcast_to(packed[None], (2**level,) + packed.shape)
+
+
+def lowest_kernel(
+    panels, columns, vector, pair_halo, chip_halo, source, blocks, aggregate, images,
+    own_piece, outgoing, extended,
+):
+    count, width = blocks.shape[0], blocks.shape[-1]
+    fill_extended(extended, vector, pair_halo, chip_halo, count, panels)
+    pieces = []
+    for tile in range(count):
+        rest = get_tile(source, tile, panels, width) - tile_apply(columns, blocks, extended, tile)
+        pieces.append(stack(rest))
+    send_shares(pieces, aggregate, images, panels, own_piece, outgoing)
 
 
 def chain_kernel(panels, own_piece, incoming, operators, maps, aggregate, upper, result):
@@ -290,31 +359,200 @@
         result[rows] = upper[rows] + lifted[:, tile * width:(tile + 1) * width]
 
 
-def call(kernel, shapes, operands, scalars=(), scratch=(), name=None):
+def outer_devices(layout, own_tiles, wide):
+    core = lax.axis_index("pair")
+    here, devices = position(), lax.axis_size(AXES)
+    chunks = []
+    for side_name, entries in layout.items():
+        is_left = (core == 0) if side_name == "out" else (core == 1)
+        before = 0
+        for entry in entries:
+            size, distance = entry["tiles"], entry["distance"]
+            start = jnp.where(is_left, wide - before - size, wide + own_tiles + before)
+            base = jnp.where(is_left, wide - distance * own_tiles, wide + distance * own_tiles) - HALO
+            owner = jnp.where(is_left, here - distance, here + distance)
+            chunks.append(dict(
+                entry, before=before, start=start, base=base, is_left=is_left,
+                valid=(owner >= 0) & (owner < devices),
+            ))
+            before += size
+    return chunks
+
+
+def chunk_rows(refs, chunk, key, tile, panels):
+    name, offset = chunk[key]
+    if offset == "core":
+        offset = lax.axis_index("pair") * (refs[name].shape[0] - HALO * panels)
+        return refs[name][pl.ds(pl.multiple_of(offset + tile * panels, panels), panels)]
+    if isinstance(tile, int):
+        return refs[name][pl.ds(offset + tile * panels, panels)]
+    return refs[name][pl.ds(pl.multiple_of(offset + tile * panels, 8), panels)]
+
+
+def wide_apply(blocks, numbers, shift, base, extended, tile):
+    links = blocks.shape[1]
+    picked = []
+    for link in range(links):
+        place = base + numbers[0, shift + tile * links + link].astype(jnp.int32)
+        picked.append(extended[jnp.clip(place, 0, extended.shape[0] - 1)])
+    return product(jnp.concatenate(picked, axis=1), weights_of(blocks, tile), NT, blocks.shape[-1])
+
+
+def chunk_diagonal(blocks, numbers, shift, chunk, tile):
+    total = None
+    for link in range(blocks.shape[1]):
+        place = chunk["base"] + numbers[0, shift + tile * blocks.shape[1] + link].astype(jnp.int32)
+        term = diagonal_row(blocks[tile, link]) * (place == chunk["start"] + tile).astype(F32)
+        total = term if total is None else total + term
+    return total
+
+
+def wide_kernel(names, layout, panels, wide, integers_at, finish, outputs, *args):
+    refs = dict(zip(names, args))
+    outs = args[len(names):len(names) + outputs]
+    extended, values = args[len(names) + outputs:][:2], args[len(names) + outputs:][2:4]
+    diagonals, near, numbers, semaphores = args[len(names) + outputs + 4:]
+    pieces = {0: [n for n in names if n.startswith("blocks_pair")], 1: [n for n in names if n.startswith("blocks_chip")]}
+    blocks, own, columns = refs["blocks"], refs["vector"], refs["columns"]
+    own_tiles, width = blocks.shape[0], blocks.shape[-1]
+    reach = near.shape[1]
+    core = lax.axis_index("pair")
+    arrivals = [
+        pltpu.make_async_copy(refs["integers_pair"].at[pl.ds(integers_at, 8)], numbers.at[0], semaphores.at[0]),
+        pltpu.make_async_copy(refs["integers_chip"].at[pl.ds(integers_at, 8)], numbers.at[1], semaphores.at[1]),
+    ]
+    for which in (0, 1):
+        at = 0
+        for name in pieces[which]:
+            size = refs[name].shape[0]
+            arrivals.append(
+                pltpu.make_async_copy(refs[name], near.at[which, pl.ds(at, size)], semaphores.at[len(arrivals)])
+            )
+            at += size
+    for copy in arrivals:
+        copy.start()
+    chunks = outer_devices(layout, own_tiles, wide)
+    for tile in range(own_tiles):
+        extended[0][wide + tile] = stack(own[pl.ds(tile * panels, panels)])
+    for chunk in chunks:
+        for tile in range(chunk["tiles"]):
+            old = jnp.where(chunk["valid"], chunk_rows(refs, chunk, "vector", tile, panels), 0.0)
+            extended[0][chunk["start"] + tile] = stack(old)
+    stages = wide // HALO
+    fresh = []
+    for stage in range(1, stages + 1):
+        before, after = extended[(stage - 1) % 2], extended[stage % 2]
+        past, future = values[(stage - 1) % 2], values[stage % 2]
+        for tile in range(own_tiles):
+            rows = pl.ds((wide + tile) * panels, panels)
+            rest = get_tile(refs["source"], tile, panels, width) - tile_apply(
+                columns, blocks, before, tile, wide - HALO
+            )
+            if stage == stages and finish == "down":
+                fresh.append(rest)
+                continue
+            old = own[pl.ds(tile * panels, panels)] if stage == 1 else past[rows]
+            new = old + OMEGA * rest / refs["diagonal"][pl.ds(tile, 1)]
+            if stage < stages:
+                future[rows] = new
+                after[wide + tile] = stack(new)
+            if stage == stages - 1 and finish == "down":
+                outs[0][pl.ds(tile * panels, panels)] = new
+            if stage == stages:
+                if finish == "up":
+                    prolong(tile, new, refs["aggregate"], refs["upper"], panels, width, own_tiles, outs[0])
+                else:
+                    put_tile(outs[0], tile, new, panels, width)
+        if stage == 1:
+            for copy in arrivals:
+                copy.wait()
+        for chunk in chunks:
+            count = min(max(wide - HALO * stage - chunk["before"], 0), chunk["tiles"])
+            first = jnp.where(chunk["is_left"], chunk["tiles"] - count, 0)
+            for k in range(count):
+                tile = k if count == chunk["tiles"] else first + k
+                place = chunk["start"] + tile
+                rows = pl.ds(pl.multiple_of(place * panels, panels), panels)
+                which, shift = chunk["columns"]
+                rest = chunk_rows(refs, chunk, "source", tile, panels) - wide_apply(
+                    near.at[which], numbers.at[which], shift, chunk["base"], before, tile
+                )
+                if stage == 1:
+                    row = chunk_diagonal(near.at[which], numbers.at[which], shift, chunk, tile)
+                    if stages > 2:
+                        diagonals[which * reach + tile] = jnp.broadcast_to(row, (8, width))
+                    old = chunk_rows(refs, chunk, "vector", tile, panels)
+                else:
+                    row = diagonals[which * reach + tile][:1]
+                    old = past[rows]
+                new = jnp.where(chunk["valid"], old + OMEGA * rest / row, 0.0)
+                if stage < stages - 1:
+                    future[rows] = new
+                after[place] = stack(new)
+    if finish == "down":
+        restrict(fresh, refs["aggregate"], refs["next_columns"], refs["next_blocks"], panels, *outs[1:4])
+    if finish == "up":
+        put_wide_edges(outs[0], outs[0].shape[0] // panels, panels, wide, outs[1], outs[2])
+
+
+def call(kernel, shapes, operands, scalars=(), remote=(), scratch=(), name=None, carry=(), tokens=(), limit=VMEM_BYTES):
     vmem = pl.BlockSpec(memory_space=pltpu.VMEM)
     smem = pl.BlockSpec(memory_space=pltpu.SMEM)
-    specs = [smem if k in scalars else vmem for k in range(len(operands))]
-    outs = pl.pallas_call(
-        kernel,
-        out_shape=[jax.ShapeDtypeStruct(s, t) for s, t in shapes],
-        in_specs=specs,
-        out_specs=[vmem] * len(shapes),
-        scratch_shapes=list(scratch),
-        compiler_params=pltpu.CompilerParams(vmem_limit_bytes=32 * 2**20),
+    free = pl.BlockSpec(memory_space=pl.ANY)
+    specs = [smem if k in scalars else free if k in remote else vmem for k in range(len(operands))]
+    taken, given, count = len(operands), len(shapes), len(carry)
+
+    def body(*refs):
+        ins, origins, refs = refs[:taken], refs[taken:taken + count], refs[taken + count + len(tokens):]
+        outs, copied, rest = refs[:given], refs[given:given + count], refs[given + count:]
+        copies = [
+            pltpu.make_async_copy(origin.at[pl.ds(first, size)], target, rest[-1].at[k])
+            for k, (origin, (_, first, size), target) in enumerate(zip(origins, carry_firsts(), copied))
+        ]
+        for copy in copies:
+            copy.start()
+        kernel(*ins, *outs, *(rest[:-1] if count else rest))
+        for copy in copies:
+            copy.wait()
+
+    def carry_firsts():
+        return [(array, first() if callable(first) else first, size) for array, first, size in carry]
+
+    extra = [jax.ShapeDtypeStruct((size,) + array.shape[1:], array.dtype) for array, _, size in carry]
+    return pl.pallas_call(
+        body,
+        out_shape=[jax.ShapeDtypeStruct(s, t) for s, t in shapes] + extra,
+        in_specs=specs + [free] * (count + len(tokens)),
+        out_specs=[vmem] * given + [free] * count,
+        scratch_shapes=list(scratch) + ([pltpu.SemaphoreType.DMA((count,))] if count else []),
+        compiler_params=pltpu.CompilerParams(vmem_limit_bytes=limit),
         name=name,
-    )(*operands)
-    return outs
+    )(*operands, *[array for array, _, _ in carry], *tokens)
 
 
 def swaps(pairs):
     return [p for a, b in pairs for p in ((a, b), (b, a))]
 
 
+def inner_swap(value):
+    count = lax.axis_size(AXES)
+    return lax.ppermute(value, AXES, swaps([(2 * k, 2 * k + 1) for k in range(count // 2)]))
+
+
+def outer_swap(value):
+    count = lax.axis_size(AXES)
+    return lax.ppermute(value, AXES, swaps([(2 * k + 1, 2 * k + 2) for k in range(count // 2 - 1)]))
+
+
 def exchange(pair_edge, chip_edge):
-    count = lax.axis_size(AXES)
-    inner = swaps([(2 * k, 2 * k + 1) for k in range(count // 2)])
-    outer = swaps([(2 * k + 1, 2 * k + 2) for k in range(count // 2 - 1)])
-    return lax.ppermute(pair_edge, AXES, inner), lax.ppermute(chip_edge, AXES, outer)
+    return inner_swap(pair_edge), outer_swap(chip_edge)
+
+
+def side(tiles, distance, vector, source=None, columns=None):
+    entry = dict(tiles=tiles, distance=distance, vector=vector)
+    if source is not None:
+        entry.update(source=source, columns=columns)
+    return entry
 
 
 def on_device(
@@ -324,78 +562,186 @@
     panels, width = pulse_rhs.shape[0], blocks_fine.shape[-1]
     devices = lax.axis_size(AXES)
     blocks = (blocks_fine, blocks_mid, blocks_low)
-    columns = (columns_fine, columns_mid, columns_low)
+    columns = (columns_fine.T, columns_mid, columns_low)
     aggregates = tuple(a.reshape(1, -1) for a in (aggregate_fine, aggregate_mid, aggregate_low))
     counts = tuple(b.shape[0] for b in blocks)
     depths = coarse_ops.shape[1]
+    wide = (6, 6)
+    reach = tuple(w - HALO for w in wide)
+    edge_rows = HALO * panels
+
+    def rows(tiles, extra=0):
+        return ((tiles * panels + extra, width), F32)
 
     def vec(level):
-        return ((counts[level] * panels, width), F32)
+        return rows(counts[level])
 
     def diag(level):
         return ((counts[level], width), F32)
 
-    edge = ((HALO * panels, width), F32)
-
     def ext(level):
         return [pltpu.VMEM((counts[level] + 2 * HALO, 2 * panels, width), BF16)]
 
-    def sweep(level, vector, halos, last=False):
-        shapes = [(pulse_rhs.shape, F32)] if last else [vec(level), edge, edge]
+    def wide_call(level, finish, layout, shapes, operands, integers, near_pair, near_chip, step):
+        operands = dict(
+            operands, source=sources[level], diagonal=diagonals[level], blocks=blocks[level], columns=columns[level],
+            integers_pair=integers[0], integers_chip=integers[1], blocks_pair=near_pair,
+            **{f"blocks_chip{k}": piece for k, piece in enumerate(near_chip)},
+        )
+        names = tuple(operands)
+        count = counts[level] + 2 * wide[level]
+        return step(
+            f"wide_{finish}{level}", functools.partial(wide_kernel, names, layout, panels, wide[level], integers[2], finish, len(shapes)),
+            shapes, tuple(operands[k] for k in names),
+            scalars=tuple(k for k, name in enumerate(names) if "columns" in name),
+            remote=tuple(k for k, name in enumerate(names) if name.startswith(("integers", "blocks_"))),
+            scratch=[pltpu.VMEM((count, 2 * panels, width), BF16)] * 2
+            + [pltpu.VMEM((count * panels, width), F32)] * 2
+            + [
+                pltpu.VMEM((2 * reach[level], 8, width), F32),
+                pltpu.VMEM((2, reach[level]) + blocks_fine.shape[1:], F32),
+                pltpu.SMEM((2, 8, width), F32),
+                pltpu.SemaphoreType.DMA((3 + len(near_chip),)),
+            ],
+        )
+
+    def facing(towards_pair, tile):
+        def first():
+            core = lax.axis_index("pair")
+            return (1 - core if towards_pair else core) * (counts[0] - reach[0]) + tile
+        return first
+
+    pieces_of = {
+        **{f"mid{k}": (blocks_mid, k, 1) for k in range(counts[1])},
+        **{f"fine{k}": (blocks_fine, facing(False, k), 1) for k in range(reach[0])},
+    }
+    arrived = {}
+
+    def step(name, kernel, shapes, operands, tokens=(), **more):
+        leaving = LEAVE.get(name, ())
         outs = call(
-            functools.partial(sweep_kernel, panels, not last),
-            shapes,
-            (columns[level], vector, *halos, sources[level], diagonals[level], blocks[level]),
-            scalars=(0,), scratch=ext(level), name=f"sweep{level}",
+            kernel, shapes, operands, name=name, carry=[pieces_of[p] for p in leaving],
+            tokens=[arrived[p] for p in ARRIVE.get(name, ())] + list(tokens), **more,
         )
-        return outs[0] if last else (outs[0], exchange(outs[1], outs[2]))
-
+        pieces = dict(zip(leaving, outs[len(shapes):]))
+        return outs[:len(shapes)], lambda: arrived.update({p: outer_swap(v) for p, v in pieces.items()})
+
+    mid_pair = inner_swap(blocks_mid)
     images = call(maps_kernel, [((width // 2, 2 * depths * width), BF16)], (coarse_ops, coarse_maps), name="maps")[0]
-    sources, diagonals, kept = [pulse_rhs], [], []
-    diagonal, vector, pair_edge, chip_edge = call(
-        first_kernel, [diag(0), vec(0), edge, edge], (columns[0], pulse_rhs, blocks[0]), scalars=(0,), name="first"
-    )
-    diagonals.append(diagonal)
-    halos = exchange(pair_edge, chip_edge)
-    for level in range(3):
-        vector, halos = sweep(level, vector, halos)
-        vector, halos = sweep(level, vector, halos)
-        kept.append(vector)
-        if level < 2:
-            source, diagonal, vector, pair_edge, chip_edge = call(
-                functools.partial(residual_kernel, panels),
-                [vec(level + 1), diag(level + 1), vec(level + 1), edge, edge],
-                (columns[level], vector, *halos, sources[level], blocks[level], aggregates[level],
-                 columns[level + 1], blocks[level + 1]),
-                scalars=(0, 7), scratch=ext(level), name=f"residual{level}",
-            )
-            sources.append(source)
-            diagonals.append(diagonal)
-            halos = exchange(pair_edge, chip_edge)
-    own_piece, outgoing = call(
-        functools.partial(lowest_kernel, panels),
-        [((panels, width), F32), ((devices, panels // 2, width), F32)],
-        (columns[2], vector, *halos, sources[2], blocks[2], aggregates[2], images),
-        scalars=(0,), scratch=ext(2), name="lowest",
-    )
-    incoming = lax.all_to_all(outgoing, AXES, 0, 0)
-    vector = call(
-        functools.partial(chain_kernel, panels), [vec(2)],
-        (own_piece, incoming, coarse_ops, coarse_maps, aggregates[2], kept[2]), name="chain",
-    )[0]
-    halos = exchange(vector, vector)
-    for level in (2, 1, 0):
-        vector, halos = sweep(level, vector, halos)
-        vector, halos = sweep(level, vector, halos)
-        if level == 0:
-            return sweep(0, vector, halos, last=True)
-        vector, pair_edge, chip_edge = call(
-            functools.partial(prolong_kernel, panels), [vec(level - 1), edge, edge],
-            (columns[level], vector, *halos, sources[level], diagonals[level], blocks[level],
-             aggregates[level - 1], kept[level - 1]),
-            scalars=(0,), scratch=ext(level), name=f"prolong{level}",
+
+    first_edge = rows(HALO + reach[0], 8)
+    (diagonal, vector, pair_edge, chip_edge), leave = step(
+        "first", functools.partial(first_kernel, reach[0]), [diag(0), vec(0), first_edge, first_edge],
+        (columns[0], pulse_rhs, blocks_fine), scalars=(0,),
+    )
+    sources, diagonals = [pulse_rhs], [diagonal]
+    halos = first_halos = exchange(pair_edge, chip_edge)
+    leave()
+    for k in range(2):
+        (vector, pair_edge, chip_edge), leave = step(
+            f"sweep0{k}", functools.partial(sweep_kernel, panels, True), [vec(0), rows(HALO), rows(HALO)],
+            (columns[0], vector, *halos, pulse_rhs, diagonal, blocks_fine), scalars=(0,), scratch=ext(0),
         )
         halos = exchange(pair_edge, chip_edge)
+        leave()
+    kept = [vector]
+    fine_pair = call(copy_kernel, [], (), name="near", carry=[(blocks_fine, facing(True, 0), reach[0])])[0]
+    fine_pair = inner_swap(fine_pair)
+    (source, diagonal, vector, packed), leave = step(
+        "residual0", functools.partial(residual_kernel, panels),
+        [vec(1), diag(1), vec(1), rows(2 * counts[1] + HALO, 8)],
+        (columns[0], vector, *halos, pulse_rhs, blocks_fine, aggregates[0], columns_mid, blocks_mid),
+        scalars=(0, 7), scratch=ext(0),
+    )
+    sources.append(source)
+    diagonals.append(diagonal)
+
+    size = counts[1] * panels
+    pair = inner_swap(packed)
+    chip = outer_swap(jnp.concatenate([packed[:2 * size + 8], pair[2 * size + 8:]]))
+    leave()
+    far = inner_swap(chip[:size])
+    first_mid = (pair, chip, 2 * size)
+
+    def mid_layout(second):
+        return {
+            "out": [side(counts[1], 1, ("chip", 0), ("chip_source", size), (1, 0)), side(HALO, 1, ("chip", second))],
+            "in": [side(counts[1], 1, ("pair", 0), ("pair_source", size), (0, 0)), side(HALO, 1, ("far", "core"))],
+        }
+
+    mid_chip = [arrived[f"mid{k}"] for k in range(counts[1])]
+    (vector, source, diagonal, next_vector), leave = wide_call(
+        1, "down", mid_layout(2 * size + 8), [vec(1), vec(2), diag(2), vec(2)],
+        dict(vector=vector, pair=pair, chip=chip, far=far, pair_source=pair, chip_source=chip,
+             aggregate=aggregates[1], next_columns=columns_low, next_blocks=blocks_low),
+        first_mid, mid_pair, mid_chip, step,
+    )
+    kept.append(vector)
+    sources.append(source)
+    diagonals.append(diagonal)
+
+    vector = next_vector
+    halos = exchange(vector, vector)
+    leave()
+
+    def sweep_low(name, vector, halos):
+        (vector,), leave = step(
+            name, functools.partial(sweep_kernel, panels, False), [vec(2)],
+            (columns_low, vector, *halos, sources[2], diagonals[2], blocks_low), scalars=(0,), scratch=ext(2),
+        )
+        halos = exchange(vector, vector)
+        leave()
+        return vector, halos
+
+    for k in range(2):
+        vector, halos = sweep_low(f"down2{k}", vector, halos)
+    (own_piece, outgoing), _ = step(
+        "lowest", functools.partial(lowest_kernel, panels),
+        [((panels, width), F32), ((devices, panels // 2, width), F32)],
+        (columns_low, vector, *halos, sources[2], blocks_low, aggregates[2], images),
+        scalars=(0,), scratch=ext(2), tokens=[fine_pair],
+    )
+    incoming = lax.all_to_all(outgoing, AXES, 0, 0)
+    (vector,), leave = step(
+        "chain", functools.partial(chain_kernel, panels), [vec(2)],
+        (own_piece, incoming, coarse_ops, coarse_maps, aggregates[2], vector),
+    )
+    halos = exchange(vector, vector)
+    leave()
+    for k in range(2):
+        vector, halos = sweep_low(f"up2{k}", vector, halos)
+    (vector, packed), leave = step(
+        "prolong2", functools.partial(prolong_kernel, panels), [vec(1), rows(counts[1] + HALO)],
+        (columns_low, vector, *halos, sources[2], diagonals[2], blocks_low, aggregates[1], kept[1]),
+        scalars=(0,), scratch=ext(2),
+    )
+
+    pair = inner_swap(packed)
+    chip = outer_swap(jnp.concatenate([vector, pair[size:]]))
+    leave()
+    far = inner_swap(chip[:size])
+    (vector, pair_edge, chip_edge), leave = wide_call(
+        1, "up", mid_layout(size), [vec(0), rows(wide[0]), rows(wide[0])],
+        dict(vector=vector, pair=pair, chip=chip, far=far, pair_source=first_mid[0], chip_source=first_mid[1],
+             aggregate=aggregates[0], upper=kept[0]),
+        first_mid, mid_pair, mid_chip, step,
+    )
+
+    pair, chip = exchange(pair_edge, chip_edge)
+    layout = {
+        name: [side(reach[0], 1, (array, 0), (array + "_source", edge_rows + 8), (which, 0)),
+               side(HALO, 1, (array, reach[0] * panels))]
+        for name, array, which in (("out", "chip", 1), ("in", "pair", 0))
+    }
+    return wide_call(
+        0, "last", layout, [(pulse_rhs.shape, F32)],
+        dict(vector=vector, pair=pair, chip=chip, pair_source=first_halos[0], chip_source=first_halos[1]),
+        (*first_halos, edge_rows), fine_pair, [arrived[f"fine{k}"] for k in range(reach[0])], step,
+    )[0][0]
+
+
+LEAVE = {'first': ('mid0', 'mid1'), 'sweep00': ('mid2',), 'sweep01': ('mid3',), 'wide_down1': ('fine0',), 'chain': ('fine1',), 'up20': ('fine2',), 'up21': ('fine3',)}
+ARRIVE = {'sweep01': ('mid0', 'mid1'), 'residual0': ('mid2',), 'down21': ('fine0',), 'up21': ('fine1',), 'prolong2': ('fine2',)}
 
 
 def solution(mesh):

time: 180 us -> 163 us (0.906)
  waiting for transfers between devices: 56.8 us -> 34.4 us
  starting transfers between devices: 70.1 us -> 74.5 us
    ppermute x36, waiting for transfers between devices: 56.8 us -> 34.4 us  [the longest x20 31 us: outer_swap(): lax.ppermute(value, AXES, swaps([(2 * k + 1, 2 * k + 2) for k in range(co...]
    ppermute x36, starting transfers between devices: 70.1 us -> 74.5 us  [the longest x20 71.2 us: outer_swap(): lax.ppermute(value, AXES, swaps([(2 * k + 1, 2 * k + 2) for k in range(co...]
    unnamed x27 -> x32, local copies, waits for them, and re-layouts: 3.96 us -> 5.12 us
    pallas_call x21 -> x16, Pallas kernels: 33.7 us -> 33.5 us  [call(): pl.pallas_call(body, out_shape=[jax.ShapeDtypeStruct(s, t) for s, t in sh...]
  transfers between devices with their start and end apart: 36 -> 36, of which waited for: 18 -> 12; matrix products, arithmetic and copies ran while one was open for 0% -> 0% of each run, Pallas kernels for 1% -> 12%
where the time goes in v2:
time: 163 us; the launch traced here: 162 us
  starting transfers between devices  74.5 us (46%)
  waiting for transfers between devices  34.4 us (21%)
  Pallas kernels  33.5 us (21%)
  blocking collectives  13.4 us (8%)
  local copies, waits for them, and re-layouts  5.15 us (3%)
    ppermute x20, starting transfers between devices, outer_swap(): lax.ppermute(value, AXES, swaps([(2 * k + 1, 2 * k + 2) for k in range(co...  71.2 us
    pallas_call x16, Pallas kernels, call(): pl.pallas_call(body, out_shape=[jax.ShapeDtypeStruct(s, t) for s, t in sh...  33.5 us
    ppermute x20, waiting for transfers between devices, outer_swap(): lax.ppermute(value, AXES, swaps([(2 * k + 1, 2 * k + 2) for k in range(co...  31 us
    all_to_all x1, blocking collectives, on_device(): incoming = lax.all_to_all(outgoing, AXES, 0, 0)  13.4 us
    unnamed x32, local copies, waits for them, and re-layouts  5.12 us
    ppermute x16, waiting for transfers between devices, inner_swap(): lax.ppermute(value, AXES, swaps([(2 * k, 2 * k + 1) for k in range(count...  3.47 us
    ppermute x16, starting transfers between devices, inner_swap(): lax.ppermute(value, AXES, swaps([(2 * k, 2 * k + 1) for k in range(count...  3.34 us
  transfers between devices with their start and end apart: 36, of which 12 were waited for; matrix products, arithmetic and copies ran while one was open for 0% of the time, Pallas kernels for 12%

profile of v2, /device:TPU:7, one launch (start us, length us, event | category | flops | bytes accessed | tf_op | source)
XLA Modules:
  0.0 161.8 jit_solution(10572198289719775998)
XLA Ops:
  6.9 3.6 %collective-permute-start.1 = (f32[200,128]{1,0:T(8,128)S(1)}, f32[200,128]{1,0:T(8,128)S(1)}, u32[]{:S(2)}, u32[]{:S(2)}) collective-permute-start(f32[200,128]{1,0:T(8,128)S(1)} %get-tuple-element.43), channel_id=1, source_target_pairs={{1,2},{2,1},{3,4},{4,3},{5,6},{6,5},{7,8},{8,7},{9,10},{10,9},{11,... | collective-permute-start | bytes 307208 | tf_op jit(solution)/shard_map/ppermute | solution.py:544
  10.5 4.0 %collective-permute-start.4 = (f32[1,4,128,128]{3,2,1,0:T(8,128)S(1)}, f32[1,4,128,128]{3,2,1,0:T(8,128)S(1)}, u32[]{:S(2)}, u32[]{:S(2)}) collective-permute-start(f32[1,4,128,128]{3,2,1,0:T(8,128)S(1)} %get-tuple-element.48), channel_id=1, source_target_pairs={{1,2},{2,1},{3,4},{4,3},{5,6},{6,5},{7,8},{8,7},{9,10},{10,9},{11,... | collective-permute-start | bytes 786440 | tf_op jit(solution)/shard_map/ppermute | solution.py:544
  14.5 3.4 %collective-permute-start.5 = (f32[1,4,128,128]{3,2,1,0:T(8,128)S(1)}, f32[1,4,128,128]{3,2,1,0:T(8,128)S(1)}, u32[]{:S(2)}, u32[]{:S(2)}) collective-permute-start(f32[1,4,128,128]{3,2,1,0:T(8,128)S(1)} %get-tuple-element.49), channel_id=1, source_target_pairs={{1,2},{2,1},{3,4},{4,3},{5,6},{6,5},{7,8},{8,7},{9,10},{10,9},{11,... | collective-permute-start | bytes 786440 | tf_op jit(solution)/shard_map/ppermute | solution.py:544
  20.0 4.0 %collective-permute-start.3 = (f32[64,128]{1,0:T(8,128)S(1)}, f32[64,128]{1,0:T(8,128)S(1)}, u32[]{:S(2)}, u32[]{:S(2)}) collective-permute-start(f32[64,128]{1,0:T(8,128)S(1)} %get-tuple-element.47), channel_id=1, source_target_pairs={{1,2},{2,1},{3,4},{4,3},{5,6},{6,5},{7,8},{8,7},{9,10},{10,9},{11,... | collective-permute-start | bytes 98312 | tf_op jit(solution)/shard_map/ppermute | solution.py:544
  24.1 3.4 %collective-permute-start.8 = (f32[1,4,128,128]{3,2,1,0:T(8,128)S(1)}, f32[1,4,128,128]{3,2,1,0:T(8,128)S(1)}, u32[]{:S(2)}, u32[]{:S(2)}) collective-permute-start(f32[1,4,128,128]{3,2,1,0:T(8,128)S(1)} %get-tuple-element.53), channel_id=1, source_target_pairs={{1,2},{2,1},{3,4},{4,3},{5,6},{6,5},{7,8},{8,7},{9,10},{10,9},{11,... | collective-permute-start | bytes 786440 | tf_op jit(solution)/shard_map/ppermute | solution.py:544
  30.3 4.0 %collective-permute-start.7 = (f32[64,128]{1,0:T(8,128)S(1)}, f32[64,128]{1,0:T(8,128)S(1)}, u32[]{:S(2)}, u32[]{:S(2)}) collective-permute-start(f32[64,128]{1,0:T(8,128)S(1)} %get-tuple-element.52), channel_id=1, source_target_pairs={{1,2},{2,1},{3,4},{4,3},{5,6},{6,5},{7,8},{8,7},{9,10},{10,9},{11,... | collective-permute-start | bytes 98312 | tf_op jit(solution)/shard_map/ppermute | solution.py:544
  34.3 3.0 %collective-permute-done.7.refs_3_ = f32[64,128]{1,0:T(8,128)S(1)} collective-permute-done((f32[64,128]{1,0:T(8,128)S(1)}, f32[64,128]{1,0:T(8,128)S(1)}, u32[]{:S(2)}, u32[]{:S(2)}) %collective-permute-start.7) | collective-permute-done | bytes 32800 | tf_op jit(solution)/shard_map/ppermute | solution.py:544
  39.7 4.0 %collective-permute-start.13 = (f32[1,4,128,128]{3,2,1,0:T(8,128)S(1)}, f32[1,4,128,128]{3,2,1,0:T(8,128)S(1)}, u32[]{:S(2)}, u32[]{:S(2)}) collective-permute-start(f32[1,4,128,128]{3,2,1,0:T(8,128)S(1)} %get-tuple-element.58), channel_id=1, source_target_pairs={{1,2},{2,1},{3,4},{4,3},{5,6},{6,5},{7,8},{8,7},{9,10},{10,9},{11,... | collective-permute-start | bytes 786440 | tf_op jit(solution)/shard_map/ppermute | solution.py:544
  43.7 3.4 %collective-permute-start.10 = (f32[328,128]{1,0:T(8,128)S(1)}, f32[328,128]{1,0:T(8,128)S(1)}, u32[]{:S(2)}, u32[]{:S(2)}) collective-permute-start(f32[328,128]{1,0:T(8,128)S(1)} %pad_maximum_fusion), channel_id=1, source_target_pairs={{1,2},{2,1},{3,4},{4,3},{5,6},{6,5},{7,8},{8,7},{9,10},{10,9},{11,... | collective-permute-start | bytes 503816 | tf_op jit(solution)/shard_map/ppermute | solution.py:544
  47.1 5.1 %collective-permute-done.10.refs_2_.refs_5_.refs_14_.refs_13_ = f32[328,128]{1,0:T(8,128)S(1)} collective-permute-done((f32[328,128]{1,0:T(8,128)S(1)}, f32[328,128]{1,0:T(8,128)S(1)}, u32[]{:S(2)}, u32[]{:S(2)}) %collective-permute-start.10) | collective-permute-done | bytes 167968 | tf_op jit(solution)/shard_map/ppermute | solution.py:544
  53.6 3.4 %wide_down1.1 = (f32[128,128]{1,0:T(8,128)S(1)}, f32[64,128]{1,0:T(8,128)S(1)}, f32[2,128]{1,0:T(2,128)S(1)}, f32[64,128]{1,0:T(8,128)S(1)}, f32[1,4,128,128]{3,2,1,0:T(8,128)S(1)}) custom-call(f32[128,128]{1,0:T(8,128)S(1)} %get-tuple-element.54.refs_0_, f32[328,128]{1,0:T(8,128)S(1)} %collective-permute-done.9.refs_1_.refs_4_.refs_13_.refs_12_, ...), custom_call_target="tpu_custom_call" | custom-call | tf_op jit(solution)/shard_map/wide_down1/pallas_call | solution.py:522
  57.0 4.6 %collective-permute-start.18 = (f32[1,4,128,128]{3,2,1,0:T(8,128)S(1)}, f32[1,4,128,128]{3,2,1,0:T(8,128)S(1)}, u32[]{:S(2)}, u32[]{:S(2)}) collective-permute-start(f32[1,4,128,128]{3,2,1,0:T(8,128)S(1)} %get-tuple-element.62), channel_id=1, source_target_pairs={{1,2},{2,1},{3,4},{4,3},{5,6},{6,5},{7,8},{8,7},{9,10},{10,9},{11,... | collective-permute-start | bytes 786440 | tf_op jit(solution)/shard_map/ppermute | solution.py:544
  61.6 2.8 %collective-permute-start.15 = (f32[64,128]{1,0:T(8,128)S(1)}, f32[64,128]{1,0:T(8,128)S(1)}, u32[]{:S(2)}, u32[]{:S(2)}) collective-permute-start(f32[64,128]{1,0:T(8,128)S(1)} %get-tuple-element.59.refs_1_), channel_id=1, source_target_pairs={{1,2},{2,1},{3,4},{4,3},{5,6},{6,5},{7,8},{8,7},{9,10},{10,9},{11,... | collective-permute-start | bytes 98312 | tf_op jit(solution)/shard_map/ppermute | solution.py:544
  64.5 4.2 %collective-permute-done.15.refs_3_ = f32[64,128]{1,0:T(8,128)S(1)} collective-permute-done((f32[64,128]{1,0:T(8,128)S(1)}, f32[64,128]{1,0:T(8,128)S(1)}, u32[]{:S(2)}, u32[]{:S(2)}) %collective-permute-start.15) | collective-permute-done | bytes 32800 | tf_op jit(solution)/shard_map/ppermute | solution.py:544
  69.5 2.9 %collective-permute-start.17 = (f32[64,128]{1,0:T(8,128)S(1)}, f32[64,128]{1,0:T(8,128)S(1)}, u32[]{:S(2)}, u32[]{:S(2)}) collective-permute-start(f32[64,128]{1,0:T(8,128)S(1)} %down20.1.refs_1_), channel_id=1, source_target_pairs={{1,2},{2,1},{3,4},{4,3},{5,6},{6,5},{7,8},{8,7},{9,10},{10,9},{11,... | collective-permute-start | bytes 98312 | tf_op jit(solution)/shard_map/ppermute | solution.py:544
  72.5 4.0 %collective-permute-done.17.refs_3_ = f32[64,128]{1,0:T(8,128)S(1)} collective-permute-done((f32[64,128]{1,0:T(8,128)S(1)}, f32[64,128]{1,0:T(8,128)S(1)}, u32[]{:S(2)}, u32[]{:S(2)}) %collective-permute-start.17) | collective-permute-done | bytes 32800 | tf_op jit(solution)/shard_map/ppermute | solution.py:544
  77.3 2.9 %collective-permute-start.20 = (f32[64,128]{1,0:T(8,128)S(1)}, f32[64,128]{1,0:T(8,128)S(1)}, u32[]{:S(2)}, u32[]{:S(2)}) collective-permute-start(f32[64,128]{1,0:T(8,128)S(1)} %down21.1.refs_1_.refs_5_), channel_id=1, source_target_pairs={{1,2},{2,1},{3,4},{4,3},{5,6},{6,5},{7,8},{8,7},{9,10},{10,9},{11,... | collective-permute-start | bytes 98312 | tf_op jit(solution)/shard_map/ppermute | solution.py:544
  85.5 13.4 %all_to_all.5.refs_1_ = f32[32,16,128]{2,1,0:T(8,128)S(1)} all-to-all(f32[32,16,128]{2,1,0:T(8,128)S(1)} %get-tuple-element.64), channel_id=1, replica_groups=mesh['parts'=16,'pair'=2] {'parts','pair'}, dimensions={0} | all-to-all | bytes 524288 | tf_op jit(solution)/shard_map/all_to_all | solution.py:704
  99.0 4.3 %chain.1 = (f32[64,128]{1,0:T(8,128)S(1)}, f32[1,4,128,128]{3,2,1,0:T(8,128)S(1)}) custom-call(f32[32,128]{1,0:T(8,128)S(1)} %get-tuple-element.63.refs_0_, f32[32,16,128]{2,1,0:T(8,128)S(1)} %all_to_all.5.refs_1_, f32[1,5,128,128]{3,2,1,0:T(8,128)S(1)} %copy-done.7, s32[1,4,128]{2,1,0:T(4,128)S(1)} %copy-done.13, s32[1,256]{1,0:T(1,128)S(1)} %bitcast.14, ...), custom_call_target="tpu_custom_call" | custom-call | tf_op jit(solution)/shard_map/chain/pallas_call | solution.py:522
  103.2 4.4 %collective-permute-start.23 = (f32[64,128]{1,0:T(8,128)S(1)}, f32[64,128]{1,0:T(8,128)S(1)}, u32[]{:S(2)}, u32[]{:S(2)}) collective-permute-start(f32[64,128]{1,0:T(8,128)S(1)} %get-tuple-element.65.refs_1_), channel_id=1, source_target_pairs={{1,2},{2,1},{3,4},{4,3},{5,6},{6,5},{7,8},{8,7},{9,10},{10,9},{11,... | collective-permute-start | bytes 98312 | tf_op jit(solution)/shard_map/ppermute | solution.py:544
  107.7 3.0 %collective-permute-start.26 = (f32[1,4,128,128]{3,2,1,0:T(8,128)S(1)}, f32[1,4,128,128]{3,2,1,0:T(8,128)S(1)}, u32[]{:S(2)}, u32[]{:S(2)}) collective-permute-start(f32[1,4,128,128]{3,2,1,0:T(8,128)S(1)} %get-tuple-element.67), channel_id=1, source_target_pairs={{1,2},{2,1},{3,4},{4,3},{5,6},{6,5},{7,8},{8,7},{9,10},{10,9},{11,... | collective-permute-start | bytes 786440 | tf_op jit(solution)/shard_map/ppermute | solution.py:544
  111.6 4.4 %collective-permute-start.29 = (f32[1,4,128,128]{3,2,1,0:T(8,128)S(1)}, f32[1,4,128,128]{3,2,1,0:T(8,128)S(1)}, u32[]{:S(2)}, u32[]{:S(2)}) collective-permute-start(f32[1,4,128,128]{3,2,1,0:T(8,128)S(1)} %get-tuple-element.70), channel_id=1, source_target_pairs={{1,2},{2,1},{3,4},{4,3},{5,6},{6,5},{7,8},{8,7},{9,10},{10,9},{11,... | collective-permute-start | bytes 786440 | tf_op jit(solution)/shard_map/ppermute | solution.py:544
  116.0 3.0 %collective-permute-start.25 = (f32[64,128]{1,0:T(8,128)S(1)}, f32[64,128]{1,0:T(8,128)S(1)}, u32[]{:S(2)}, u32[]{:S(2)}) collective-permute-start(f32[64,128]{1,0:T(8,128)S(1)} %get-tuple-element.66.refs_1_), channel_id=1, source_target_pairs={{1,2},{2,1},{3,4},{4,3},{5,6},{6,5},{7,8},{8,7},{9,10},{10,9},{11,... | collective-permute-start | bytes 98312 | tf_op jit(solution)/shard_map/ppermute | solution.py:544
  119.1 4.1 %collective-permute-done.25.refs_3_ = f32[64,128]{1,0:T(8,128)S(1)} collective-permute-done((f32[64,128]{1,0:T(8,128)S(1)}, f32[64,128]{1,0:T(8,128)S(1)}, u32[]{:S(2)}, u32[]{:S(2)}) %collective-permute-start.25) | collective-permute-done | bytes 32800 | tf_op jit(solution)/shard_map/ppermute | solution.py:544
  124.1 3.0 %collective-permute-start.28 = (f32[64,128]{1,0:T(8,128)S(1)}, f32[64,128]{1,0:T(8,128)S(1)}, u32[]{:S(2)}, u32[]{:S(2)}) collective-permute-start(f32[64,128]{1,0:T(8,128)S(1)} %get-tuple-element.68.refs_1_), channel_id=1, source_target_pairs={{1,2},{2,1},{3,4},{4,3},{5,6},{6,5},{7,8},{8,7},{9,10},{10,9},{11,... | collective-permute-start | bytes 98312 | tf_op jit(solution)/shard_map/ppermute | solution.py:544
  127.9 3.3 %collective-permute-done.28.refs_3_ = f32[64,128]{1,0:T(8,128)S(1)} collective-permute-done((f32[64,128]{1,0:T(8,128)S(1)}, f32[64,128]{1,0:T(8,128)S(1)}, u32[]{:S(2)}, u32[]{:S(2)}) %collective-permute-start.28) | collective-permute-done | bytes 32800 | tf_op jit(solution)/shard_map/ppermute | solution.py:544
  133.8 2.9 %collective-permute-start.31 = (f32[192,128]{1,0:T(8,128)S(1)}, f32[192,128]{1,0:T(8,128)S(1)}, u32[]{:S(2)}, u32[]{:S(2)}) collective-permute-start(f32[192,128]{1,0:T(8,128)S(1)} %pad_maximum_fusion.1), channel_id=1, source_target_pairs={{1,2},{2,1},{3,4},{4,3},{5,6},{6,5},{7,8},{8,7},{9,10},{10,9},{11,... | collective-permute-start | bytes 294920 | tf_op jit(solution)/shard_map/ppermute | solution.py:544
  136.8 4.6 %collective-permute-start.35 = (f32[1,4,128,128]{3,2,1,0:T(8,128)S(1)}, f32[1,4,128,128]{3,2,1,0:T(8,128)S(1)}, u32[]{:S(2)}, u32[]{:S(2)}) collective-permute-start(f32[1,4,128,128]{3,2,1,0:T(8,128)S(1)} %get-tuple-element.76), channel_id=1, source_target_pairs={{1,2},{2,1},{3,4},{4,3},{5,6},{6,5},{7,8},{8,7},{9,10},{10,9},{11,... | collective-permute-start | bytes 786440 | tf_op jit(solution)/shard_map/ppermute | solution.py:544
  142.9 4.0 %wide_up1.1 = (f32[512,128]{1,0:T(8,128)S(1)}, f32[192,128]{1,0:T(8,128)S(1)}, f32[192,128]{1,0:T(8,128)S(1)}) custom-call(f32[128,128]{1,0:T(8,128)S(1)} %get-tuple-element.71.refs_0_, f32[192,128]{1,0:T(8,128)S(1)} %collective-permute-done.30.refs_1_, f32[192,128]{1,0:T(8,128)S(1)} %collective-permute-done.31.refs_2_, ...), custom_call_target="tpu_custom_call" | custom-call | tf_op jit(solution)/shard_map/wide_up1/pallas_call | solution.py:522
  147.1 3.0 %collective-permute-start.34 = (f32[192,128]{1,0:T(8,128)S(1)}, f32[192,128]{1,0:T(8,128)S(1)}, u32[]{:S(2)}, u32[]{:S(2)}) collective-permute-start(f32[192,128]{1,0:T(8,128)S(1)} %get-tuple-element.75), channel_id=1, source_target_pairs={{1,2},{2,1},{3,4},{4,3},{5,6},{6,5},{7,8},{8,7},{9,10},{10,9},{11,... | collective-permute-start | bytes 294920 | tf_op jit(solution)/shard_map/ppermute | solution.py:544
  150.1 4.7 %collective-permute-done.34.refs_2_ = f32[192,128]{1,0:T(8,128)S(1)} collective-permute-done((f32[192,128]{1,0:T(8,128)S(1)}, f32[192,128]{1,0:T(8,128)S(1)}, u32[]{:S(2)}, u32[]{:S(2)}) %collective-permute-start.34) | collective-permute-done | bytes 98336 | tf_op jit(solution)/shard_map/ppermute | solution.py:544
  154.9 6.8 %wide_last0.1 = f32[32,2048]{1,0:T(8,128)} custom-call(f32[512,128]{1,0:T(8,128)S(1)} %get-tuple-element.73.refs_0_, f32[192,128]{1,0:T(8,128)S(1)} %collective-permute-done.33.refs_1_, f32[192,128]{1,0:T(8,128)S(1)} %collective-permute-done.34.refs_2_, f32[200,128]{1,0:T(8,128)S(1)} %collective-permute-done.refs_2_.refs_3_.refs_9_, ...), custom_call_target="tpu_custom_call" | custom-call | tf_op jit(solution)/shard_map/wide_last0/pallas_call | solution.py:522
  (96 shorter events, 29.5 us)
Async XLA Ops:
  0.0 53.6 %collective-permute-start.12 = (f32[4,4,128,128]{3,2,1,0:T(8,128)}, f32[4,4,128,128]{3,2,1,0:T(8,128)S(1)}, u32[]{:S(2)}, u32[]{:S(2)}) collective-permute-start(f32[4,4,128,128]{3,2,1,0:T(8,128)} %refs_10_.1), channel_id=1, source_target_pairs={{0,1},{1,0},{2,3},{3,2},{4,5},{5,4},{6,7},{7,6},{8,9},{9,8},{10,11... | collective-permute-start | bytes 3145736 | tf_op jit(solution)/shard_map/ppermute | solution.py:539
  6.8 11.1 %collective-permute-start = (f32[200,128]{1,0:T(8,128)S(1)}, f32[200,128]{1,0:T(8,128)S(1)}, u32[]{:S(2)}, u32[]{:S(2)}) collective-permute-start(f32[200,128]{1,0:T(8,128)S(1)} %get-tuple-element.42), channel_id=1, source_target_pairs={{0,1},{1,0},{2,3},{3,2},{4,5},{5,4},{6,7},{7,6},{8,9},{9,8},{10,11... | collective-permute-start | bytes 307208 | tf_op jit(solution)/shard_map/ppermute | solution.py:539
  6.9 11.0 %collective-permute-start.1 = (f32[200,128]{1,0:T(8,128)S(1)}, f32[200,128]{1,0:T(8,128)S(1)}, u32[]{:S(2)}, u32[]{:S(2)}) collective-permute-start(f32[200,128]{1,0:T(8,128)S(1)} %get-tuple-element.43), channel_id=1, source_target_pairs={{1,2},{2,1},{3,4},{4,3},{5,6},{6,5},{7,8},{8,7},{9,10},{10,9},{11,... | collective-permute-start | bytes 307208 | tf_op jit(solution)/shard_map/ppermute | solution.py:544
  10.5 17.2 %collective-permute-start.4 = (f32[1,4,128,128]{3,2,1,0:T(8,128)S(1)}, f32[1,4,128,128]{3,2,1,0:T(8,128)S(1)}, u32[]{:S(2)}, u32[]{:S(2)}) collective-permute-start(f32[1,4,128,128]{3,2,1,0:T(8,128)S(1)} %get-tuple-element.48), channel_id=1, source_target_pairs={{1,2},{2,1},{3,4},{4,3},{5,6},{6,5},{7,8},{8,7},{9,10},{10,9},{11,... | collective-permute-start | bytes 786440 | tf_op jit(solution)/shard_map/ppermute | solution.py:544
  14.5 13.2 %collective-permute-start.5 = (f32[1,4,128,128]{3,2,1,0:T(8,128)S(1)}, f32[1,4,128,128]{3,2,1,0:T(8,128)S(1)}, u32[]{:S(2)}, u32[]{:S(2)}) collective-permute-start(f32[1,4,128,128]{3,2,1,0:T(8,128)S(1)} %get-tuple-element.49), channel_id=1, source_target_pairs={{1,2},{2,1},{3,4},{4,3},{5,6},{6,5},{7,8},{8,7},{9,10},{10,9},{11,... | collective-permute-start | bytes 786440 | tf_op jit(solution)/shard_map/ppermute | solution.py:544
  20.0 4.1 %collective-permute-start.2 = (f32[64,128]{1,0:T(8,128)S(1)}, f32[64,128]{1,0:T(8,128)S(1)}, u32[]{:S(2)}, u32[]{:S(2)}) collective-permute-start(f32[64,128]{1,0:T(8,128)S(1)} %get-tuple-element.46), channel_id=1, source_target_pairs={{0,1},{1,0},{2,3},{3,2},{4,5},{5,4},{6,7},{7,6},{8,9},{9,8},{10,11... | collective-permute-start | bytes 98312 | tf_op jit(solution)/shard_map/ppermute | solution.py:539
  20.0 7.5 %collective-permute-start.3 = (f32[64,128]{1,0:T(8,128)S(1)}, f32[64,128]{1,0:T(8,128)S(1)}, u32[]{:S(2)}, u32[]{:S(2)}) collective-permute-start(f32[64,128]{1,0:T(8,128)S(1)} %get-tuple-element.47), channel_id=1, source_target_pairs={{1,2},{2,1},{3,4},{4,3},{5,6},{6,5},{7,8},{8,7},{9,10},{10,9},{11,... | collective-permute-start | bytes 98312 | tf_op jit(solution)/shard_map/ppermute | solution.py:544
  24.1 13.3 %collective-permute-start.8 = (f32[1,4,128,128]{3,2,1,0:T(8,128)S(1)}, f32[1,4,128,128]{3,2,1,0:T(8,128)S(1)}, u32[]{:S(2)}, u32[]{:S(2)}) collective-permute-start(f32[1,4,128,128]{3,2,1,0:T(8,128)S(1)} %get-tuple-element.53), channel_id=1, source_target_pairs={{1,2},{2,1},{3,4},{4,3},{5,6},{6,5},{7,8},{8,7},{9,10},{10,9},{11,... | collective-permute-start | bytes 786440 | tf_op jit(solution)/shard_map/ppermute | solution.py:544
  27.6 54.5 %collective-permute-start.21 = (f32[4,4,128,128]{3,2,1,0:T(8,128)S(1)}, f32[4,4,128,128]{3,2,1,0:T(8,128)S(1)}, u32[]{:S(2)}, u32[]{:S(2)}) collective-permute-start(f32[4,4,128,128]{3,2,1,0:T(8,128)S(1)} %near.1), channel_id=1, source_target_pairs={{0,1},{1,0},{2,3},{3,2},{4,5},{5,4},{6,7},{7,6},{8,9},{9,8},{10,11... | collective-permute-start | bytes 3145736 | tf_op jit(solution)/shard_map/ppermute | solution.py:539
  29.8 4.5 %collective-permute-start.6 = (f32[64,128]{1,0:T(8,128)S(1)}, f32[64,128]{1,0:T(8,128)S(1)}, u32[]{:S(2)}, u32[]{:S(2)}) collective-permute-start(f32[64,128]{1,0:T(8,128)S(1)} %get-tuple-element.51), channel_id=1, source_target_pairs={{0,1},{1,0},{2,3},{3,2},{4,5},{5,4},{6,7},{7,6},{8,9},{9,8},{10,11... | collective-permute-start | bytes 98312 | tf_op jit(solution)/shard_map/ppermute | solution.py:539
  30.3 7.0 %collective-permute-start.7 = (f32[64,128]{1,0:T(8,128)S(1)}, f32[64,128]{1,0:T(8,128)S(1)}, u32[]{:S(2)}, u32[]{:S(2)}) collective-permute-start(f32[64,128]{1,0:T(8,128)S(1)} %get-tuple-element.52), channel_id=1, source_target_pairs={{1,2},{2,1},{3,4},{4,3},{5,6},{6,5},{7,8},{8,7},{9,10},{10,9},{11,... | collective-permute-start | bytes 98312 | tf_op jit(solution)/shard_map/ppermute | solution.py:544
  39.6 4.1 %collective-permute-start.9 = (f32[328,128]{1,0:T(8,128)S(1)}, f32[328,128]{1,0:T(8,128)S(1)}, u32[]{:S(2)}, u32[]{:S(2)}) collective-permute-start(f32[328,128]{1,0:T(8,128)S(1)} %get-tuple-element.55), channel_id=1, source_target_pairs={{0,1},{1,0},{2,3},{3,2},{4,5},{5,4},{6,7},{7,6},{8,9},{9,8},{10,11... | collective-permute-start | bytes 503816 | tf_op jit(solution)/shard_map/ppermute | solution.py:539
  39.7 13.0 %collective-permute-start.13 = (f32[1,4,128,128]{3,2,1,0:T(8,128)S(1)}, f32[1,4,128,128]{3,2,1,0:T(8,128)S(1)}, u32[]{:S(2)}, u32[]{:S(2)}) collective-permute-start(f32[1,4,128,128]{3,2,1,0:T(8,128)S(1)} %get-tuple-element.58), channel_id=1, source_target_pairs={{1,2},{2,1},{3,4},{4,3},{5,6},{6,5},{7,8},{8,7},{9,10},{10,9},{11,... | collective-permute-start | bytes 786440 | tf_op jit(solution)/shard_map/ppermute | solution.py:544
  43.7 8.5 %collective-permute-start.10 = (f32[328,128]{1,0:T(8,128)S(1)}, f32[328,128]{1,0:T(8,128)S(1)}, u32[]{:S(2)}, u32[]{:S(2)}) collective-permute-start(f32[328,128]{1,0:T(8,128)S(1)} %pad_maximum_fusion), channel_id=1, source_target_pairs={{1,2},{2,1},{3,4},{4,3},{5,6},{6,5},{7,8},{8,7},{9,10},{10,9},{11,... | collective-permute-start | bytes 503816 | tf_op jit(solution)/shard_map/ppermute | solution.py:544
  57.0 19.5 %collective-permute-start.18 = (f32[1,4,128,128]{3,2,1,0:T(8,128)S(1)}, f32[1,4,128,128]{3,2,1,0:T(8,128)S(1)}, u32[]{:S(2)}, u32[]{:S(2)}) collective-permute-start(f32[1,4,128,128]{3,2,1,0:T(8,128)S(1)} %get-tuple-element.62), channel_id=1, source_target_pairs={{1,2},{2,1},{3,4},{4,3},{5,6},{6,5},{7,8},{8,7},{9,10},{10,9},{11,... | collective-permute-start | bytes 786440 | tf_op jit(solution)/shard_map/ppermute | solution.py:544
  61.6 7.0 %collective-permute-start.15 = (f32[64,128]{1,0:T(8,128)S(1)}, f32[64,128]{1,0:T(8,128)S(1)}, u32[]{:S(2)}, u32[]{:S(2)}) collective-permute-start(f32[64,128]{1,0:T(8,128)S(1)} %get-tuple-element.59.refs_1_), channel_id=1, source_target_pairs={{1,2},{2,1},{3,4},{4,3},{5,6},{6,5},{7,8},{8,7},{9,10},{10,9},{11,... | collective-permute-start | bytes 98312 | tf_op jit(solution)/shard_map/ppermute | solution.py:544
  64.4 4.2 %collective-permute-start.14 = (f32[64,128]{1,0:T(8,128)S(1)}, f32[64,128]{1,0:T(8,128)S(1)}, u32[]{:S(2)}, u32[]{:S(2)}) collective-permute-start(f32[64,128]{1,0:T(8,128)S(1)} %get-tuple-element.59.refs_1_), channel_id=1, source_target_pairs={{0,1},{1,0},{2,3},{3,2},{4,5},{5,4},{6,7},{7,6},{8,9},{9,8},{10,11... | collective-permute-start | bytes 98312 | tf_op jit(solution)/shard_map/ppermute | solution.py:539
  69.5 7.0 %collective-permute-start.17 = (f32[64,128]{1,0:T(8,128)S(1)}, f32[64,128]{1,0:T(8,128)S(1)}, u32[]{:S(2)}, u32[]{:S(2)}) collective-permute-start(f32[64,128]{1,0:T(8,128)S(1)} %down20.1.refs_1_), channel_id=1, source_target_pairs={{1,2},{2,1},{3,4},{4,3},{5,6},{6,5},{7,8},{8,7},{9,10},{10,9},{11,... | collective-permute-start | bytes 98312 | tf_op jit(solution)/shard_map/ppermute | solution.py:544
  72.4 4.1 %collective-permute-start.16 = (f32[64,128]{1,0:T(8,128)S(1)}, f32[64,128]{1,0:T(8,128)S(1)}, u32[]{:S(2)}, u32[]{:S(2)}) collective-permute-start(f32[64,128]{1,0:T(8,128)S(1)} %down20.1.refs_1_), channel_id=1, source_target_pairs={{0,1},{1,0},{2,3},{3,2},{4,5},{5,4},{6,7},{7,6},{8,9},{9,8},{10,11... | collective-permute-start | bytes 98312 | tf_op jit(solution)/shard_map/ppermute | solution.py:539
  77.3 7.0 %collective-permute-start.20 = (f32[64,128]{1,0:T(8,128)S(1)}, f32[64,128]{1,0:T(8,128)S(1)}, u32[]{:S(2)}, u32[]{:S(2)}) collective-permute-start(f32[64,128]{1,0:T(8,128)S(1)} %down21.1.refs_1_.refs_5_), channel_id=1, source_target_pairs={{1,2},{2,1},{3,4},{4,3},{5,6},{6,5},{7,8},{8,7},{9,10},{10,9},{11,... | collective-permute-start | bytes 98312 | tf_op jit(solution)/shard_map/ppermute | solution.py:544
  80.3 4.1 %collective-permute-start.19 = (f32[64,128]{1,0:T(8,128)S(1)}, f32[64,128]{1,0:T(8,128)S(1)}, u32[]{:S(2)}, u32[]{:S(2)}) collective-permute-start(f32[64,128]{1,0:T(8,128)S(1)} %down21.1.refs_1_.refs_5_), channel_id=1, source_target_pairs={{0,1},{1,0},{2,3},{3,2},{4,5},{5,4},{6,7},{7,6},{8,9},{9,8},{10,11... | collective-permute-start | bytes 98312 | tf_op jit(solution)/shard_map/ppermute | solution.py:539
  103.2 7.5 %collective-permute-start.23 = (f32[64,128]{1,0:T(8,128)S(1)}, f32[64,128]{1,0:T(8,128)S(1)}, u32[]{:S(2)}, u32[]{:S(2)}) collective-permute-start(f32[64,128]{1,0:T(8,128)S(1)} %get-tuple-element.65.refs_1_), channel_id=1, source_target_pairs={{1,2},{2,1},{3,4},{4,3},{5,6},{6,5},{7,8},{8,7},{9,10},{10,9},{11,... | collective-permute-start | bytes 98312 | tf_op jit(solution)/shard_map/ppermute | solution.py:544
  107.7 15.4 %collective-permute-start.26 = (f32[1,4,128,128]{3,2,1,0:T(8,128)S(1)}, f32[1,4,128,128]{3,2,1,0:T(8,128)S(1)}, u32[]{:S(2)}, u32[]{:S(2)}) collective-permute-start(f32[1,4,128,128]{3,2,1,0:T(8,128)S(1)} %get-tuple-element.67), channel_id=1, source_target_pairs={{1,2},{2,1},{3,4},{4,3},{5,6},{6,5},{7,8},{8,7},{9,10},{10,9},{11,... | collective-permute-start | bytes 786440 | tf_op jit(solution)/shard_map/ppermute | solution.py:544
  111.6 16.3 %collective-permute-start.29 = (f32[1,4,128,128]{3,2,1,0:T(8,128)S(1)}, f32[1,4,128,128]{3,2,1,0:T(8,128)S(1)}, u32[]{:S(2)}, u32[]{:S(2)}) collective-permute-start(f32[1,4,128,128]{3,2,1,0:T(8,128)S(1)} %get-tuple-element.70), channel_id=1, source_target_pairs={{1,2},{2,1},{3,4},{4,3},{5,6},{6,5},{7,8},{8,7},{9,10},{10,9},{11,... | collective-permute-start | bytes 786440 | tf_op jit(solution)/shard_map/ppermute | solution.py:544
  116.0 7.1 %collective-permute-start.25 = (f32[64,128]{1,0:T(8,128)S(1)}, f32[64,128]{1,0:T(8,128)S(1)}, u32[]{:S(2)}, u32[]{:S(2)}) collective-permute-start(f32[64,128]{1,0:T(8,128)S(1)} %get-tuple-element.66.refs_1_), channel_id=1, source_target_pairs={{1,2},{2,1},{3,4},{4,3},{5,6},{6,5},{7,8},{8,7},{9,10},{10,9},{11,... | collective-permute-start | bytes 98312 | tf_op jit(solution)/shard_map/ppermute | solution.py:544
  119.0 4.1 %collective-permute-start.24 = (f32[64,128]{1,0:T(8,128)S(1)}, f32[64,128]{1,0:T(8,128)S(1)}, u32[]{:S(2)}, u32[]{:S(2)}) collective-permute-start(f32[64,128]{1,0:T(8,128)S(1)} %get-tuple-element.66.refs_1_), channel_id=1, source_target_pairs={{0,1},{1,0},{2,3},{3,2},{4,5},{5,4},{6,7},{7,6},{8,9},{9,8},{10,11... | collective-permute-start | bytes 98312 | tf_op jit(solution)/shard_map/ppermute | solution.py:539
  124.1 7.2 %collective-permute-start.28 = (f32[64,128]{1,0:T(8,128)S(1)}, f32[64,128]{1,0:T(8,128)S(1)}, u32[]{:S(2)}, u32[]{:S(2)}) collective-permute-start(f32[64,128]{1,0:T(8,128)S(1)} %get-tuple-element.68.refs_1_), channel_id=1, source_target_pairs={{1,2},{2,1},{3,4},{4,3},{5,6},{6,5},{7,8},{8,7},{9,10},{10,9},{11,... | collective-permute-start | bytes 98312 | tf_op jit(solution)/shard_map/ppermute | solution.py:544
  127.1 4.1 %collective-permute-start.27 = (f32[64,128]{1,0:T(8,128)S(1)}, f32[64,128]{1,0:T(8,128)S(1)}, u32[]{:S(2)}, u32[]{:S(2)}) collective-permute-start(f32[64,128]{1,0:T(8,128)S(1)} %get-tuple-element.68.refs_1_), channel_id=1, source_target_pairs={{0,1},{1,0},{2,3},{3,2},{4,5},{5,4},{6,7},{7,6},{8,9},{9,8},{10,11... | collective-permute-start | bytes 98312 | tf_op jit(solution)/shard_map/ppermute | solution.py:539
  133.8 7.8 %collective-permute-start.31 = (f32[192,128]{1,0:T(8,128)S(1)}, f32[192,128]{1,0:T(8,128)S(1)}, u32[]{:S(2)}, u32[]{:S(2)}) collective-permute-start(f32[192,128]{1,0:T(8,128)S(1)} %pad_maximum_fusion.1), channel_id=1, source_target_pairs={{1,2},{2,1},{3,4},{4,3},{5,6},{6,5},{7,8},{8,7},{9,10},{10,9},{11,... | collective-permute-start | bytes 294920 | tf_op jit(solution)/shard_map/ppermute | solution.py:544
  136.8 13.4 %collective-permute-start.35 = (f32[1,4,128,128]{3,2,1,0:T(8,128)S(1)}, f32[1,4,128,128]{3,2,1,0:T(8,128)S(1)}, u32[]{:S(2)}, u32[]{:S(2)}) collective-permute-start(f32[1,4,128,128]{3,2,1,0:T(8,128)S(1)} %get-tuple-element.76), channel_id=1, source_target_pairs={{1,2},{2,1},{3,4},{4,3},{5,6},{6,5},{7,8},{8,7},{9,10},{10,9},{11,... | collective-permute-start | bytes 786440 | tf_op jit(solution)/shard_map/ppermute | solution.py:544
  146.9 3.2 %collective-permute-start.33 = (f32[192,128]{1,0:T(8,128)S(1)}, f32[192,128]{1,0:T(8,128)S(1)}, u32[]{:S(2)}, u32[]{:S(2)}) collective-permute-start(f32[192,128]{1,0:T(8,128)S(1)} %get-tuple-element.74), channel_id=1, source_target_pairs={{0,1},{1,0},{2,3},{3,2},{4,5},{5,4},{6,7},{7,6},{8,9},{9,8},{10,11... | collective-permute-start | bytes 294920 | tf_op jit(solution)/shard_map/ppermute | solution.py:539
  147.1 7.7 %collective-permute-start.34 = (f32[192,128]{1,0:T(8,128)S(1)}, f32[192,128]{1,0:T(8,128)S(1)}, u32[]{:S(2)}, u32[]{:S(2)}) collective-permute-start(f32[192,128]{1,0:T(8,128)S(1)} %get-tuple-element.75), channel_id=1, source_target_pairs={{1,2},{2,1},{3,4},{4,3},{5,6},{6,5},{7,8},{8,7},{9,10},{10,9},{11,... | collective-permute-start | bytes 294920 | tf_op jit(solution)/shard_map/ppermute | solution.py:544
  (20 other events, 279.5 us)

commit v3 on v2

--- a/solution.py
+++ b/solution.py
@@ -92,6 +92,32 @@
         extended[(1 - core) * (count + HALO) + tile] = stack(pair_halo[rows])
 
 
+def dims(blocks):
+    if len(blocks.shape) == 4:
+        return blocks.shape[0], blocks.shape[1], blocks.shape[-1]
+    return blocks.shape[0], 2 * blocks.shape[1] // blocks.shape[2], blocks.shape[2] // 2
+
+
+def prepare_kernel(blocks_hbm, weights, blocks, semaphores):
+    count, links, width = blocks.shape[0], blocks.shape[1], blocks.shape[-1]
+    chunks = semaphores.shape[0]
+    size = count // chunks
+    copies = [
+        pltpu.make_async_copy(blocks_hbm.at[pl.ds(k * size, size)], blocks.at[pl.ds(k * size, size)], semaphores.at[k])
+        for k in range(chunks)
+    ]
+    for copy in copies:
+        copy.start()
+    for tile in range(count):
+        if tile % size == 0:
+            copies[tile // size].wait()
+        for link in range(links):
+            high, low = split(blocks[tile, link].T)
+            rows = slice(link * width, (link + 1) * width)
+            weights[tile, rows, :width] = high
+            weights[tile, rows, width:] = low
+
+
 def weights_of(blocks, tile):
     parts = [split(blocks[tile, k]) for k in range(blocks.shape[1])]
     return jnp.concatenate(
@@ -100,8 +126,11 @@
 
 
 def tile_apply(columns, blocks, extended, tile, shift=0):
-    picked = [extended[column(columns, blocks, tile, k) + shift] for k in range(blocks.shape[1])]
-    return product(jnp.concatenate(picked, axis=1), weights_of(blocks, tile), NT, blocks.shape[-1])
+    _, links, width = dims(blocks)
+    picked = jnp.concatenate([extended[column(columns, blocks, tile, k) + shift] for k in range(links)], axis=1)
+    if len(blocks.shape) == 3:
+        return product(picked, blocks[tile], NN, width)
+    return product(picked, weights_of(blocks, tile), NT, width)
 
 
 def put_edges(vector, count, panels, pair_edge, chip_edge):
@@ -135,17 +164,29 @@
     return integer_row([column(columns, blocks, first + t, k) for t in range(tiles) for k in range(links)], width)
 
 
-def first_kernel(reach, columns, source, blocks, diagonal, vector, pair_edge, chip_edge):
+def first_kernel(
+    reach, columns, source, blocks_hbm, diagonal, vector, pair_edge, chip_edge, blocks, semaphores
+):
     panels = source.shape[0]
     count, width = blocks.shape[0], blocks.shape[-1]
     core = lax.axis_index("pair")
     start = HALO * panels
+    chunks = semaphores.shape[0]
+    size = count // chunks
+    copies = [
+        pltpu.make_async_copy(blocks_hbm.at[pl.ds(k * size, size)], blocks.at[pl.ds(k * size, size)], semaphores.at[k])
+        for k in range(chunks)
+    ]
+    for copy in copies:
+        copy.start()
     for edge, turn in ((pair_edge, 1 - core), (chip_edge, core)):
         edge[pl.ds(start, 8)] = columns_row(columns, blocks, turn * (count - reach), reach, width)
         for tile in range(reach):
             ahead, behind = get_tile(source, tile, panels, width), get_tile(source, count - reach + tile, panels, width)
             edge[pl.ds(start + 8 + tile * panels, panels)] = jnp.where(turn == 1, behind, ahead)
     for tile in range(count):
+        if tile % size == 0:
+            copies[tile // size].wait()
         row = tile_diagonal(columns, blocks, tile)
         diagonal[pl.ds(tile, 1)] = row
         vector[pl.ds(tile * panels, panels)] = OMEGA * get_tile(source, tile, panels, width) / row
@@ -158,7 +199,7 @@
 
 def sweep_kernel(panels, edges, columns, vector, pair_halo, chip_halo, source, diagonal, blocks, result, *rest):
     extended = rest[-1]
-    count, width = blocks.shape[0], blocks.shape[-1]
+    count, _, width = dims(blocks)
     fill_extended(extended, vector, pair_halo, chip_halo, count, panels)
     for tile in range(count):
         product_tile = tile_apply(columns, blocks, extended, tile)
@@ -187,7 +228,7 @@
     panels, columns, vector, pair_halo, chip_halo, source, blocks, aggregate, next_columns, next_blocks,
     next_source, next_diagonal, next_vector, packed, extended,
 ):
-    count, width = blocks.shape[0], blocks.shape[-1]
+    count, _, width = dims(blocks)
     fill_extended(extended, vector, pair_halo, chip_halo, count, panels)
     pieces = [
         get_tile(source, tile, panels, width) - tile_apply(columns, blocks, extended, tile) for tile in range(count)
@@ -414,7 +455,7 @@
     diagonals, near, numbers, semaphores = args[len(names) + outputs + 4:]
     pieces = {0: [n for n in names if n.startswith("blocks_pair")], 1: [n for n in names if n.startswith("blocks_chip")]}
     blocks, own, columns = refs["blocks"], refs["vector"], refs["columns"]
-    own_tiles, width = blocks.shape[0], blocks.shape[-1]
+    own_tiles, _, width = dims(blocks)
     reach = near.shape[1]
     core = lax.axis_index("pair")
     arrivals = [
@@ -523,7 +564,7 @@
         body,
         out_shape=[jax.ShapeDtypeStruct(s, t) for s, t in shapes] + extra,
         in_specs=specs + [free] * (count + len(tokens)),
-        out_specs=[vmem] * given + [free] * count,
+        out_specs=[vmem] * (given + count),
         scratch_shapes=list(scratch) + ([pltpu.SemaphoreType.DMA((count,))] if count else []),
         compiler_params=pltpu.CompilerParams(vmem_limit_bytes=limit),
         name=name,
@@ -584,7 +625,7 @@
 
     def wide_call(level, finish, layout, shapes, operands, integers, near_pair, near_chip, step):
         operands = dict(
-            operands, source=sources[level], diagonal=diagonals[level], blocks=blocks[level], columns=columns[level],
+            operands, source=sources[level], diagonal=diagonals[level], blocks=weights if level == 0 else blocks[level], columns=columns[level],
             integers_pair=integers[0], integers_chip=integers[1], blocks_pair=near_pair,
             **{f"blocks_chip{k}": piece for k, piece in enumerate(near_chip)},
         )
@@ -632,15 +673,20 @@
     first_edge = rows(HALO + reach[0], 8)
     (diagonal, vector, pair_edge, chip_edge), leave = step(
         "first", functools.partial(first_kernel, reach[0]), [diag(0), vec(0), first_edge, first_edge],
-        (columns[0], pulse_rhs, blocks_fine), scalars=(0,),
+        (columns[0], pulse_rhs, blocks_fine), scalars=(0,), remote=(2,), scratch=[pltpu.VMEM(blocks_fine.shape, F32), pltpu.SemaphoreType.DMA((4,))],
     )
     sources, diagonals = [pulse_rhs], [diagonal]
     halos = first_halos = exchange(pair_edge, chip_edge)
     leave()
+    links = blocks_fine.shape[1]
+    weights = call(
+        prepare_kernel, [((counts[0], links * width, 2 * width), BF16)], (blocks_fine,), remote=(0,),
+        scratch=[pltpu.VMEM(blocks_fine.shape, F32), pltpu.SemaphoreType.DMA((4,))], name="prepare",
+    )[0]
     for k in range(2):
         (vector, pair_edge, chip_edge), leave = step(
             f"sweep0{k}", functools.partial(sweep_kernel, panels, True), [vec(0), rows(HALO), rows(HALO)],
-            (columns[0], vector, *halos, pulse_rhs, diagonal, blocks_fine), scalars=(0,), scratch=ext(0),
+            (columns[0], vector, *halos, pulse_rhs, diagonal, weights), scalars=(0,), scratch=ext(0),
         )
         halos = exchange(pair_edge, chip_edge)
         leave()
@@ -650,7 +696,7 @@
     (source, diagonal, vector, packed), leave = step(
         "residual0", functools.partial(residual_kernel, panels),
         [vec(1), diag(1), vec(1), rows(2 * counts[1] + HALO, 8)],
-        (columns[0], vector, *halos, pulse_rhs, blocks_fine, aggregates[0], columns_mid, blocks_mid),
+        (columns[0], vector, *halos, pulse_rhs, weights, aggregates[0], columns_mid, blocks_mid),
         scalars=(0, 7), scratch=ext(0),
     )
     sources.append(source)
@@ -740,8 +786,8 @@
     )[0][0]
 
 
-LEAVE = {'first': ('mid0', 'mid1'), 'sweep00': ('mid2',), 'sweep01': ('mid3',), 'wide_down1': ('fine0',), 'chain': ('fine1',), 'up20': ('fine2',), 'up21': ('fine3',)}
-ARRIVE = {'sweep01': ('mid0', 'mid1'), 'residual0': ('mid2',), 'down21': ('fine0',), 'up21': ('fine1',), 'prolong2': ('fine2',)}
+LEAVE = {'first': ('mid0', 'mid1'), 'sweep00': ('mid2',), 'sweep01': ('mid3',), 'down20': ('fine0',), 'chain': ('fine1',), 'up20': ('fine2',), 'up21': ('fine3',)}
+ARRIVE = {'sweep01': ('mid0', 'mid1'), 'residual0': ('mid2',), 'lowest': ('fine0',), 'up21': ('fine1',), 'prolong2': ('fine2',)}
 
 
 def solution(mesh):

time: 163 us -> 160 us (0.982)
  waiting for transfers between devices: 34.4 us -> 32.1 us
    ppermute x20, waiting for transfers between devices: 31 us -> 28.4 us  [outer_swap(): lax.ppermute(value, AXES, swaps([(2 * k + 1, 2 * k + 2) for k in range(co...]
    pallas_call x16 -> x17, Pallas kernels: 33.5 us -> 32.3 us  [call(): pl.pallas_call(body, out_shape=[jax.ShapeDtypeStruct(s, t) for s, t in sh...]
  transfers between devices with their start and end apart: 36 -> 36, of which waited for: 12 -> 12; matrix products, arithmetic and copies ran while one was open for 0% -> 0% of each run, Pallas kernels for 12% -> 13%
where the time goes in v3:
time: 160 us; the launch traced here: 159 us
  starting transfers between devices  75.5 us (47%)
  Pallas kernels  32.3 us (20%)
  waiting for transfers between devices  32.1 us (20%)
  blocking collectives  13.3 us (8%)
  local copies, waits for them, and re-layouts  5.14 us (3%)
    ppermute x20, starting transfers between devices, outer_swap(): lax.ppermute(value, AXES, swaps([(2 * k + 1, 2 * k + 2) for k in range(co...  72.5 us
    pallas_call x17, Pallas kernels, call(): pl.pallas_call(body, out_shape=[jax.ShapeDtypeStruct(s, t) for s, t in sh...  32.3 us
    ppermute x20, waiting for transfers between devices, outer_swap(): lax.ppermute(value, AXES, swaps([(2 * k + 1, 2 * k + 2) for k in range(co...  28.4 us
    all_to_all x1, blocking collectives, on_device(): incoming = lax.all_to_all(outgoing, AXES, 0, 0)  13.3 us
    unnamed x32, local copies, waits for them, and re-layouts  5.12 us
    ppermute x16, waiting for transfers between devices, inner_swap(): lax.ppermute(value, AXES, swaps([(2 * k, 2 * k + 1) for k in range(count...  3.79 us
  transfers between devices with their start and end apart: 36, of which 12 were waited for; matrix products, arithmetic and copies ran while one was open for 0% of the time, Pallas kernels for 13%

profile of v3, /device:TPU:7, one launch (start us, length us, event | category | flops | bytes accessed | tf_op | source)
XLA Modules:
  0.0 159.2 jit_solution(4677048314949494070)
XLA Ops:
  7.3 3.5 %collective-permute-start.1 = (f32[200,128]{1,0:T(8,128)S(1)}, f32[200,128]{1,0:T(8,128)S(1)}, u32[]{:S(2)}, u32[]{:S(2)}) collective-permute-start(f32[200,128]{1,0:T(8,128)S(1)} %get-tuple-element.44), channel_id=1, source_target_pairs={{1,2},{2,1},{3,4},{4,3},{5,6},{6,5},{7,8},{8,7},{9,10},{10,9},{11,... | collective-permute-start | bytes 307208 | tf_op jit(solution)/shard_map/ppermute | solution.py:585
  10.8 3.9 %collective-permute-start.4 = (f32[1,4,128,128]{3,2,1,0:T(8,128)S(1)}, f32[1,4,128,128]{3,2,1,0:T(8,128)S(1)}, u32[]{:S(2)}, u32[]{:S(2)}) collective-permute-start(f32[1,4,128,128]{3,2,1,0:T(8,128)S(1)} %get-tuple-element.49), channel_id=1, source_target_pairs={{1,2},{2,1},{3,4},{4,3},{5,6},{6,5},{7,8},{8,7},{9,10},{10,9},{11,... | collective-permute-start | bytes 786440 | tf_op jit(solution)/shard_map/ppermute | solution.py:585
  14.6 3.5 %collective-permute-start.5 = (f32[1,4,128,128]{3,2,1,0:T(8,128)S(1)}, f32[1,4,128,128]{3,2,1,0:T(8,128)S(1)}, u32[]{:S(2)}, u32[]{:S(2)}) collective-permute-start(f32[1,4,128,128]{3,2,1,0:T(8,128)S(1)} %get-tuple-element.50), channel_id=1, source_target_pairs={{1,2},{2,1},{3,4},{4,3},{5,6},{6,5},{7,8},{8,7},{9,10},{10,9},{11,... | collective-permute-start | bytes 786440 | tf_op jit(solution)/shard_map/ppermute | solution.py:585
  21.5 3.9 %collective-permute-start.3 = (f32[64,128]{1,0:T(8,128)S(1)}, f32[64,128]{1,0:T(8,128)S(1)}, u32[]{:S(2)}, u32[]{:S(2)}) collective-permute-start(f32[64,128]{1,0:T(8,128)S(1)} %get-tuple-element.48), channel_id=1, source_target_pairs={{1,2},{2,1},{3,4},{4,3},{5,6},{6,5},{7,8},{8,7},{9,10},{10,9},{11,... | collective-permute-start | bytes 98312 | tf_op jit(solution)/shard_map/ppermute | solution.py:585
  25.3 3.5 %collective-permute-start.8 = (f32[1,4,128,128]{3,2,1,0:T(8,128)S(1)}, f32[1,4,128,128]{3,2,1,0:T(8,128)S(1)}, u32[]{:S(2)}, u32[]{:S(2)}) collective-permute-start(f32[1,4,128,128]{3,2,1,0:T(8,128)S(1)} %get-tuple-element.54), channel_id=1, source_target_pairs={{1,2},{2,1},{3,4},{4,3},{5,6},{6,5},{7,8},{8,7},{9,10},{10,9},{11,... | collective-permute-start | bytes 786440 | tf_op jit(solution)/shard_map/ppermute | solution.py:585
  31.2 3.9 %collective-permute-start.7 = (f32[64,128]{1,0:T(8,128)S(1)}, f32[64,128]{1,0:T(8,128)S(1)}, u32[]{:S(2)}, u32[]{:S(2)}) collective-permute-start(f32[64,128]{1,0:T(8,128)S(1)} %get-tuple-element.53), channel_id=1, source_target_pairs={{1,2},{2,1},{3,4},{4,3},{5,6},{6,5},{7,8},{8,7},{9,10},{10,9},{11,... | collective-permute-start | bytes 98312 | tf_op jit(solution)/shard_map/ppermute | solution.py:585
  35.0 3.1 %collective-permute-done.7.refs_3_ = f32[64,128]{1,0:T(8,128)S(1)} collective-permute-done((f32[64,128]{1,0:T(8,128)S(1)}, f32[64,128]{1,0:T(8,128)S(1)}, u32[]{:S(2)}, u32[]{:S(2)}) %collective-permute-start.7) | collective-permute-done | bytes 32800 | tf_op jit(solution)/shard_map/ppermute | solution.py:585
  40.0 3.9 %collective-permute-start.13 = (f32[1,4,128,128]{3,2,1,0:T(8,128)S(1)}, f32[1,4,128,128]{3,2,1,0:T(8,128)S(1)}, u32[]{:S(2)}, u32[]{:S(2)}) collective-permute-start(f32[1,4,128,128]{3,2,1,0:T(8,128)S(1)} %get-tuple-element.59), channel_id=1, source_target_pairs={{1,2},{2,1},{3,4},{4,3},{5,6},{6,5},{7,8},{8,7},{9,10},{10,9},{11,... | collective-permute-start | bytes 786440 | tf_op jit(solution)/shard_map/ppermute | solution.py:585
  43.9 3.5 %collective-permute-start.10 = (f32[328,128]{1,0:T(8,128)S(1)}, f32[328,128]{1,0:T(8,128)S(1)}, u32[]{:S(2)}, u32[]{:S(2)}) collective-permute-start(f32[328,128]{1,0:T(8,128)S(1)} %pad_maximum_fusion), channel_id=1, source_target_pairs={{1,2},{2,1},{3,4},{4,3},{5,6},{6,5},{7,8},{8,7},{9,10},{10,9},{11,... | collective-permute-start | bytes 503816 | tf_op jit(solution)/shard_map/ppermute | solution.py:585
  47.4 5.0 %collective-permute-done.10.refs_2_.refs_5_.refs_14_.refs_13_ = f32[328,128]{1,0:T(8,128)S(1)} collective-permute-done((f32[328,128]{1,0:T(8,128)S(1)}, f32[328,128]{1,0:T(8,128)S(1)}, u32[]{:S(2)}, u32[]{:S(2)}) %collective-permute-start.10) | collective-permute-done | bytes 167968 | tf_op jit(solution)/shard_map/ppermute | solution.py:585
  53.7 3.4 %wide_down1.1 = (f32[128,128]{1,0:T(8,128)S(1)}, f32[64,128]{1,0:T(8,128)S(1)}, f32[2,128]{1,0:T(2,128)S(1)}, f32[64,128]{1,0:T(8,128)S(1)}) custom-call(f32[128,128]{1,0:T(8,128)S(1)} %get-tuple-element.55.refs_0_, f32[328,128]{1,0:T(8,128)S(1)} %collective-permute-done.9.refs_1_.refs_4_.refs_13_.refs_12_, ...), custom_call_target="tpu_custom_call" | custom-call | tf_op jit(solution)/shard_map/wide_down1/pallas_call | solution.py:563
  57.1 3.6 %collective-permute-start.15 = (f32[64,128]{1,0:T(8,128)S(1)}, f32[64,128]{1,0:T(8,128)S(1)}, u32[]{:S(2)}, u32[]{:S(2)}) collective-permute-start(f32[64,128]{1,0:T(8,128)S(1)} %get-tuple-element.60.refs_1_), channel_id=1, source_target_pairs={{1,2},{2,1},{3,4},{4,3},{5,6},{6,5},{7,8},{8,7},{9,10},{10,9},{11,... | collective-permute-start | bytes 98312 | tf_op jit(solution)/shard_map/ppermute | solution.py:585
  60.8 3.4 %collective-permute-done.15.refs_3_ = f32[64,128]{1,0:T(8,128)S(1)} collective-permute-done((f32[64,128]{1,0:T(8,128)S(1)}, f32[64,128]{1,0:T(8,128)S(1)}, u32[]{:S(2)}, u32[]{:S(2)}) %collective-permute-start.15) | collective-permute-done | bytes 32800 | tf_op jit(solution)/shard_map/ppermute | solution.py:585
  65.0 3.6 %collective-permute-start.20 = (f32[1,4,128,128]{3,2,1,0:T(8,128)S(1)}, f32[1,4,128,128]{3,2,1,0:T(8,128)S(1)}, u32[]{:S(2)}, u32[]{:S(2)}) collective-permute-start(f32[1,4,128,128]{3,2,1,0:T(8,128)S(1)} %get-tuple-element.64), channel_id=1, source_target_pairs={{1,2},{2,1},{3,4},{4,3},{5,6},{6,5},{7,8},{8,7},{9,10},{10,9},{11,... | collective-permute-start | bytes 786440 | tf_op jit(solution)/shard_map/ppermute | solution.py:585
  68.6 3.8 %collective-permute-start.17 = (f32[64,128]{1,0:T(8,128)S(1)}, f32[64,128]{1,0:T(8,128)S(1)}, u32[]{:S(2)}, u32[]{:S(2)}) collective-permute-start(f32[64,128]{1,0:T(8,128)S(1)} %get-tuple-element.63.refs_1_), channel_id=1, source_target_pairs={{1,2},{2,1},{3,4},{4,3},{5,6},{6,5},{7,8},{8,7},{9,10},{10,9},{11,... | collective-permute-start | bytes 98312 | tf_op jit(solution)/shard_map/ppermute | solution.py:585
  72.5 3.2 %collective-permute-done.17.refs_3_ = f32[64,128]{1,0:T(8,128)S(1)} collective-permute-done((f32[64,128]{1,0:T(8,128)S(1)}, f32[64,128]{1,0:T(8,128)S(1)}, u32[]{:S(2)}, u32[]{:S(2)}) %collective-permute-start.17) | collective-permute-done | bytes 32800 | tf_op jit(solution)/shard_map/ppermute | solution.py:585
  76.5 3.9 %collective-permute-start.19 = (f32[64,128]{1,0:T(8,128)S(1)}, f32[64,128]{1,0:T(8,128)S(1)}, u32[]{:S(2)}, u32[]{:S(2)}) collective-permute-start(f32[64,128]{1,0:T(8,128)S(1)} %down21.1.refs_1_.refs_5_), channel_id=1, source_target_pairs={{1,2},{2,1},{3,4},{4,3},{5,6},{6,5},{7,8},{8,7},{9,10},{10,9},{11,... | collective-permute-start | bytes 98312 | tf_op jit(solution)/shard_map/ppermute | solution.py:585
  84.7 13.3 %all_to_all.5.refs_1_ = f32[32,16,128]{2,1,0:T(8,128)S(1)} all-to-all(f32[32,16,128]{2,1,0:T(8,128)S(1)} %get-tuple-element.66), channel_id=1, replica_groups=mesh['parts'=16,'pair'=2] {'parts','pair'}, dimensions={0} | all-to-all | bytes 524288 | tf_op jit(solution)/shard_map/all_to_all | solution.py:750
  98.0 4.3 %chain.1 = (f32[64,128]{1,0:T(8,128)S(1)}, f32[1,4,128,128]{3,2,1,0:T(8,128)S(1)}) custom-call(f32[32,128]{1,0:T(8,128)S(1)} %get-tuple-element.65.refs_0_, f32[32,16,128]{2,1,0:T(8,128)S(1)} %all_to_all.5.refs_1_, f32[1,5,128,128]{3,2,1,0:T(8,128)S(1)} %copy-done.7, s32[1,4,128]{2,1,0:T(4,128)S(1)} %copy-done.13, s32[1,256]{1,0:T(1,128)S(1)} %bitcast.14, ...), custom_call_target="tpu_custom_call" | custom-call | tf_op jit(solution)/shard_map/chain/pallas_call | solution.py:563
  102.3 4.4 %collective-permute-start.23 = (f32[64,128]{1,0:T(8,128)S(1)}, f32[64,128]{1,0:T(8,128)S(1)}, u32[]{:S(2)}, u32[]{:S(2)}) collective-permute-start(f32[64,128]{1,0:T(8,128)S(1)} %get-tuple-element.67.refs_1_), channel_id=1, source_target_pairs={{1,2},{2,1},{3,4},{4,3},{5,6},{6,5},{7,8},{8,7},{9,10},{10,9},{11,... | collective-permute-start | bytes 98312 | tf_op jit(solution)/shard_map/ppermute | solution.py:585
  106.7 3.0 %collective-permute-start.26 = (f32[1,4,128,128]{3,2,1,0:T(8,128)S(1)}, f32[1,4,128,128]{3,2,1,0:T(8,128)S(1)}, u32[]{:S(2)}, u32[]{:S(2)}) collective-permute-start(f32[1,4,128,128]{3,2,1,0:T(8,128)S(1)} %get-tuple-element.69), channel_id=1, source_target_pairs={{1,2},{2,1},{3,4},{4,3},{5,6},{6,5},{7,8},{8,7},{9,10},{10,9},{11,... | collective-permute-start | bytes 786440 | tf_op jit(solution)/shard_map/ppermute | solution.py:585
  110.6 4.4 %collective-permute-start.29 = (f32[1,4,128,128]{3,2,1,0:T(8,128)S(1)}, f32[1,4,128,128]{3,2,1,0:T(8,128)S(1)}, u32[]{:S(2)}, u32[]{:S(2)}) collective-permute-start(f32[1,4,128,128]{3,2,1,0:T(8,128)S(1)} %get-tuple-element.72), channel_id=1, source_target_pairs={{1,2},{2,1},{3,4},{4,3},{5,6},{6,5},{7,8},{8,7},{9,10},{10,9},{11,... | collective-permute-start | bytes 786440 | tf_op jit(solution)/shard_map/ppermute | solution.py:585
  115.0 3.0 %collective-permute-start.25 = (f32[64,128]{1,0:T(8,128)S(1)}, f32[64,128]{1,0:T(8,128)S(1)}, u32[]{:S(2)}, u32[]{:S(2)}) collective-permute-start(f32[64,128]{1,0:T(8,128)S(1)} %get-tuple-element.68.refs_1_), channel_id=1, source_target_pairs={{1,2},{2,1},{3,4},{4,3},{5,6},{6,5},{7,8},{8,7},{9,10},{10,9},{11,... | collective-permute-start | bytes 98312 | tf_op jit(solution)/shard_map/ppermute | solution.py:585
  118.1 4.1 %collective-permute-done.25.refs_3_ = f32[64,128]{1,0:T(8,128)S(1)} collective-permute-done((f32[64,128]{1,0:T(8,128)S(1)}, f32[64,128]{1,0:T(8,128)S(1)}, u32[]{:S(2)}, u32[]{:S(2)}) %collective-permute-start.25) | collective-permute-done | bytes 32800 | tf_op jit(solution)/shard_map/ppermute | solution.py:585
  123.1 3.0 %collective-permute-start.28 = (f32[64,128]{1,0:T(8,128)S(1)}, f32[64,128]{1,0:T(8,128)S(1)}, u32[]{:S(2)}, u32[]{:S(2)}) collective-permute-start(f32[64,128]{1,0:T(8,128)S(1)} %get-tuple-element.70.refs_1_), channel_id=1, source_target_pairs={{1,2},{2,1},{3,4},{4,3},{5,6},{6,5},{7,8},{8,7},{9,10},{10,9},{11,... | collective-permute-start | bytes 98312 | tf_op jit(solution)/shard_map/ppermute | solution.py:585
  126.9 3.3 %collective-permute-done.28.refs_3_ = f32[64,128]{1,0:T(8,128)S(1)} collective-permute-done((f32[64,128]{1,0:T(8,128)S(1)}, f32[64,128]{1,0:T(8,128)S(1)}, u32[]{:S(2)}, u32[]{:S(2)}) %collective-permute-start.28) | collective-permute-done | bytes 32800 | tf_op jit(solution)/shard_map/ppermute | solution.py:585
  132.9 2.9 %collective-permute-start.31 = (f32[192,128]{1,0:T(8,128)S(1)}, f32[192,128]{1,0:T(8,128)S(1)}, u32[]{:S(2)}, u32[]{:S(2)}) collective-permute-start(f32[192,128]{1,0:T(8,128)S(1)} %pad_maximum_fusion.1), channel_id=1, source_target_pairs={{1,2},{2,1},{3,4},{4,3},{5,6},{6,5},{7,8},{8,7},{9,10},{10,9},{11,... | collective-permute-start | bytes 294920 | tf_op jit(solution)/shard_map/ppermute | solution.py:585
  135.8 4.6 %collective-permute-start.35 = (f32[1,4,128,128]{3,2,1,0:T(8,128)S(1)}, f32[1,4,128,128]{3,2,1,0:T(8,128)S(1)}, u32[]{:S(2)}, u32[]{:S(2)}) collective-permute-start(f32[1,4,128,128]{3,2,1,0:T(8,128)S(1)} %get-tuple-element.78), channel_id=1, source_target_pairs={{1,2},{2,1},{3,4},{4,3},{5,6},{6,5},{7,8},{8,7},{9,10},{10,9},{11,... | collective-permute-start | bytes 786440 | tf_op jit(solution)/shard_map/ppermute | solution.py:585
  141.9 4.0 %wide_up1.1 = (f32[512,128]{1,0:T(8,128)S(1)}, f32[192,128]{1,0:T(8,128)S(1)}, f32[192,128]{1,0:T(8,128)S(1)}) custom-call(f32[128,128]{1,0:T(8,128)S(1)} %get-tuple-element.73.refs_0_, f32[192,128]{1,0:T(8,128)S(1)} %collective-permute-done.30.refs_1_, f32[192,128]{1,0:T(8,128)S(1)} %collective-permute-done.31.refs_2_, ...), custom_call_target="tpu_custom_call" | custom-call | tf_op jit(solution)/shard_map/wide_up1/pallas_call | solution.py:563
  146.2 3.0 %collective-permute-start.34 = (f32[192,128]{1,0:T(8,128)S(1)}, f32[192,128]{1,0:T(8,128)S(1)}, u32[]{:S(2)}, u32[]{:S(2)}) collective-permute-start(f32[192,128]{1,0:T(8,128)S(1)} %get-tuple-element.77), channel_id=1, source_target_pairs={{1,2},{2,1},{3,4},{4,3},{5,6},{6,5},{7,8},{8,7},{9,10},{10,9},{11,... | collective-permute-start | bytes 294920 | tf_op jit(solution)/shard_map/ppermute | solution.py:585
  149.2 4.7 %collective-permute-done.34.refs_2_ = f32[192,128]{1,0:T(8,128)S(1)} collective-permute-done((f32[192,128]{1,0:T(8,128)S(1)}, f32[192,128]{1,0:T(8,128)S(1)}, u32[]{:S(2)}, u32[]{:S(2)}) %collective-permute-start.34) | collective-permute-done | bytes 98336 | tf_op jit(solution)/shard_map/ppermute | solution.py:585
  153.9 5.2 %wide_last0.1 = f32[32,2048]{1,0:T(8,128)} custom-call(f32[512,128]{1,0:T(8,128)S(1)} %get-tuple-element.75.refs_0_, f32[192,128]{1,0:T(8,128)S(1)} %collective-permute-done.33.refs_1_, f32[192,128]{1,0:T(8,128)S(1)} %collective-permute-done.34.refs_2_, f32[200,128]{1,0:T(8,128)S(1)} %collective-permute-done.refs_2_.refs_3_.refs_9_, ...), custom_call_target="tpu_custom_call" | custom-call | tf_op jit(solution)/shard_map/wide_last0/pallas_call | solution.py:563
  (97 shorter events, 29.0 us)
Async XLA Ops:
  0.0 53.7 %collective-permute-start.12 = (f32[4,4,128,128]{3,2,1,0:T(8,128)}, f32[4,4,128,128]{3,2,1,0:T(8,128)S(1)}, u32[]{:S(2)}, u32[]{:S(2)}) collective-permute-start(f32[4,4,128,128]{3,2,1,0:T(8,128)} %refs_10_.1), channel_id=1, source_target_pairs={{0,1},{1,0},{2,3},{3,2},{4,5},{5,4},{6,7},{7,6},{8,9},{9,8},{10,11... | collective-permute-start | bytes 3145736 | tf_op jit(solution)/shard_map/ppermute | solution.py:580
  7.2 12.7 %collective-permute-start = (f32[200,128]{1,0:T(8,128)S(1)}, f32[200,128]{1,0:T(8,128)S(1)}, u32[]{:S(2)}, u32[]{:S(2)}) collective-permute-start(f32[200,128]{1,0:T(8,128)S(1)} %get-tuple-element.43), channel_id=1, source_target_pairs={{0,1},{1,0},{2,3},{3,2},{4,5},{5,4},{6,7},{7,6},{8,9},{9,8},{10,11... | collective-permute-start | bytes 307208 | tf_op jit(solution)/shard_map/ppermute | solution.py:580
  7.3 12.6 %collective-permute-start.1 = (f32[200,128]{1,0:T(8,128)S(1)}, f32[200,128]{1,0:T(8,128)S(1)}, u32[]{:S(2)}, u32[]{:S(2)}) collective-permute-start(f32[200,128]{1,0:T(8,128)S(1)} %get-tuple-element.44), channel_id=1, source_target_pairs={{1,2},{2,1},{3,4},{4,3},{5,6},{6,5},{7,8},{8,7},{9,10},{10,9},{11,... | collective-permute-start | bytes 307208 | tf_op jit(solution)/shard_map/ppermute | solution.py:585
  10.8 18.3 %collective-permute-start.4 = (f32[1,4,128,128]{3,2,1,0:T(8,128)S(1)}, f32[1,4,128,128]{3,2,1,0:T(8,128)S(1)}, u32[]{:S(2)}, u32[]{:S(2)}) collective-permute-start(f32[1,4,128,128]{3,2,1,0:T(8,128)S(1)} %get-tuple-element.49), channel_id=1, source_target_pairs={{1,2},{2,1},{3,4},{4,3},{5,6},{6,5},{7,8},{8,7},{9,10},{10,9},{11,... | collective-permute-start | bytes 786440 | tf_op jit(solution)/shard_map/ppermute | solution.py:585
  14.6 14.4 %collective-permute-start.5 = (f32[1,4,128,128]{3,2,1,0:T(8,128)S(1)}, f32[1,4,128,128]{3,2,1,0:T(8,128)S(1)}, u32[]{:S(2)}, u32[]{:S(2)}) collective-permute-start(f32[1,4,128,128]{3,2,1,0:T(8,128)S(1)} %get-tuple-element.50), channel_id=1, source_target_pairs={{1,2},{2,1},{3,4},{4,3},{5,6},{6,5},{7,8},{8,7},{9,10},{10,9},{11,... | collective-permute-start | bytes 786440 | tf_op jit(solution)/shard_map/ppermute | solution.py:585
  21.4 4.0 %collective-permute-start.2 = (f32[64,128]{1,0:T(8,128)S(1)}, f32[64,128]{1,0:T(8,128)S(1)}, u32[]{:S(2)}, u32[]{:S(2)}) collective-permute-start(f32[64,128]{1,0:T(8,128)S(1)} %get-tuple-element.47), channel_id=1, source_target_pairs={{0,1},{1,0},{2,3},{3,2},{4,5},{5,4},{6,7},{7,6},{8,9},{9,8},{10,11... | collective-permute-start | bytes 98312 | tf_op jit(solution)/shard_map/ppermute | solution.py:580
  21.5 7.5 %collective-permute-start.3 = (f32[64,128]{1,0:T(8,128)S(1)}, f32[64,128]{1,0:T(8,128)S(1)}, u32[]{:S(2)}, u32[]{:S(2)}) collective-permute-start(f32[64,128]{1,0:T(8,128)S(1)} %get-tuple-element.48), channel_id=1, source_target_pairs={{1,2},{2,1},{3,4},{4,3},{5,6},{6,5},{7,8},{8,7},{9,10},{10,9},{11,... | collective-permute-start | bytes 98312 | tf_op jit(solution)/shard_map/ppermute | solution.py:585
  25.3 12.8 %collective-permute-start.8 = (f32[1,4,128,128]{3,2,1,0:T(8,128)S(1)}, f32[1,4,128,128]{3,2,1,0:T(8,128)S(1)}, u32[]{:S(2)}, u32[]{:S(2)}) collective-permute-start(f32[1,4,128,128]{3,2,1,0:T(8,128)S(1)} %get-tuple-element.54), channel_id=1, source_target_pairs={{1,2},{2,1},{3,4},{4,3},{5,6},{6,5},{7,8},{8,7},{9,10},{10,9},{11,... | collective-permute-start | bytes 786440 | tf_op jit(solution)/shard_map/ppermute | solution.py:585
  29.0 53.2 %collective-permute-start.21 = (f32[4,4,128,128]{3,2,1,0:T(8,128)S(1)}, f32[4,4,128,128]{3,2,1,0:T(8,128)S(1)}, u32[]{:S(2)}, u32[]{:S(2)}) collective-permute-start(f32[4,4,128,128]{3,2,1,0:T(8,128)S(1)} %near.1), channel_id=1, source_target_pairs={{0,1},{1,0},{2,3},{3,2},{4,5},{5,4},{6,7},{7,6},{8,9},{9,8},{10,11... | collective-permute-start | bytes 3145736 | tf_op jit(solution)/shard_map/ppermute | solution.py:580
  30.6 4.4 %collective-permute-start.6 = (f32[64,128]{1,0:T(8,128)S(1)}, f32[64,128]{1,0:T(8,128)S(1)}, u32[]{:S(2)}, u32[]{:S(2)}) collective-permute-start(f32[64,128]{1,0:T(8,128)S(1)} %get-tuple-element.52), channel_id=1, source_target_pairs={{0,1},{1,0},{2,3},{3,2},{4,5},{5,4},{6,7},{7,6},{8,9},{9,8},{10,11... | collective-permute-start | bytes 98312 | tf_op jit(solution)/shard_map/ppermute | solution.py:580
  31.2 7.0 %collective-permute-start.7 = (f32[64,128]{1,0:T(8,128)S(1)}, f32[64,128]{1,0:T(8,128)S(1)}, u32[]{:S(2)}, u32[]{:S(2)}) collective-permute-start(f32[64,128]{1,0:T(8,128)S(1)} %get-tuple-element.53), channel_id=1, source_target_pairs={{1,2},{2,1},{3,4},{4,3},{5,6},{6,5},{7,8},{8,7},{9,10},{10,9},{11,... | collective-permute-start | bytes 98312 | tf_op jit(solution)/shard_map/ppermute | solution.py:585
  39.9 4.0 %collective-permute-start.9 = (f32[328,128]{1,0:T(8,128)S(1)}, f32[328,128]{1,0:T(8,128)S(1)}, u32[]{:S(2)}, u32[]{:S(2)}) collective-permute-start(f32[328,128]{1,0:T(8,128)S(1)} %get-tuple-element.56), channel_id=1, source_target_pairs={{0,1},{1,0},{2,3},{3,2},{4,5},{5,4},{6,7},{7,6},{8,9},{9,8},{10,11... | collective-permute-start | bytes 503816 | tf_op jit(solution)/shard_map/ppermute | solution.py:580
  40.0 12.5 %collective-permute-start.13 = (f32[1,4,128,128]{3,2,1,0:T(8,128)S(1)}, f32[1,4,128,128]{3,2,1,0:T(8,128)S(1)}, u32[]{:S(2)}, u32[]{:S(2)}) collective-permute-start(f32[1,4,128,128]{3,2,1,0:T(8,128)S(1)} %get-tuple-element.59), channel_id=1, source_target_pairs={{1,2},{2,1},{3,4},{4,3},{5,6},{6,5},{7,8},{8,7},{9,10},{10,9},{11,... | collective-permute-start | bytes 786440 | tf_op jit(solution)/shard_map/ppermute | solution.py:585
  43.9 8.5 %collective-permute-start.10 = (f32[328,128]{1,0:T(8,128)S(1)}, f32[328,128]{1,0:T(8,128)S(1)}, u32[]{:S(2)}, u32[]{:S(2)}) collective-permute-start(f32[328,128]{1,0:T(8,128)S(1)} %pad_maximum_fusion), channel_id=1, source_target_pairs={{1,2},{2,1},{3,4},{4,3},{5,6},{6,5},{7,8},{8,7},{9,10},{10,9},{11,... | collective-permute-start | bytes 503816 | tf_op jit(solution)/shard_map/ppermute | solution.py:585
  57.1 7.0 %collective-permute-start.15 = (f32[64,128]{1,0:T(8,128)S(1)}, f32[64,128]{1,0:T(8,128)S(1)}, u32[]{:S(2)}, u32[]{:S(2)}) collective-permute-start(f32[64,128]{1,0:T(8,128)S(1)} %get-tuple-element.60.refs_1_), channel_id=1, source_target_pairs={{1,2},{2,1},{3,4},{4,3},{5,6},{6,5},{7,8},{8,7},{9,10},{10,9},{11,... | collective-permute-start | bytes 98312 | tf_op jit(solution)/shard_map/ppermute | solution.py:585
  60.7 3.4 %collective-permute-start.14 = (f32[64,128]{1,0:T(8,128)S(1)}, f32[64,128]{1,0:T(8,128)S(1)}, u32[]{:S(2)}, u32[]{:S(2)}) collective-permute-start(f32[64,128]{1,0:T(8,128)S(1)} %get-tuple-element.60.refs_1_), channel_id=1, source_target_pairs={{0,1},{1,0},{2,3},{3,2},{4,5},{5,4},{6,7},{7,6},{8,9},{9,8},{10,11... | collective-permute-start | bytes 98312 | tf_op jit(solution)/shard_map/ppermute | solution.py:580
  65.0 18.5 %collective-permute-start.20 = (f32[1,4,128,128]{3,2,1,0:T(8,128)S(1)}, f32[1,4,128,128]{3,2,1,0:T(8,128)S(1)}, u32[]{:S(2)}, u32[]{:S(2)}) collective-permute-start(f32[1,4,128,128]{3,2,1,0:T(8,128)S(1)} %get-tuple-element.64), channel_id=1, source_target_pairs={{1,2},{2,1},{3,4},{4,3},{5,6},{6,5},{7,8},{8,7},{9,10},{10,9},{11,... | collective-permute-start | bytes 786440 | tf_op jit(solution)/shard_map/ppermute | solution.py:585
  68.6 7.0 %collective-permute-start.17 = (f32[64,128]{1,0:T(8,128)S(1)}, f32[64,128]{1,0:T(8,128)S(1)}, u32[]{:S(2)}, u32[]{:S(2)}) collective-permute-start(f32[64,128]{1,0:T(8,128)S(1)} %get-tuple-element.63.refs_1_), channel_id=1, source_target_pairs={{1,2},{2,1},{3,4},{4,3},{5,6},{6,5},{7,8},{8,7},{9,10},{10,9},{11,... | collective-permute-start | bytes 98312 | tf_op jit(solution)/shard_map/ppermute | solution.py:585
  72.4 3.3 %collective-permute-start.16 = (f32[64,128]{1,0:T(8,128)S(1)}, f32[64,128]{1,0:T(8,128)S(1)}, u32[]{:S(2)}, u32[]{:S(2)}) collective-permute-start(f32[64,128]{1,0:T(8,128)S(1)} %get-tuple-element.63.refs_1_), channel_id=1, source_target_pairs={{0,1},{1,0},{2,3},{3,2},{4,5},{5,4},{6,7},{7,6},{8,9},{9,8},{10,11... | collective-permute-start | bytes 98312 | tf_op jit(solution)/shard_map/ppermute | solution.py:580
  76.5 7.0 %collective-permute-start.19 = (f32[64,128]{1,0:T(8,128)S(1)}, f32[64,128]{1,0:T(8,128)S(1)}, u32[]{:S(2)}, u32[]{:S(2)}) collective-permute-start(f32[64,128]{1,0:T(8,128)S(1)} %down21.1.refs_1_.refs_5_), channel_id=1, source_target_pairs={{1,2},{2,1},{3,4},{4,3},{5,6},{6,5},{7,8},{8,7},{9,10},{10,9},{11,... | collective-permute-start | bytes 98312 | tf_op jit(solution)/shard_map/ppermute | solution.py:585
  80.4 3.2 %collective-permute-start.18 = (f32[64,128]{1,0:T(8,128)S(1)}, f32[64,128]{1,0:T(8,128)S(1)}, u32[]{:S(2)}, u32[]{:S(2)}) collective-permute-start(f32[64,128]{1,0:T(8,128)S(1)} %down21.1.refs_1_.refs_5_), channel_id=1, source_target_pairs={{0,1},{1,0},{2,3},{3,2},{4,5},{5,4},{6,7},{7,6},{8,9},{9,8},{10,11... | collective-permute-start | bytes 98312 | tf_op jit(solution)/shard_map/ppermute | solution.py:580
  102.3 7.5 %collective-permute-start.23 = (f32[64,128]{1,0:T(8,128)S(1)}, f32[64,128]{1,0:T(8,128)S(1)}, u32[]{:S(2)}, u32[]{:S(2)}) collective-permute-start(f32[64,128]{1,0:T(8,128)S(1)} %get-tuple-element.67.refs_1_), channel_id=1, source_target_pairs={{1,2},{2,1},{3,4},{4,3},{5,6},{6,5},{7,8},{8,7},{9,10},{10,9},{11,... | collective-permute-start | bytes 98312 | tf_op jit(solution)/shard_map/ppermute | solution.py:585
  106.7 15.4 %collective-permute-start.26 = (f32[1,4,128,128]{3,2,1,0:T(8,128)S(1)}, f32[1,4,128,128]{3,2,1,0:T(8,128)S(1)}, u32[]{:S(2)}, u32[]{:S(2)}) collective-permute-start(f32[1,4,128,128]{3,2,1,0:T(8,128)S(1)} %get-tuple-element.69), channel_id=1, source_target_pairs={{1,2},{2,1},{3,4},{4,3},{5,6},{6,5},{7,8},{8,7},{9,10},{10,9},{11,... | collective-permute-start | bytes 786440 | tf_op jit(solution)/shard_map/ppermute | solution.py:585
  110.6 16.3 %collective-permute-start.29 = (f32[1,4,128,128]{3,2,1,0:T(8,128)S(1)}, f32[1,4,128,128]{3,2,1,0:T(8,128)S(1)}, u32[]{:S(2)}, u32[]{:S(2)}) collective-permute-start(f32[1,4,128,128]{3,2,1,0:T(8,128)S(1)} %get-tuple-element.72), channel_id=1, source_target_pairs={{1,2},{2,1},{3,4},{4,3},{5,6},{6,5},{7,8},{8,7},{9,10},{10,9},{11,... | collective-permute-start | bytes 786440 | tf_op jit(solution)/shard_map/ppermute | solution.py:585
  115.0 7.1 %collective-permute-start.25 = (f32[64,128]{1,0:T(8,128)S(1)}, f32[64,128]{1,0:T(8,128)S(1)}, u32[]{:S(2)}, u32[]{:S(2)}) collective-permute-start(f32[64,128]{1,0:T(8,128)S(1)} %get-tuple-element.68.refs_1_), channel_id=1, source_target_pairs={{1,2},{2,1},{3,4},{4,3},{5,6},{6,5},{7,8},{8,7},{9,10},{10,9},{11,... | collective-permute-start | bytes 98312 | tf_op jit(solution)/shard_map/ppermute | solution.py:585
  118.0 4.1 %collective-permute-start.24 = (f32[64,128]{1,0:T(8,128)S(1)}, f32[64,128]{1,0:T(8,128)S(1)}, u32[]{:S(2)}, u32[]{:S(2)}) collective-permute-start(f32[64,128]{1,0:T(8,128)S(1)} %get-tuple-element.68.refs_1_), channel_id=1, source_target_pairs={{0,1},{1,0},{2,3},{3,2},{4,5},{5,4},{6,7},{7,6},{8,9},{9,8},{10,11... | collective-permute-start | bytes 98312 | tf_op jit(solution)/shard_map/ppermute | solution.py:580
  123.1 7.2 %collective-permute-start.28 = (f32[64,128]{1,0:T(8,128)S(1)}, f32[64,128]{1,0:T(8,128)S(1)}, u32[]{:S(2)}, u32[]{:S(2)}) collective-permute-start(f32[64,128]{1,0:T(8,128)S(1)} %get-tuple-element.70.refs_1_), channel_id=1, source_target_pairs={{1,2},{2,1},{3,4},{4,3},{5,6},{6,5},{7,8},{8,7},{9,10},{10,9},{11,... | collective-permute-start | bytes 98312 | tf_op jit(solution)/shard_map/ppermute | solution.py:585
  126.1 4.1 %collective-permute-start.27 = (f32[64,128]{1,0:T(8,128)S(1)}, f32[64,128]{1,0:T(8,128)S(1)}, u32[]{:S(2)}, u32[]{:S(2)}) collective-permute-start(f32[64,128]{1,0:T(8,128)S(1)} %get-tuple-element.70.refs_1_), channel_id=1, source_target_pairs={{0,1},{1,0},{2,3},{3,2},{4,5},{5,4},{6,7},{7,6},{8,9},{9,8},{10,11... | collective-permute-start | bytes 98312 | tf_op jit(solution)/shard_map/ppermute | solution.py:580
  132.9 7.8 %collective-permute-start.31 = (f32[192,128]{1,0:T(8,128)S(1)}, f32[192,128]{1,0:T(8,128)S(1)}, u32[]{:S(2)}, u32[]{:S(2)}) collective-permute-start(f32[192,128]{1,0:T(8,128)S(1)} %pad_maximum_fusion.1), channel_id=1, source_target_pairs={{1,2},{2,1},{3,4},{4,3},{5,6},{6,5},{7,8},{8,7},{9,10},{10,9},{11,... | collective-permute-start | bytes 294920 | tf_op jit(solution)/shard_map/ppermute | solution.py:585
  135.8 13.4 %collective-permute-start.35 = (f32[1,4,128,128]{3,2,1,0:T(8,128)S(1)}, f32[1,4,128,128]{3,2,1,0:T(8,128)S(1)}, u32[]{:S(2)}, u32[]{:S(2)}) collective-permute-start(f32[1,4,128,128]{3,2,1,0:T(8,128)S(1)} %get-tuple-element.78), channel_id=1, source_target_pairs={{1,2},{2,1},{3,4},{4,3},{5,6},{6,5},{7,8},{8,7},{9,10},{10,9},{11,... | collective-permute-start | bytes 786440 | tf_op jit(solution)/shard_map/ppermute | solution.py:585
  145.9 3.2 %collective-permute-start.33 = (f32[192,128]{1,0:T(8,128)S(1)}, f32[192,128]{1,0:T(8,128)S(1)}, u32[]{:S(2)}, u32[]{:S(2)}) collective-permute-start(f32[192,128]{1,0:T(8,128)S(1)} %get-tuple-element.76), channel_id=1, source_target_pairs={{0,1},{1,0},{2,3},{3,2},{4,5},{5,4},{6,7},{7,6},{8,9},{9,8},{10,11... | collective-permute-start | bytes 294920 | tf_op jit(solution)/shard_map/ppermute | solution.py:580
  146.2 7.7 %collective-permute-start.34 = (f32[192,128]{1,0:T(8,128)S(1)}, f32[192,128]{1,0:T(8,128)S(1)}, u32[]{:S(2)}, u32[]{:S(2)}) collective-permute-start(f32[192,128]{1,0:T(8,128)S(1)} %get-tuple-element.77), channel_id=1, source_target_pairs={{1,2},{2,1},{3,4},{4,3},{5,6},{6,5},{7,8},{8,7},{9,10},{10,9},{11,... | collective-permute-start | bytes 294920 | tf_op jit(solution)/shard_map/ppermute | solution.py:585
  (20 other events, 263.0 us)
